TPU v7x, 32 devices: a whole 2x2x4 slice. The times are simulated.
32 devices in a mesh: fsdp: 2 (over x), ctx: 8 (over z, y), tp: 2 (over core).
Axes of the slice: x: 2, y: 2, z: 4, core: 2. Of those that a mesh axis runs over, the one named last changes fastest.
Arguments:
- tokens: bfloat16 [4096, 1024], P(('fsdp', 'ctx', 'tp')), may hold values from -6 to 6
- qkv_weight: bfloat16 [2, 1024, 3, 1024], P(None, 'fsdp', None, 'tp'), may hold values from -0.1875 to 0.1875
- out_weight: bfloat16 [2, 1024, 1024], P(None, 'tp', 'fsdp'), may hold values from -0.5 to 0.5
- up_weight: bfloat16 [2, 1024, 4096], P(None, 'fsdp', 'tp'), may hold values from -0.1875 to 0.1875
- down_weight: bfloat16 [2, 4096, 1024], P(None, 'tp', 'fsdp'), may hold values from -0.125 to 0.125
- qv_bias: float32 [2, 2, 1024], P(None, None, 'tp'), may hold values from -3 to 3
- up_bias: float32 [2, 4096], P(None, 'tp'), may hold values from -2 to 2
- norm_gains: float32 [2, 2, 1024], replicated, may hold values from 0.25 to 1.75
- row_biases: float32 [2, 4, 1024], replicated, may hold values from -2 to 2
- parent_ids: int32 [32], replicated, may hold values from 0 to 30, as said below
- depth_offsets: int32 [32], replicated, may hold values from 0 to 1920, as said below
- cotangent: bfloat16 [4096, 1024], P(('fsdp', 'ctx', 'tp')), may hold values from -6 to 6
Outputs:
- output: bfloat16 [4096, 1024], P(('fsdp', 'ctx', 'tp'))
- input_grad: float32 [4096, 1024], P(('fsdp', 'ctx', 'tp'))
- qkv_weight_grad: float32 [2, 1024, 3, 1024], P(None, 'fsdp', None, 'tp')
- out_weight_grad: float32 [2, 1024, 1024], P(None, 'tp', 'fsdp')
- up_weight_grad: float32 [2, 1024, 4096], P(None, 'fsdp', 'tp')
- down_weight_grad: float32 [2, 4096, 1024], P(None, 'tp', 'fsdp')
- qv_bias_grad: float32 [2, 2, 1024], P(None, None, 'tp')
- up_bias_grad: float32 [2, 4096], P(None, 'tp')
- gain_grad: float32 [2, 2, 1024], replicated
- bias_grad: float32 [2, 4, 1024], replicated
Inputs may be any that keep to these rules, and one draw needn't show every extreme that they name: `parent_ids`: segments form trees of 16 consecutive segments, starting at multiples of 16; a tree's first segment is its root and its own parent; any other segment's parent is an earlier segment of the same tree. In the last tree every other segment's parent is the segment just before it. `depth_offsets`: A root's depth offset is 0; any other segment's is its parent's plus 128.
All inputs are finite; a program needn't handle non-finite values.
Results may differ from a plain program's by a relative error of at most 0.023.
Values may be sent and summed in bfloat16 or wider, within the bound.
No kernel may reach another device: no remote copies, remote signals or barrier semaphores. Data moves between devices by JAX's collectives and lax.ppermute only.
A program may use at most 384 MiB of HBM per device.

v0:
```python
import jax
import jax.numpy as jnp
from jax import lax
from jax.sharding import PartitionSpec as P

HEAD_DIM = 128
LAYERS = 2
SEG = 128
TREE_MAX = 64


EPSILON = 1e-05
MASKED = -1e30


def layer_norm(values, gain, shift):
    centered = values - jnp.mean(values, axis=-1, keepdims=True)
    variance = jnp.mean(centered * centered, axis=-1, keepdims=True)
    return centered * lax.rsqrt(variance + EPSILON) * gain + shift


def smooth_act(values):
    return jax.nn.gelu(values, approximate=True)


def whole_group(values):
    return lax.all_gather(values, "tp", axis=0, tiled=True)


def own_rows(partial_value):
    return lax.psum_scatter(
        partial_value.astype(jnp.bfloat16), "tp", scatter_dimension=0, tiled=True
    ).astype(jnp.float32)


def layer_weights(qkv_weight, out_weight, up_weight, down_weight, layer_index):
    return (
        lax.all_gather(qkv_weight[layer_index], "fsdp", axis=0, tiled=True),
        lax.all_gather(out_weight[layer_index], "fsdp", axis=1, tiled=True),
        lax.all_gather(up_weight[layer_index], "fsdp", axis=0, tiled=True),
        lax.all_gather(down_weight[layer_index], "fsdp", axis=1, tiled=True),
    )


def reduce_weights(grads):
    shards = (
        lax.psum_scatter(
            grads[0].astype(jnp.bfloat16), "fsdp", scatter_dimension=1, tiled=True
        ).astype(jnp.float32),
        lax.psum_scatter(
            grads[1].astype(jnp.bfloat16), "fsdp", scatter_dimension=2, tiled=True
        ).astype(jnp.float32),
        lax.psum_scatter(
            grads[2].astype(jnp.bfloat16), "fsdp", scatter_dimension=1, tiled=True
        ).astype(jnp.float32),
        lax.psum_scatter(
            grads[3].astype(jnp.bfloat16), "fsdp", scatter_dimension=2, tiled=True
        ).astype(jnp.float32),
    )
    return (
        lax.psum(shards[0].astype(jnp.bfloat16), "ctx").astype(jnp.float32),
        lax.psum(shards[1].astype(jnp.bfloat16), "ctx").astype(jnp.float32),
        lax.psum(shards[2].astype(jnp.bfloat16), "ctx").astype(jnp.float32),
        lax.psum(shards[3].astype(jnp.bfloat16), "ctx").astype(jnp.float32),
    )


def path_scores(query_b, keys_b, slopes, distance, allowed):
    products = jnp.einsum("qhd,khd->hqk", query_b, keys_b, preferred_element_type=jnp.float32)
    scores = products * HEAD_DIM ** (-0.5) - slopes[:, None, None] * distance[None]
    return jnp.where(allowed[None], scores, MASKED)


def attend(query_b, keys_b, values_b, slopes, distance, allowed):
    scores = path_scores(query_b, keys_b, slopes, distance, allowed)
    row_top = jnp.max(scores, axis=-1, keepdims=True)
    log_total = row_top + jnp.log(jnp.sum(jnp.exp(scores - row_top), axis=-1, keepdims=True))
    probs_b = jnp.exp(scores - log_total).astype(jnp.bfloat16)
    context = jnp.einsum("hqk,khd->qhd", probs_b, values_b, preferred_element_type=jnp.float32)
    return (context, log_total)


def attend_back(query_b, keys_b, values_b, log_total, d_context_b, slopes, distance, allowed):
    scores = path_scores(query_b, keys_b, slopes, distance, allowed)
    probs = jnp.exp(scores - log_total)
    probs_b = probs.astype(jnp.bfloat16)
    d_probs = jnp.einsum("qhd,khd->hqk", d_context_b, values_b, preferred_element_type=jnp.float32)
    d_scores_b = (probs * (d_probs - jnp.sum(probs * d_probs, axis=-1, keepdims=True))).astype(
        jnp.bfloat16
    )
    d_query = jnp.einsum(
        "hqk,khd->qhd", d_scores_b, keys_b, preferred_element_type=jnp.float32
    ) * HEAD_DIM ** (-0.5)
    d_keys = jnp.einsum(
        "hqk,qhd->khd", d_scores_b, query_b, preferred_element_type=jnp.float32
    ) * HEAD_DIM ** (-0.5)
    d_values = jnp.einsum("hqk,qhd->khd", probs_b, d_context_b, preferred_element_type=jnp.float32)
    return (d_query, d_keys, d_values)


def on_device(
    tokens,
    qkv_weight,
    out_weight,
    up_weight,
    down_weight,
    qv_bias,
    up_bias,
    norm_gains,
    row_biases,
    parent_ids,
    depth_offsets,
    cotangent,
):
    group_count = tokens.shape[0] * lax.axis_size("tp")
    local_heads = qkv_weight.shape[3] // HEAD_DIM
    local_width = qkv_weight.shape[3]
    seg_local = group_count // SEG
    half_segs = seg_local * lax.axis_size("ctx")
    half_start = lax.axis_index("fsdp") * half_segs
    first_local = lax.axis_index("ctx") * seg_local
    half_parents = lax.dynamic_slice_in_dim(parent_ids, half_start, half_segs) - half_start
    half_depths = lax.dynamic_slice_in_dim(depth_offsets, half_start, half_segs)
    key_segments = jnp.arange(half_segs, dtype=jnp.int32)
    query_segments = first_local + jnp.arange(seg_local, dtype=jnp.int32)

    def climb(step_index, state):
        current, member = state
        upward = jnp.sum(
            jnp.where(current[:, None] == key_segments[None, :], half_parents[None, :], 0), axis=1
        )
        return (upward, member | (upward[:, None] == key_segments[None, :]))

    same_segment = query_segments[:, None] == key_segments[None, :]
    ignored, member = lax.fori_loop(0, TREE_MAX, climb, (query_segments, same_segment))
    strict = member & jnp.logical_not(same_segment)
    positions = jnp.arange(SEG, dtype=jnp.int32)
    earlier = positions[None, :] <= positions[:, None]
    allowed = strict[:, None, :, None] | same_segment[:, None, :, None] & earlier[None, :, None, :]
    allowed = allowed.reshape(group_count, half_segs * SEG)
    query_offsets = lax.dynamic_slice_in_dim(half_depths, first_local, seg_local)
    query_depth = (query_offsets[:, None] + positions[None, :]).reshape(-1)
    key_depth = (half_depths[:, None] + positions[None, :]).reshape(-1)
    distance = (query_depth[:, None] - key_depth[None, :]).astype(jnp.float32)
    head_ids = lax.axis_index("tp") * local_heads + jnp.arange(local_heads, dtype=jnp.int32)
    slopes = jnp.exp2(-(head_ids + 1).astype(jnp.float32))

    def to_heads(values):
        return values.reshape(values.shape[0], local_heads, HEAD_DIM)

    hidden = tokens.astype(jnp.float32)
    saved = []
    for layer_index in range(LAYERS):
        w_qkv, w_out, w_up, w_down = layer_weights(
            qkv_weight, out_weight, up_weight, down_weight, layer_index
        )
        normed_all = whole_group(
            layer_norm(hidden, norm_gains[layer_index, 0], row_biases[layer_index, 0]).astype(
                jnp.bfloat16
            )
        )
        projected = jnp.einsum("td,dcf->tcf", normed_all, w_qkv, preferred_element_type=jnp.float32)
        query_b = (projected[:, 0] + qv_bias[layer_index, 0]).astype(jnp.bfloat16)
        keys_b = projected[:, 1].astype(jnp.bfloat16)
        values_b = (projected[:, 2] + qv_bias[layer_index, 1]).astype(jnp.bfloat16)
        keys_all, values_all = (
            lax.all_gather(keys_b, "ctx", axis=0, tiled=True),
            lax.all_gather(values_b, "ctx", axis=0, tiled=True),
        )
        context, log_total = attend(
            to_heads(query_b), to_heads(keys_all), to_heads(values_all), slopes, distance, allowed
        )
        context_b = context.reshape(group_count, local_width).astype(jnp.bfloat16)
        attended = (
            own_rows(jnp.dot(context_b, w_out, preferred_element_type=jnp.float32))
            + row_biases[layer_index, 1]
        )
        middle = hidden + attended
        normed_two_all = whole_group(
            layer_norm(middle, norm_gains[layer_index, 1], row_biases[layer_index, 2]).astype(
                jnp.bfloat16
            )
        )
        pre_act = (
            jnp.dot(normed_two_all, w_up, preferred_element_type=jnp.float32) + up_bias[layer_index]
        )
        activity_b = smooth_act(pre_act).astype(jnp.bfloat16)
        branch = (
            own_rows(jnp.dot(activity_b, w_down, preferred_element_type=jnp.float32))
            + row_biases[layer_index, 3]
        )
        kept_keys = None
        saved.append(
            (
                hidden,
                middle,
                normed_all,
                query_b,
                keys_b,
                values_b,
                log_total,
                context_b,
                normed_two_all,
                pre_act,
                activity_b,
                kept_keys,
            )
        )
        hidden = middle + branch
    output = hidden.astype(jnp.bfloat16)
    grad = cotangent.astype(jnp.float32)
    weight_parts = [None] * LAYERS
    qv_parts = [None] * LAYERS
    up_parts = [None] * LAYERS
    gain_parts = [None] * LAYERS
    shift_parts = [None] * LAYERS
    for layer_index in reversed(range(LAYERS)):
        (
            hidden_in,
            middle,
            normed_all,
            query_b,
            keys_b,
            values_b,
            log_total,
            context_b,
            normed_two_all,
            pre_act,
            activity_b,
            kept_keys,
        ) = saved[layer_index]
        w_qkv, w_out, w_up, w_down = layer_weights(
            qkv_weight, out_weight, up_weight, down_weight, layer_index
        )
        branch_grad_b = grad.astype(jnp.bfloat16)
        branch_all = whole_group(branch_grad_b)
        d_down = jnp.einsum("tf,td->fd", activity_b, branch_all, preferred_element_type=jnp.float32)
        d_activity = jnp.einsum("td,fd->tf", branch_all, w_down, preferred_element_type=jnp.float32)
        ignored, pull_act = jax.vjp(smooth_act, pre_act)
        d_pre_b = pull_act(d_activity)[0].astype(jnp.bfloat16)
        d_up = jnp.einsum("td,tf->df", normed_two_all, d_pre_b, preferred_element_type=jnp.float32)
        d_normed_two = own_rows(
            jnp.einsum("tf,df->td", d_pre_b, w_up, preferred_element_type=jnp.float32)
        )
        ignored, pull_middle = jax.vjp(
            layer_norm, middle, norm_gains[layer_index, 1], row_biases[layer_index, 2]
        )
        d_middle_norm, d_gain_two, d_shift_two = pull_middle(d_normed_two)
        d_middle = grad + d_middle_norm
        attend_grad_b = d_middle.astype(jnp.bfloat16)
        attend_all = whole_group(attend_grad_b)
        d_out = jnp.einsum("tf,td->fd", context_b, attend_all, preferred_element_type=jnp.float32)
        d_context_b = jnp.einsum(
            "td,fd->tf", attend_all, w_out, preferred_element_type=jnp.float32
        ).astype(jnp.bfloat16)
        keys_all, values_all = (
            lax.all_gather(keys_b, "ctx", axis=0, tiled=True),
            lax.all_gather(values_b, "ctx", axis=0, tiled=True),
        )
        d_query, d_keys, d_values = attend_back(
            to_heads(query_b),
            to_heads(keys_all),
            to_heads(values_all),
            log_total,
            to_heads(d_context_b),
            slopes,
            distance,
            allowed,
        )
        key_terms = jnp.stack(
            (d_keys.reshape(-1, local_width), d_values.reshape(-1, local_width)), axis=1
        )
        key_grads = lax.psum_scatter(
            key_terms.astype(jnp.bfloat16), "ctx", scatter_dimension=0, tiled=True
        ).astype(jnp.float32)
        d_query_b = d_query.reshape(group_count, local_width).astype(jnp.bfloat16)
        d_keys_b = key_grads[:, 0].astype(jnp.bfloat16)
        d_values_b = key_grads[:, 1].astype(jnp.bfloat16)
        d_projected = jnp.stack((d_query_b, d_keys_b, d_values_b), axis=1)
        d_qkv = jnp.einsum(
            "td,tcf->dcf", normed_all, d_projected, preferred_element_type=jnp.float32
        )
        d_normed = own_rows(
            jnp.einsum("tcf,dcf->td", d_projected, w_qkv, preferred_element_type=jnp.float32)
        )
        ignored, pull_input = jax.vjp(
            layer_norm, hidden_in, norm_gains[layer_index, 0], row_biases[layer_index, 0]
        )
        d_input_norm, d_gain_one, d_shift_one = pull_input(d_normed)
        grad = d_middle + d_input_norm
        qv_parts[layer_index] = jnp.stack(
            (
                jnp.sum(d_query_b.astype(jnp.float32), axis=0),
                jnp.sum(d_values_b.astype(jnp.float32), axis=0),
            )
        )
        up_parts[layer_index] = jnp.sum(d_pre_b.astype(jnp.float32), axis=0)
        gain_parts[layer_index] = jnp.stack((d_gain_one, d_gain_two))
        shift_parts[layer_index] = jnp.stack(
            (
                d_shift_one,
                jnp.sum(attend_grad_b.astype(jnp.float32), axis=0),
                d_shift_two,
                jnp.sum(branch_grad_b.astype(jnp.float32), axis=0),
            )
        )
        layer_grads = (d_qkv, d_out, d_up, d_down)
        weight_parts[layer_index] = reduce_weights(
            tuple((member_grad[None] for member_grad in layer_grads))
        )
    reduced = tuple(
        (
            jnp.concatenate(
                [weight_parts[layer_index][slot_index] for layer_index in range(LAYERS)], axis=0
            )
            for slot_index in range(4)
        )
    )
    qv_grad, up_grad = lax.psum((jnp.stack(qv_parts), jnp.stack(up_parts)), ("fsdp", "ctx"))
    gain_grad, shift_grad = lax.psum(
        (jnp.stack(gain_parts), jnp.stack(shift_parts)), ("fsdp", "ctx", "tp")
    )
    return (
        output,
        grad,
        reduced[0],
        reduced[1],
        reduced[2],
        reduced[3],
        qv_grad,
        up_grad,
        gain_grad,
        shift_grad,
    )


def solution(mesh):
    in_specs = (
        P(("fsdp", "ctx", "tp"), None),
        P(None, "fsdp", None, "tp"),
        P(None, "tp", "fsdp"),
        P(None, "fsdp", "tp"),
        P(None, "tp", "fsdp"),
        P(None, None, "tp"),
        P(None, "tp"),
        P(),
        P(),
        P(),
        P(),
        P(("fsdp", "ctx", "tp"), None),
    )
    out_specs = (
        P(("fsdp", "ctx", "tp"), None),
        P(("fsdp", "ctx", "tp"), None),
        P(None, "fsdp", None, "tp"),
        P(None, "tp", "fsdp"),
        P(None, "fsdp", "tp"),
        P(None, "tp", "fsdp"),
        P(None, None, "tp"),
        P(None, "tp"),
        P(),
        P(),
    )
    return jax.shard_map(
        on_device, mesh=mesh, in_specs=in_specs, out_specs=out_specs, check_vma=False
    )
```

profile of v0, /device:TPU:0, one launch (start us, length us, event | category | flops | bytes accessed | tf_op | source)
XLA Modules:
  0.0 1745.8 jit_solution(16552032611406206770)
XLA Ops:
  14.5 44.5 %all-gather.27.cloned.1.call-done = bf16[1,1024,3,512]{3,1,2,0:T(8,128)(2,1)} async-done(((bf16[1,512,3,512]{3,1,2,0:T(8,128)(2,1)}), bf16[1,1024,3,512]{3,1,2,0:T(8,128)(2,1)}) %all-gather.27.cloned.1.call-update) | async-done | bytes 3145744 | tf_op jit(solution)/shard_map/all_gather | solution.py:38
  64.9 17.4 while.14
  85.2 27.3 %all-gather.29.cloned.1.call-done = bf16[2048,1,512]{2,0,1:T(8,128)(2,1)} async-done(((bf16[256,1,512]{2,0,1:T(8,128)(2,1)}), bf16[2048,1,512]{2,0,1:T(8,128)(2,1)}) %all-gather.29.cloned.1.call-update) | async-done | bytes 2097168 | tf_op jit(solution)/shard_map/all_gather | solution.py:167
  124.1 39.0 %all-gather.23.cloned.1.call-done = bf16[2048,512]{1,0:T(8,128)(2,1)} async-done(((bf16[256,512]{1,0:T(8,128)(2,1)}), bf16[2048,512]{1,0:T(8,128)(2,1)}) %all-gather.23.cloned.1.call-update) | async-done | bytes 2097168 | tf_op jit(solution)/shard_map/all_gather | solution.py:168
  168.7 16.1 all-gather.31.cloned.1.call-done
  203.6 51.3 %all-gather.33.cloned.1.call-done = bf16[1,1024,2048]{2,1,0:T(8,128)(2,1)} async-done(((bf16[1,512,2048]{2,1,0:T(8,128)(2,1)}), bf16[1,1024,2048]{2,1,0:T(8,128)(2,1)}) %all-gather.33.cloned.1.call-update) | async-done | bytes 4194320 | tf_op jit(solution)/shard_map/all_gather | solution.py:40
  259.7 54.1 %all-gather.35.cloned.1.call-done = bf16[1,2048,1024]{2,1,0:T(8,128)(2,1)} async-done(((bf16[1,2048,512]{2,1,0:T(8,128)(2,1)}), bf16[1,2048,1024]{2,1,0:T(8,128)(2,1)}) %all-gather.35.cloned.1.call-update) | async-done | bytes 4194320 | tf_op jit(solution)/shard_map/all_gather | solution.py:41
  319.8 7.3 reduce-scatter.21.cloned.1.call-done
  330.9 43.9 %all-gather.37.cloned.1.call-done = bf16[1,1024,3,512]{3,1,2,0:T(8,128)(2,1)} async-done(((bf16[1,512,3,512]{3,1,2,0:T(8,128)(2,1)}), bf16[1,1024,3,512]{3,1,2,0:T(8,128)(2,1)}) %all-gather.37.cloned.1.call-update) | async-done | bytes 3145744 | tf_op jit(solution)/shard_map/all_gather | solution.py:38
  380.9 47.0 %all-gather.39.cloned.1.call-done = bf16[2048,1,512]{2,0,1:T(8,128)(2,1)} async-done(((bf16[256,1,512]{2,0,1:T(8,128)(2,1)}), bf16[2048,1,512]{2,0,1:T(8,128)(2,1)}) %all-gather.39.cloned.1.call-update) | async-done | bytes 2097168 | tf_op jit(solution)/shard_map/all_gather | solution.py:167
  439.6 38.2 %all-gather.25.cloned.1.call-done = bf16[2048,512]{1,0:T(8,128)(2,1)} async-done(((bf16[256,512]{1,0:T(8,128)(2,1)}), bf16[2048,512]{1,0:T(8,128)(2,1)}) %all-gather.25.cloned.1.call-update) | async-done | bytes 2097168 | tf_op jit(solution)/shard_map/all_gather | solution.py:168
  483.5 16.1 all-gather.41.cloned.1.call-done
  514.5 55.3 %all-gather.43.cloned.1.call-done = bf16[1,1024,2048]{2,1,0:T(8,128)(2,1)} async-done(((bf16[1,512,2048]{2,1,0:T(8,128)(2,1)}), bf16[1,1024,2048]{2,1,0:T(8,128)(2,1)}) %all-gather.43.cloned.1.call-update) | async-done | bytes 4194320 | tf_op jit(solution)/shard_map/all_gather | solution.py:40
  574.6 54.1 %all-gather.45.cloned.1.call-done = bf16[1,2048,1024]{2,1,0:T(8,128)(2,1)} async-done(((bf16[1,2048,512]{2,1,0:T(8,128)(2,1)}), bf16[1,2048,1024]{2,1,0:T(8,128)(2,1)}) %all-gather.45.cloned.1.call-update) | async-done | bytes 4194320 | tf_op jit(solution)/shard_map/all_gather | solution.py:41
  645.7 10.6 reduce-scatter.25.cloned.1.call-done
  662.8 6.5 convolution_convert_fusion.1
  695.9 82.2 %reduce-scatter.29.cloned.1.call-done = bf16[256,2,512]{2,0,1:T(8,128)(2,1)} async-done(((bf16[2048,2,512]{2,0,1:T(8,128)(2,1)}), bf16[256,2,512]{2,0,1:T(8,128)(2,1)}) %reduce-scatter.29.cloned.1.call-update) | async-done | bytes 524304 | tf_op jit(solution)/shard_map/reduce_scatter | solution.py:273
  782.0 7.8 reduce-scatter.31.cloned.1.call-done
  802.6 9.2 reduce-scatter.33.cloned.1.call-done
  818.5 6.5 convolution_convert_fusion
  876.9 56.9 %reduce-scatter.35.cloned.1.call-done = bf16[256,2,512]{2,0,1:T(8,128)(2,1)} async-done(((bf16[2048,2,512]{2,0,1:T(8,128)(2,1)}), bf16[256,2,512]{2,0,1:T(8,128)(2,1)}) %reduce-scatter.35.cloned.1.call-update) | async-done | bytes 524304 | tf_op jit(solution)/shard_map/reduce_scatter | solution.py:273
  942.4 14.5 reduce-scatter.45.cloned.1.call-done
  956.9 57.2 %reduce-scatter.49.cloned.1.call-done = bf16[1,512,2048]{2,1,0:T(8,128)(2,1)} async-done(((bf16[1,1024,2048]{2,1,0:T(8,128)(2,1)}), bf16[1,512,2048]{2,1,0:T(8,128)(2,1)}) %reduce-scatter.49.cloned.1.call-update) | async-done | bytes 2097168 | tf_op jit(solution)/shard_map/reduce_scatter | solution.py:53
  1014.1 56.6 %reduce-scatter.53.cloned.1.call-done = bf16[1,2048,512]{2,1,0:T(8,128)(2,1)} async-done(((bf16[1,2048,1024]{2,1,0:T(8,128)(2,1)}), bf16[1,2048,512]{2,1,0:T(8,128)(2,1)}) %reduce-scatter.53.cloned.1.call-update) | async-done | bytes 2097168 | tf_op jit(solution)/shard_map/reduce_scatter | solution.py:56
  1070.7 22.6 %reduce-scatter.43.cloned.1.call-done = bf16[1,512,512]{2,1,0:T(8,128)(2,1)} async-done(((bf16[1,512,1024]{2,1,0:T(8,128)(2,1)}), bf16[1,512,512]{2,1,0:T(8,128)(2,1)}) %reduce-scatter.43.cloned.1.call-update) | async-done | bytes 524304 | tf_op jit(solution)/shard_map/reduce_scatter | solution.py:50
  1093.3 45.6 %reduce-scatter.41.cloned.1.call-done = bf16[1,512,3,512]{3,1,2,0:T(8,128)(2,1)} async-done(((bf16[1,1024,3,512]{3,1,2,0:T(8,128)(2,1)}), bf16[1,512,3,512]{3,1,2,0:T(8,128)(2,1)}) %reduce-scatter.41.cloned.1.call-update) | async-done | bytes 1572880 | tf_op jit(solution)/shard_map/reduce_scatter | solution.py:47
  1138.8 56.5 %reduce-scatter.51.cloned.1.call-done = bf16[1,2048,512]{2,1,0:T(8,128)(2,1)} async-done(((bf16[1,2048,1024]{2,1,0:T(8,128)(2,1)}), bf16[1,2048,512]{2,1,0:T(8,128)(2,1)}) %reduce-scatter.51.cloned.1.call-update) | async-done | bytes 2097168 | tf_op jit(solution)/shard_map/reduce_scatter | solution.py:56
  1195.3 56.7 %reduce-scatter.47.cloned.1.call-done = bf16[1,512,2048]{2,1,0:T(8,128)(2,1)} async-done(((bf16[1,1024,2048]{2,1,0:T(8,128)(2,1)}), bf16[1,512,2048]{2,1,0:T(8,128)(2,1)}) %reduce-scatter.47.cloned.1.call-update) | async-done | bytes 2097168 | tf_op jit(solution)/shard_map/reduce_scatter | solution.py:53
  1252.1 46.2 %reduce-scatter.39.cloned.1.call-done = bf16[1,512,3,512]{3,1,2,0:T(8,128)(2,1)} async-done(((bf16[1,1024,3,512]{3,1,2,0:T(8,128)(2,1)}), bf16[1,512,3,512]{3,1,2,0:T(8,128)(2,1)}) %reduce-scatter.39.cloned.1.call-update) | async-done | bytes 1572880 | tf_op jit(solution)/shard_map/reduce_scatter | solution.py:47
  1299.5 79.1 %all-reduce.1 = (f32[2,2,512]{2,1,0:T(2,128)}, f32[2,2048]{1,0:T(2,128)}) all-reduce(f32[2,2,512]{2,1,0:T(2,128)S(1)} %pad_maximum_fusion.11, f32[2,2048]{1,0:T(2,128)S(1)} %pad_maximum_fusion.9), channel_id=1, replica_groups=mesh['fsdp'=2,'ctx'=8,'tp'=2] {'fsdp','ctx'}, use_global_device_ids=true, to_apply=%region_55.56 | all-reduce | flops 6144 | bytes 49152 | tf_op jit(solution)/shard_map/psum | solution.py:319
  1381.2 42.2 %all-reduce = (f32[2,2,1024]{2,1,0:T(2,128)}, f32[2,4,1024]{2,1,0:T(4,128)}) all-reduce(f32[2,2,1024]{2,1,0:T(2,128)S(1)} %pad_maximum_fusion.10, f32[2,4,1024]{2,1,0:T(4,128)S(1)} %pad_maximum_fusion.8), channel_id=1, replica_groups=mesh['fsdp'=2,'ctx'=8,'tp'=2] {'fsdp','ctx','tp'}, use_global_device_ids=true, to_apply=%region_63.64 | all-reduce | flops 12288 | bytes 98304 | tf_op jit(solution)/shard_map/psum | solution.py:320
  1425.6 296.8 %all-reduce.5.cloned.1.call-done = (bf16[1,512,3,512]{3,1,2,0:T(8,128)(2,1)}, bf16[1,512,3,512]{3,1,2,0:T(8,128)(2,1)}, bf16[1,512,512]{2,1,0:T(8,128)(2,1)}, bf...) async-done(((bf16[1,512,3,512]{3,1,2,0:T(8,128)(2,1)}, ...) | async-done | bytes 12582928 | tf_op jit(solution)/shard_map/psum | solution.py:61
  (554 shorter events, 281.9 us)
Async XLA Ops:
  7.2 51.8 %all-gather.27.cloned.1.call-start = ((), (), s32[]{:S(2)}) async-start(), calls=%async_computation.38 | async-start | bytes 4718592 | tf_op jit(solution)/shard_map/all_gather | solution.py:38
  11.2 101.3 %all-gather.29.cloned.1.call-start = ((), (), s32[]{:S(2)}) async-start(), calls=%async_computation.39 | async-start | bytes 2359296 | tf_op jit(solution)/shard_map/all_gather | solution.py:167
  62.7 100.4 %all-gather.23.cloned.1.call-start = ((), (), s32[]{:S(2)}) async-start(), calls=%async_computation.18 | async-start | bytes 2359296 | tf_op jit(solution)/shard_map/all_gather | solution.py:168
  63.5 121.3 %all-gather.31.cloned.1.call-start = ((), (), s32[]{:S(2)}) async-start(), calls=%async_computation.40 | async-start | bytes 1572864 | tf_op jit(solution)/shard_map/all_gather | solution.py:39
  64.6 133.1 %reduce-scatter.19.cloned.1.call-start = ((), (), s32[]{:S(2)}) async-start(), calls=%async_computation.19 | async-start | bytes 786432 | tf_op jit(solution)/shard_map/reduce_scatter | solution.py:31
  187.4 67.5 %all-gather.33.cloned.1.call-start = ((), (), s32[]{:S(2)}) async-start(), calls=%async_computation.41 | async-start | bytes 6291456 | tf_op jit(solution)/shard_map/all_gather | solution.py:40
  192.3 121.6 %all-gather.35.cloned.1.call-start = ((), (), s32[]{:S(2)}) async-start(), calls=%async_computation.42 | async-start | bytes 6291456 | tf_op jit(solution)/shard_map/all_gather | solution.py:41
  197.0 130.1 %reduce-scatter.21.cloned.1.call-start = ((), (), s32[]{:S(2)}) async-start(), calls=%async_computation.20 | async-start | bytes 786432 | tf_op jit(solution)/shard_map/reduce_scatter | solution.py:31
  319.0 55.8 %all-gather.37.cloned.1.call-start = ((), (), s32[]{:S(2)}) async-start(), calls=%async_computation.43 | async-start | bytes 4718592 | tf_op jit(solution)/shard_map/all_gather | solution.py:38
  319.7 108.1 %all-gather.39.cloned.1.call-start = ((), (), s32[]{:S(2)}) async-start(), calls=%async_computation.44 | async-start | bytes 2359296 | tf_op jit(solution)/shard_map/all_gather | solution.py:167
  378.4 99.4 %all-gather.25.cloned.1.call-start = ((), (), s32[]{:S(2)}) async-start(), calls=%async_computation.21 | async-start | bytes 2359296 | tf_op jit(solution)/shard_map/all_gather | solution.py:168
  379.2 120.4 %all-gather.41.cloned.1.call-start = ((), (), s32[]{:S(2)}) async-start(), calls=%async_computation.45 | async-start | bytes 1572864 | tf_op jit(solution)/shard_map/all_gather | solution.py:39
  379.8 130.6 %reduce-scatter.23.cloned.1.call-start = ((), (), s32[]{:S(2)}) async-start(), calls=%async_computation.22 | async-start | bytes 786432 | tf_op jit(solution)/shard_map/reduce_scatter | solution.py:31
  502.1 67.7 %all-gather.43.cloned.1.call-start = ((), (), s32[]{:S(2)}) async-start(), calls=%async_computation.46 | async-start | bytes 6291456 | tf_op jit(solution)/shard_map/all_gather | solution.py:40
  502.7 125.9 %all-gather.45.cloned.1.call-start = ((), (), s32[]{:S(2)}) async-start(), calls=%async_computation.47 | async-start | bytes 6291456 | tf_op jit(solution)/shard_map/all_gather | solution.py:41
  503.3 141.2 %reduce-scatter.27.cloned.1.call-start = ((), (), s32[]{:S(2)}) async-start(), calls=%async_computation.24 | async-start | bytes 786432 | tf_op jit(solution)/shard_map/reduce_scatter | solution.py:31
  636.3 19.9 %reduce-scatter.25.cloned.1.call-start = ((), (), s32[]{:S(2)}) async-start(), calls=%async_computation.23 | async-start | bytes 786432 | tf_op jit(solution)/shard_map/reduce_scatter | solution.py:31
  641.5 136.5 %reduce-scatter.29.cloned.1.call-start = ((), (), s32[]{:S(2)}) async-start(), calls=%async_computation.25 | async-start | bytes 4718592 | tf_op jit(solution)/shard_map/reduce_scatter | solution.py:273
  688.8 101.0 %reduce-scatter.31.cloned.1.call-start = ((), (), s32[]{:S(2)}) async-start(), calls=%async_computation.26 | async-start | bytes 786432 | tf_op jit(solution)/shard_map/reduce_scatter | solution.py:31
  781.9 29.9 %reduce-scatter.33.cloned.1.call-start = ((), (), s32[]{:S(2)}) async-start(), calls=%async_computation.27 | async-start | bytes 786432 | tf_op jit(solution)/shard_map/reduce_scatter | solution.py:31
  802.5 131.3 %reduce-scatter.35.cloned.1.call-start = ((), (), s32[]{:S(2)}) async-start(), calls=%async_computation.28 | async-start | bytes 4718592 | tf_op jit(solution)/shard_map/reduce_scatter | solution.py:273
  844.5 112.4 %reduce-scatter.45.cloned.1.call-start = ((), (), s32[]{:S(2)}) async-start(), calls=%async_computation.33 | async-start | bytes 1572864 | tf_op jit(solution)/shard_map/reduce_scatter | solution.py:50
  847.0 167.1 %reduce-scatter.49.cloned.1.call-start = ((), (), s32[]{:S(2)}) async-start(), calls=%async_computation.35 | async-start | bytes 6291456 | tf_op jit(solution)/shard_map/reduce_scatter | solution.py:53
  850.6 220.0 %reduce-scatter.53.cloned.1.call-start = ((), (), s32[]{:S(2)}) async-start(), calls=%async_computation.37 | async-start | bytes 6291456 | tf_op jit(solution)/shard_map/reduce_scatter | solution.py:56
  856.0 237.3 %reduce-scatter.43.cloned.1.call-start = ((), (), s32[]{:S(2)}) async-start(), calls=%async_computation.32 | async-start | bytes 1572864 | tf_op jit(solution)/shard_map/reduce_scatter | solution.py:50
  858.4 280.4 %reduce-scatter.41.cloned.1.call-start = ((), (), s32[]{:S(2)}) async-start(), calls=%async_computation.31 | async-start | bytes 4718592 | tf_op jit(solution)/shard_map/reduce_scatter | solution.py:47
  861.2 334.1 %reduce-scatter.51.cloned.1.call-start = ((), (), s32[]{:S(2)}) async-start(), calls=%async_computation.36 | async-start | bytes 6291456 | tf_op jit(solution)/shard_map/reduce_scatter | solution.py:56
  866.6 385.5 %reduce-scatter.47.cloned.1.call-start = ((), (), s32[]{:S(2)}) async-start(), calls=%async_computation.34 | async-start | bytes 6291456 | tf_op jit(solution)/shard_map/reduce_scatter | solution.py:53
  871.3 427.0 %reduce-scatter.39.cloned.1.call-start = ((), (), s32[]{:S(2)}) async-start(), calls=%async_computation.30 | async-start | bytes 4718592 | tf_op jit(solution)/shard_map/reduce_scatter | solution.py:47
  937.6 441.0 %reduce-scatter.37.cloned.1.call-start = ((), (), s32[]{:S(2)}) async-start(), calls=%async_computation.29 | async-start | bytes 786432 | tf_op jit(solution)/shard_map/reduce_scatter | solution.py:31
  942.3 780.1 %all-reduce.5.cloned.1.call-start = ((), (), s32[]{:S(2)}) async-start(), calls=%async_computation.48 | async-start | bytes 25165824 | tf_op jit(solution)/shard_map/psum | solution.py:61
  1299.3 124.1 %copy-start.24 = (bf16[128,1024]{1,0:T(8,128)(2,1)S(1)}, bf16[128,1024]{1,0:T(8,128)(2,1)}, u32[]{:S(2)}) copy-start(bf16[128,1024]{1,0:T(8,128)(2,1)} %reduce-scatter.33.cloned.1.call-done) | copy-start | bytes 786436
  (74 other events, 897.7 us)
Sparse Core Ops, SparseCore 0:
  11.3 47.6 all-gather.26
  62.8 49.7 all-gather.28
  115.2 47.7 all-gather.22
  165.0 19.7 all-gather.30
  187.5 7.9 reduce-scatter.18
  196.9 57.8 all-gather.32
  257.1 56.7 all-gather.34
  319.1 7.9 reduce-scatter.20
  328.6 46.0 all-gather.36
  378.5 49.2 all-gather.38
  430.0 47.7 all-gather.24
  479.8 19.7 all-gather.40
  502.4 7.9 reduce-scatter.22
  511.8 57.8 all-gather.42
  571.8 56.7 all-gather.44
  636.4 7.9 reduce-scatter.26
  647.1 9.0 reduce-scatter.24
  688.9 89.0 reduce-scatter.28
  782.0 7.6 reduce-scatter.30
  802.6 9.1 reduce-scatter.32
  844.6 89.2 reduce-scatter.34
  936.7 20.1 reduce-scatter.44
  959.8 54.2 reduce-scatter.48
  1016.3 54.3 reduce-scatter.52
  1072.9 20.3 reduce-scatter.42
  1095.4 43.3 reduce-scatter.40
  1141.0 54.3 reduce-scatter.50
  1197.7 54.3 reduce-scatter.46
  1254.9 43.3 reduce-scatter.38
  1301.0 7.9 reduce-scatter.36
  1314.7 407.7 all-reduce.4
where the time goes:
time: 1760 us; the launch traced here: 1750 us
  waiting for transfers between devices  1320 us (75%)
  blocking collectives  140 us (8%)
  matrix products  131 us (7%)
  other arithmetic  73.2 us (4%)
  local copies, waits for them, and re-layouts  60.2 us (3%)
    psum x1, waiting for transfers between devices, reduce_weights(): lax.psum(shards[0].astype(jnp.bfloat16), 'ctx').astype(jnp.float32)  297 us
    reduce_scatter x2, waiting for transfers between devices, on_device(): lax.psum_scatter(key_terms.astype(jnp.bfloat16), 'ctx', scatter_dimension...  139 us
    reduce_scatter x2, waiting for transfers between devices, reduce_weights(): lax.psum_scatter(grads[2].astype(jnp.bfloat16), 'fsdp', scatter_dimension...  114 us
    reduce_scatter x2, waiting for transfers between devices, reduce_weights(): lax.psum_scatter(grads[3].astype(jnp.bfloat16), 'fsdp', scatter_dimension...  113 us
    all_gather x2, waiting for transfers between devices, layer_weights(): lax.all_gather(down_weight[layer_index], 'fsdp', axis=1, tiled=True)  108 us
    all_gather x2, waiting for transfers between devices, layer_weights(): lax.all_gather(up_weight[layer_index], 'fsdp', axis=0, tiled=True)  107 us
    reduce_scatter x2, waiting for transfers between devices, reduce_weights(): lax.psum_scatter(grads[0].astype(jnp.bfloat16), 'fsdp', scatter_dimension...  91.8 us
    all_gather x2, waiting for transfers between devices, layer_weights(): lax.all_gather(qkv_weight[layer_index], 'fsdp', axis=0, tiled=True)  88.4 us
  transfers between devices with their start and end apart: 31, of which 29 were waited for; matrix products, arithmetic and copies ran while one was open for 7% of the time, Pallas kernels for 0%

commit v1 on v0

v1 whole, which is shorter than its diff:
```python
import functools

import jax
import jax.numpy as jnp
from jax import lax
from jax.experimental import pallas as pl
from jax.experimental.pallas import tpu as pltpu
from jax.sharding import PartitionSpec as P

HEAD_DIM = 128
LAYERS = 2
SEG = 128
EPSILON = 1e-05
MASKED = -1e30
SCALE = HEAD_DIM ** (-0.5)
GELU_A = 0.7978845608028654
GELU_B = 0.044715
BF = jnp.bfloat16
F32 = jnp.float32
VLIM = 56 * 1024 * 1024

NN = (((1,), (0,)), ((), ()))
NT = (((1,), (1,)), ((), ()))
TN = (((0,), (0,)), ((), ()))


def mm(a, b, dims=NN):
    return lax.dot_general(a, b, dims, preferred_element_type=F32)


def sds(shape, dtype):
    return jax.ShapeDtypeStruct(shape, dtype)


VSPEC = pl.BlockSpec(memory_space=pltpu.VMEM)
SSPEC = pl.BlockSpec(memory_space=pltpu.SMEM)


def cost(flops, nbytes):
    return pl.CostEstimate(flops=int(flops), bytes_accessed=int(nbytes), transcendentals=0)


def norm_rows(v):
    centered = v - jnp.mean(v, axis=-1, keepdims=True)
    rstd = lax.rsqrt(jnp.mean(centered * centered, axis=-1, keepdims=True) + EPSILON)
    return centered * rstd, rstd


def norm_back(d, v, gain):
    xhat, rstd = norm_rows(v)
    dx = d * gain
    back = rstd * (
        dx
        - jnp.mean(dx, axis=-1, keepdims=True)
        - xhat * jnp.mean(dx * xhat, axis=-1, keepdims=True)
    )
    d_gain = jnp.sum(d * xhat, axis=0, keepdims=True)
    d_shift = jnp.sum(d, axis=0, keepdims=True)
    return back, d_gain, d_shift


class Dims:
    def __init__(self, tokens, qkv_weight, up_weight):
        self.tp = lax.axis_size("tp")
        self.C = lax.axis_size("ctx")
        self.T = tokens.shape[0] * self.tp
        self.D = tokens.shape[1]
        self.H = self.D // lax.axis_size("fsdp")
        self.Q = self.H // 2
        self.W = qkv_weight.shape[3]
        self.F = up_weight.shape[2]
        self.lh = self.W // HEAD_DIM
        self.g = self.C // self.lh
        self.rq = self.T // self.g
        self.chunk = self.rq + 2 * self.T
        self.bits = self.C.bit_length() - 1


def offs(sc, d):
    x = sc[0]
    y = sc[1]
    own = pl.multiple_of(x * d.H, d.H)
    oth = pl.multiple_of((1 - x) * d.H, d.H)
    first = pl.multiple_of((1 - x) * d.H + y * d.Q, d.Q)
    second = pl.multiple_of((1 - x) * d.H + (1 - y) * d.Q, d.Q)
    return own, oth, first, second


def qkv_body(d, first, *refs):
    if first:
        sc, hid, gain, shift, w, w1, w2, qvb = refs[:8]
        rest = refs[8:]
        hidden = hid[...].astype(F32)
    else:
        sc, mid, pa, pb, bias, gain, shift, w, w1, w2, qvb = refs[:11]
        rest = refs[11:]
        hidden = mid[...] + ((pa[...].astype(F32) + pb[...].astype(F32)) + bias[...])
    h_out, n_out, ns_out = rest[:3]
    chunks = rest[3 : 3 + d.C]
    scr = rest[3 + d.C]
    own, oth, p1, p2 = offs(sc, d)
    h_out[...] = hidden
    xhat, _ = norm_rows(hidden)
    n_out[...] = (xhat * gain[...] + shift[...]).astype(BF)
    ns_out[...] = n_out[:, pl.ds(oth, d.H)]
    a0 = n_out[:, pl.ds(own, d.H)]
    a1 = n_out[:, pl.ds(p1, d.Q)]
    a2 = n_out[:, pl.ds(p2, d.Q)]
    for n in range(3):
        proj = mm(a0, w[n]) + mm(a1, w1[n]) + mm(a2, w2[n])
        if n == 0:
            proj = proj + qvb[0:1, :]
        if n == 2:
            proj = proj + qvb[1:2, :]
        scr[n] = proj.astype(BF)
    c = sc[2]
    for o in range(d.C):
        to = lax.rem(c + o, d.C)
        col = pl.multiple_of(lax.div(to, d.g) * HEAD_DIM, HEAD_DIM)
        row = pl.multiple_of(lax.rem(to, d.g) * d.rq, d.rq)
        chunks[o][0 : d.rq, :] = scr[0, pl.ds(row, d.rq), pl.ds(col, HEAD_DIM)]
        chunks[o][d.rq : d.rq + d.T, :] = scr[1, :, pl.ds(col, HEAD_DIM)]
        chunks[o][d.rq + d.T :, :] = scr[2, :, pl.ds(col, HEAD_DIM)]


def whole(shape):
    return pl.BlockSpec(shape, lambda *_: (0,) * len(shape))


def qkv_forward(d, layer, sc, hid, gain, shift, w, pieces, qvb):
    first = not isinstance(hid, tuple)
    hid = (hid,) if first else hid
    wspec = pl.BlockSpec((None, 3, d.H, d.W), lambda i: (layer, 0, 0, 0))
    in_specs = [SSPEC] + [whole(a.shape) for a in hid]
    in_specs += [whole(gain.shape), whole(shift.shape), wspec]
    in_specs += [whole(a.shape) for a in pieces] + [whole(qvb.shape)]
    outs = [sds((d.T, d.D), F32), sds((d.T, d.D), BF), sds((d.T, d.H), BF)]
    outs += [sds((d.chunk, HEAD_DIM), BF)] * d.C
    return pl.pallas_call(
        functools.partial(qkv_body, d, first),
        grid=(1,),
        in_specs=in_specs,
        out_specs=[whole(o.shape) for o in outs],
        out_shape=outs,
        scratch_shapes=[pltpu.VMEM((3, d.T, d.W), BF)],
        compiler_params=pltpu.CompilerParams(vmem_limit_bytes=VLIM),
        cost_estimate=cost(2 * d.T * d.D * 3 * d.W, 8e6),
        name="qkv_forward",
    )(sc, *hid, gain, shift, w, *pieces, qvb)


def load_chunks(d, sc, chunks, qs, ks, vs):
    c = sc[2]
    for o in range(d.C):
        src = lax.rem(c - o + d.C, d.C)
        qs[src] = chunks[o][0 : d.rq, :]
        ks[src] = chunks[o][d.rq : d.rq + d.T, :]
        vs[src] = chunks[o][d.rq + d.T :, :]


def score_block(d, sc, kb, q, k, s, ext):
    part = lax.rem(sc[2], d.g)
    seg = s * (d.T // SEG) + lax.div(part * d.rq, SEG)
    scores = mm(q, k, NT) * SCALE + kb[pl.ds(seg, 1), 0:ext]
    col = lax.broadcasted_iota(jnp.int32, (d.rq, ext), 1) - s * d.T
    row = lax.broadcasted_iota(jnp.int32, (d.rq, ext), 0) + part * d.rq
    return jnp.where(col <= row, scores, MASKED)


UNROLL = 8


def each_source(d, one):
    if d.C <= UNROLL:
        for s in range(d.C):
            one(s, s + 1)
    else:
        lax.fori_loop(0, d.C, lambda s, carry: (one(s, d.C), carry)[1], 0)


def attend_body(d, *refs):
    sc, kb = refs[:2]
    chunks = refs[2 : 2 + d.C]
    outs = refs[2 + d.C : 2 + 2 * d.C]
    qs, ks, vs, cs = refs[2 + 2 * d.C :]
    load_chunks(d, sc, chunks, qs, ks, vs)
    def one(s, seen):
        ext = seen * d.T
        k = ks[0:seen].reshape(ext, HEAD_DIM)
        v = vs[0:seen].reshape(ext, HEAD_DIM)
        scores = score_block(d, sc, kb, qs[s], k, s, ext)
        e = jnp.exp(scores - jnp.max(scores, axis=-1, keepdims=True))
        total = jnp.sum(e, axis=-1, keepdims=True)
        cs[s] = (mm(e.astype(BF), v) / total).astype(BF)

    each_source(d, one)
    c = sc[2]
    for o in range(d.C):
        outs[o][...] = cs[lax.rem(c + o, d.C)]


def attend_forward(d, sc, kb, chunks):
    return pl.pallas_call(
        functools.partial(attend_body, d),
        in_specs=[SSPEC] + [VSPEC] * (1 + d.C),
        out_specs=[VSPEC] * d.C,
        out_shape=[sds((d.rq, HEAD_DIM), BF)] * d.C,
        scratch_shapes=[
            pltpu.VMEM((d.C, d.rq, HEAD_DIM), BF),
            pltpu.VMEM((d.C, d.T, HEAD_DIM), BF),
            pltpu.VMEM((d.C, d.T, HEAD_DIM), BF),
            pltpu.VMEM((d.C, d.rq, HEAD_DIM), BF),
        ],
        compiler_params=pltpu.CompilerParams(vmem_limit_bytes=VLIM),
        cost_estimate=cost(2 * d.C * d.rq * d.C * d.T * HEAD_DIM * 2, 3e6),
        name="attend_forward",
    )(sc, kb, *chunks)


def out_body(d, *refs):
    sc, w, w1, w2 = refs[:4]
    chunks = refs[4 : 4 + d.C]
    ctx, part = refs[4 + d.C :]
    c = sc[2]
    for o in range(d.C):
        src = lax.rem(c - o + d.C, d.C)
        col = pl.multiple_of(lax.div(src, d.g) * HEAD_DIM, HEAD_DIM)
        row = pl.multiple_of(lax.rem(src, d.g) * d.rq, d.rq)
        ctx[pl.ds(row, d.rq), pl.ds(col, HEAD_DIM)] = chunks[o][...]
    own, oth, _, _ = offs(sc, d)
    half = d.W // 2
    k1 = pl.multiple_of(sc[1] * half, half)
    k2 = pl.multiple_of((1 - sc[1]) * half, half)
    part[:, pl.ds(own, d.H)] = mm(ctx[...], w[...]).astype(BF)
    part[:, pl.ds(oth, d.H)] = (
        mm(ctx[:, pl.ds(k1, half)], w1[...]) + mm(ctx[:, pl.ds(k2, half)], w2[...])
    ).astype(BF)


def out_forward(d, layer, sc, w, pieces, chunks):
    wspec = pl.BlockSpec((None, d.W, d.H), lambda i: (layer, 0, 0))
    outs = [sds((d.T, d.W), BF), sds((d.T, d.D), BF)]
    return pl.pallas_call(
        functools.partial(out_body, d),
        grid=(1,),
        in_specs=[SSPEC, wspec] + [whole(a.shape) for a in (*pieces, *chunks)],
        out_specs=[whole(o.shape) for o in outs],
        out_shape=outs,
        compiler_params=pltpu.CompilerParams(vmem_limit_bytes=VLIM),
        cost_estimate=cost(2 * d.T * d.D * d.W, 3e6),
        name="out_forward",
    )(sc, w, *pieces, *chunks)


def ffn_body(d, tiles, sc, hid, pa, pb, bias, gain, shift, u, u1, u2, ub, w, w1, w2,
             mid, n2, ns, act, dg, part, acc):
    f = pl.program_id(0)
    own, oth, p1, p2 = offs(sc, d)

    @pl.when(f == 0)
    def _():
        m = hid[...] + ((pa[...].astype(F32) + pb[...].astype(F32)) + bias[...])
        mid[...] = m
        xhat, _ = norm_rows(m)
        n2[...] = (xhat * gain[...] + shift[...]).astype(BF)
        ns[...] = n2[:, pl.ds(oth, d.H)]
        acc[...] = jnp.zeros_like(acc)

    pre = (
        mm(n2[:, pl.ds(own, d.H)], u[...])
        + mm(n2[:, pl.ds(p1, d.Q)], u1[...])
        + mm(n2[:, pl.ds(p2, d.Q)], u2[...])
        + ub[...]
    )
    sq = pre * pre
    th = jnp.tanh(GELU_A * pre * (1.0 + GELU_B * sq))
    half = 0.5 * (1.0 + th)
    a = (pre * half).astype(BF)
    act[...] = a
    dg[...] = (
        half + 0.5 * pre * (1.0 - th * th) * (GELU_A * (1.0 + 3.0 * GELU_B * sq))
    ).astype(BF)
    acc[:, pl.ds(own, d.H)] += mm(a, w[...])
    mine = lax.div(f, tiles // 2) == sc[1]

    @pl.when(mine)
    def _():
        acc[:, pl.ds(oth, d.H)] += mm(a, w1[...])

    @pl.when(jnp.logical_not(mine))
    def _():
        acc[:, pl.ds(oth, d.H)] += mm(a, w2[...])

    @pl.when(f == tiles - 1)
    def _():
        part[...] = acc[...].astype(BF)


FT = 512


def ffn_specs(d, layer, tiles):
    u = pl.BlockSpec((None, d.H, FT), lambda f: (layer, 0, f))
    up = pl.BlockSpec((d.Q, FT), lambda f: (0, f))
    w = pl.BlockSpec((None, FT, d.H), lambda f: (layer, f, 0))
    wp = pl.BlockSpec((FT, d.H), lambda f: (lax.rem(f, tiles // 2), 0))
    return u, up, w, wp


def ffn_forward(d, layer, sc, hid, pa, pb, bias, gain, shift, up_w, up_p, ub, dn_w, dn_p):
    tiles = d.F // FT
    u, up, w, wp = ffn_specs(d, layer, tiles)
    col = pl.BlockSpec((d.T, FT), lambda f: (0, f))
    row = whole((1, d.D))
    full = whole((d.T, d.D))
    return pl.pallas_call(
        functools.partial(ffn_body, d, tiles),
        grid=(tiles,),
        in_specs=[SSPEC, full, full, full, row, row, row, u, up, up,
                  pl.BlockSpec((1, FT), lambda f: (0, f)), w, wp, wp],
        out_specs=[full, full, whole((d.T, d.H)), col, col, full],
        out_shape=[sds((d.T, d.D), F32), sds((d.T, d.D), BF), sds((d.T, d.H), BF),
                   sds((d.T, d.F), BF), sds((d.T, d.F), BF), sds((d.T, d.D), BF)],
        scratch_shapes=[pltpu.VMEM((d.T, d.D), F32)],
        compiler_params=pltpu.CompilerParams(vmem_limit_bytes=VLIM),
        cost_estimate=cost(4 * d.T * d.D * d.F, 14e6),
        name="ffn_forward",
    )(sc, hid, pa, pb, bias, gain, shift, up_w, *up_p, ub, dn_w, *dn_p)


def ffn_back_body(d, tiles, sc, grad, dg, u, u1, u2, w, w1, w2,
                  db, dbs, dpre, usum, bsum, part, acc, dact):
    f = pl.program_id(0)
    own, oth, p1, p2 = offs(sc, d)

    @pl.when(f == 0)
    def _():
        db[...] = grad[...].astype(BF)
        dbs[...] = db[:, pl.ds(oth, d.H)]
        bsum[...] = jnp.sum(db[...].astype(F32), axis=0, keepdims=True)
        acc[...] = jnp.zeros_like(acc)

    mine = lax.div(f, tiles // 2) == sc[1]

    @pl.when(mine)
    def _():
        dact[...] = mm(db[:, pl.ds(oth, d.H)], w1[...], NT)

    @pl.when(jnp.logical_not(mine))
    def _():
        dact[...] = mm(db[:, pl.ds(oth, d.H)], w2[...], NT)

    da = dact[...] + mm(db[:, pl.ds(own, d.H)], w[...], NT)
    dp = (da * dg[...].astype(F32)).astype(BF)
    dpre[...] = dp
    usum[...] = jnp.sum(dp.astype(F32), axis=0, keepdims=True)
    acc[:, pl.ds(own, d.H)] += mm(dp, u[...], NT)
    acc[:, pl.ds(p1, d.Q)] += mm(dp, u1[...], NT)
    acc[:, pl.ds(p2, d.Q)] += mm(dp, u2[...], NT)

    @pl.when(f == tiles - 1)
    def _():
        part[...] = acc[...].astype(BF)


def ffn_backward(d, layer, sc, grad, dg, up_w, up_p, dn_w, dn_p):
    tiles = d.F // FT
    u, up, w, wp = ffn_specs(d, layer, tiles)
    col = pl.BlockSpec((d.T, FT), lambda f: (0, f))
    full = whole((d.T, d.D))
    return pl.pallas_call(
        functools.partial(ffn_back_body, d, tiles),
        grid=(tiles,),
        in_specs=[SSPEC, full, col, u, up, up, w, wp, wp],
        out_specs=[full, whole((d.T, d.H)), col, pl.BlockSpec((1, FT), lambda f: (0, f)),
                   whole((1, d.D)), full],
        out_shape=[sds((d.T, d.D), BF), sds((d.T, d.H), BF), sds((d.T, d.F), BF),
                   sds((1, d.F), F32), sds((1, d.D), F32), sds((d.T, d.D), BF)],
        scratch_shapes=[pltpu.VMEM((d.T, d.D), F32), pltpu.VMEM((d.T, FT), F32)],
        compiler_params=pltpu.CompilerParams(vmem_limit_bytes=VLIM),
        cost_estimate=cost(4 * d.T * d.D * d.F, 14e6),
        name="ffn_backward",
    )(sc, grad, dg, up_w, *up_p, dn_w, *dn_p)


def context_back_body(d, *refs):
    sc, grad, pa, pb, mid, gain, w, w1, w2 = refs[:9]
    dmid, da, das, gsum, ssum, asum = refs[9:15]
    chunks = refs[15 : 15 + d.C]
    dctx = refs[15 + d.C]
    own, oth, _, _ = offs(sc, d)
    back, g, s = norm_back(pa[...].astype(F32) + pb[...].astype(F32), mid[...], gain[...])
    gsum[...] = g
    ssum[...] = s
    total = grad[...].astype(F32) + back
    dmid[...] = total
    da[...] = total.astype(BF)
    das[...] = da[:, pl.ds(oth, d.H)]
    asum[...] = jnp.sum(da[...].astype(F32), axis=0, keepdims=True)
    half = d.W // 2
    k1 = pl.multiple_of(sc[1] * half, half)
    k2 = pl.multiple_of((1 - sc[1]) * half, half)
    dctx[...] = mm(da[:, pl.ds(own, d.H)], w[...], NT)
    dctx[:, pl.ds(k1, half)] += mm(da[:, pl.ds(oth, d.H)], w1[...], NT)
    dctx[:, pl.ds(k2, half)] += mm(da[:, pl.ds(oth, d.H)], w2[...], NT)
    c = sc[2]
    for o in range(d.C):
        to = lax.rem(c + o, d.C)
        col = pl.multiple_of(lax.div(to, d.g) * HEAD_DIM, HEAD_DIM)
        row = pl.multiple_of(lax.rem(to, d.g) * d.rq, d.rq)
        chunks[o][...] = dctx[pl.ds(row, d.rq), pl.ds(col, HEAD_DIM)].astype(BF)


def context_backward(d, layer, sc, grad, pa, pb, mid, gain, w, pieces):
    wspec = pl.BlockSpec((None, d.W, d.H), lambda i: (layer, 0, 0))
    outs = [sds((d.T, d.D), F32), sds((d.T, d.D), BF), sds((d.T, d.H), BF)]
    outs += [sds((1, d.D), F32)] * 3 + [sds((d.rq, HEAD_DIM), BF)] * d.C
    return pl.pallas_call(
        functools.partial(context_back_body, d),
        grid=(1,),
        in_specs=[SSPEC] + [whole(a.shape) for a in (grad, pa, pb, mid, gain)]
        + [wspec] + [whole(a.shape) for a in pieces],
        out_specs=[whole(o.shape) for o in outs],
        out_shape=outs,
        scratch_shapes=[pltpu.VMEM((d.T, d.W), F32)],
        compiler_params=pltpu.CompilerParams(vmem_limit_bytes=VLIM),
        cost_estimate=cost(2 * d.T * d.D * d.W, 6e6),
        name="context_backward",
    )(sc, grad, pa, pb, mid, gain, w, *pieces)


def attend_back_body(d, *refs):
    sc, kb = refs[:2]
    chunks = refs[2 : 2 + d.C]
    dchunks = refs[2 + d.C : 2 + 2 * d.C]
    outs = refs[2 + 2 * d.C : 2 + 3 * d.C]
    qs, ks, vs, cs, dqs, dks, dvs = refs[2 + 3 * d.C :]
    load_chunks(d, sc, chunks, qs, ks, vs)
    c = sc[2]
    for o in range(d.C):
        cs[lax.rem(c - o + d.C, d.C)] = dchunks[o][...]
    dks[...] = jnp.zeros_like(dks)
    dvs[...] = jnp.zeros_like(dvs)
    def one(s, seen):
        ext = seen * d.T
        k = ks[0:seen].reshape(ext, HEAD_DIM)
        v = vs[0:seen].reshape(ext, HEAD_DIM)
        q = qs[s]
        dc = cs[s]
        scores = score_block(d, sc, kb, q, k, s, ext)
        e = jnp.exp(scores - jnp.max(scores, axis=-1, keepdims=True))
        p = e / jnp.sum(e, axis=-1, keepdims=True)
        dp = mm(dc, v, NT)
        ds = (p * (dp - jnp.sum(p * dp, axis=-1, keepdims=True))).astype(BF)
        dqs[s] = (mm(ds, k) * SCALE).astype(BF)
        dks[0:seen] += mm(ds, q, TN).reshape(seen, d.T, HEAD_DIM)
        dvs[0:seen] += mm(p.astype(BF), dc, TN).reshape(seen, d.T, HEAD_DIM)

    each_source(d, one)
    for o in range(d.C):
        to = lax.rem(c + o, d.C)
        outs[o][0 : d.rq, :] = dqs[to]
        outs[o][d.rq : d.rq + d.T, :] = (dks[to] * SCALE).astype(BF)
        outs[o][d.rq + d.T :, :] = dvs[to].astype(BF)


def attend_backward(d, sc, kb, chunks, dchunks):
    return pl.pallas_call(
        functools.partial(attend_back_body, d),
        in_specs=[SSPEC] + [VSPEC] * (1 + 2 * d.C),
        out_specs=[VSPEC] * d.C,
        out_shape=[sds((d.chunk, HEAD_DIM), BF)] * d.C,
        scratch_shapes=[
            pltpu.VMEM((d.C, d.rq, HEAD_DIM), BF),
            pltpu.VMEM((d.C, d.T, HEAD_DIM), BF),
            pltpu.VMEM((d.C, d.T, HEAD_DIM), BF),
            pltpu.VMEM((d.C, d.rq, HEAD_DIM), BF),
            pltpu.VMEM((d.C, d.rq, HEAD_DIM), BF),
            pltpu.VMEM((d.C, d.T, HEAD_DIM), F32),
            pltpu.VMEM((d.C, d.T, HEAD_DIM), F32),
        ],
        compiler_params=pltpu.CompilerParams(vmem_limit_bytes=VLIM),
        cost_estimate=cost(5 * d.C * d.rq * d.C * d.T * HEAD_DIM * 2, 4e6),
        name="attend_backward",
    )(sc, kb, *chunks, *dchunks)


def qkv_back_body(d, *refs):
    sc, w, w1, w2 = refs[:4]
    chunks = refs[4 : 4 + d.C]
    dproj, qvsum, part, dk, dv = refs[4 + d.C :]
    c = sc[2]
    dk[...] = jnp.zeros_like(dk)
    dv[...] = jnp.zeros_like(dv)
    for o in range(d.C):
        src = lax.rem(c - o + d.C, d.C)
        col = pl.multiple_of(lax.div(src, d.g) * HEAD_DIM, HEAD_DIM)
        row = pl.multiple_of(lax.rem(src, d.g) * d.rq, d.rq)
        dproj[0, pl.ds(row, d.rq), pl.ds(col, HEAD_DIM)] = chunks[o][0 : d.rq, :]
        dk[:, pl.ds(col, HEAD_DIM)] += chunks[o][d.rq : d.rq + d.T, :].astype(F32)
        dv[:, pl.ds(col, HEAD_DIM)] += chunks[o][d.rq + d.T :, :].astype(F32)
    dproj[1] = dk[...].astype(BF)
    dproj[2] = dv[...].astype(BF)
    qvsum[0:1, :] = jnp.sum(dproj[0].astype(F32), axis=0, keepdims=True)
    qvsum[1:2, :] = jnp.sum(dproj[2].astype(F32), axis=0, keepdims=True)
    own, _, p1, p2 = offs(sc, d)
    for ref, at, width in ((w, own, d.H), (w1, p1, d.Q), (w2, p2, d.Q)):
        total = mm(dproj[0], ref[0], NT)
        total = total + mm(dproj[1], ref[1], NT)
        total = total + mm(dproj[2], ref[2], NT)
        part[:, pl.ds(at, width)] = total.astype(BF)


def qkv_backward(d, layer, sc, w, pieces, chunks):
    wspec = pl.BlockSpec((None, 3, d.H, d.W), lambda i: (layer, 0, 0, 0))
    outs = [sds((3, d.T, d.W), BF), sds((2, d.W), F32), sds((d.T, d.D), BF)]
    return pl.pallas_call(
        functools.partial(qkv_back_body, d),
        grid=(1,),
        in_specs=[SSPEC, wspec] + [whole(a.shape) for a in (*pieces, *chunks)],
        out_specs=[whole(o.shape) for o in outs],
        out_shape=outs,
        scratch_shapes=[pltpu.VMEM((d.T, d.W), F32)] * 2,
        compiler_params=pltpu.CompilerParams(vmem_limit_bytes=VLIM),
        cost_estimate=cost(2 * d.T * d.D * 3 * d.W, 7e6),
        name="qkv_backward",
    )(sc, w, *pieces, *chunks)


def input_back_body(dmid, pa, pb, hid, gain, grad, gsum, ssum):
    back, g, s = norm_back(pa[...].astype(F32) + pb[...].astype(F32), hid[...], gain[...])
    grad[...] = dmid[...] + back
    gsum[...] = g
    ssum[...] = s


def input_backward(d, dmid, pa, pb, hid, gain):
    return pl.pallas_call(
        input_back_body,
        in_specs=[VSPEC] * 5,
        out_specs=[VSPEC] * 3,
        out_shape=[sds((d.T, d.D), F32)] + [sds((1, d.D), F32)] * 2,
        compiler_params=pltpu.CompilerParams(vmem_limit_bytes=VLIM),
        cost_estimate=cost(3e6, 5e6),
        name="input_backward",
    )(dmid, pa, pb, hid, gain)


def reverse_bits(value, bits):
    out = 0
    for k in range(bits):
        bit = lax.rem(lax.div(value, 1 << k), 2)
        out = out + bit * (1 << (bits - 1 - k))
    return out


def wgrad_body(d, kind, nm, rows, cols, sc, a, a2, b, b2, keep, send):
    x = sc[0]
    c = sc[2]
    own = pl.multiple_of(x * d.H, d.H)
    rb = rows // d.C
    tile = min(512, rows)
    for m in range(nm):
        for r0 in range(0, rows, tile):
            for c0 in range(0, cols, 512):
                if kind in ("up", "qkv"):
                    left = a[:, pl.ds(own, d.H)]
                    left2 = a2[...]
                    if kind == "up":
                        right, right2 = b[:, c0 : c0 + 512], b2[:, c0 : c0 + 512]
                    else:
                        right, right2 = b[m], b2[m]
                else:
                    left, left2 = a[:, r0 : r0 + tile], a2[:, r0 : r0 + tile]
                    right, right2 = b[:, pl.ds(own, d.H)], b2[...]
                total = (mm(left, right, TN) + mm(left2, right2, TN)).astype(BF)
                for k in range(tile // rb):
                    block = r0 // rb + k
                    spot = reverse_bits(lax.bitwise_xor(c, block), d.bits)
                    piece = total[k * rb : (k + 1) * rb, :]

                    @pl.when(spot < d.C // 2)
                    def _():
                        keep[spot, m, :, c0 : c0 + 512] = piece

                    @pl.when(spot >= d.C // 2)
                    def _():
                        send[spot - d.C // 2, m, :, c0 : c0 + 512] = piece


def weight_grad(d, kind, sc, a, a2, b, b2):
    nm = 3 if kind == "qkv" else 1
    rows = a.shape[1] if kind in ("down", "out") else d.H
    cols = d.H if kind in ("down", "out") else b.shape[-1]
    shape = (d.C // 2, nm, rows // d.C, cols)
    return pl.pallas_call(
        functools.partial(wgrad_body, d, kind, nm, rows, cols),
        in_specs=[SSPEC] + [VSPEC] * 4,
        out_specs=[VSPEC] * 2,
        out_shape=[sds(shape, BF)] * 2,
        compiler_params=pltpu.CompilerParams(vmem_limit_bytes=VLIM),
        cost_estimate=cost(4 * d.T * nm * rows * cols, 8e6),
        name="weight_grad_" + kind,
    )(sc, a, a2, b, b2)


def place_body(levels, table, *refs):
    outs = refs[-1]
    ins = refs[: levels + 1]
    r = table[pl.program_id(0)]
    for k in range(levels + 1):
        low = 0 if k == 0 else 1 << (k - 1)
        high = 1 << k

        @pl.when(jnp.logical_and(r >= low, r < high))
        def _():
            outs[...] = ins[k][0].astype(F32)


def place(d, layer, table, parts, before, name):
    _, nm, rb, cols = parts[0].shape
    rows = rb * d.C

    def spec(k):
        low = 0 if k == 0 else 1 << (k - 1)
        count = 1 if k == 0 else 1 << (k - 1)
        return pl.BlockSpec(
            (1, nm, rb, cols), lambda b, t: (jnp.clip(t[b] - low, 0, count - 1), 0, 0, 0)
        )

    in_specs = [spec(k) for k in range(d.bits + 1)]
    extra = ()
    alias = {}
    if before is not None:
        in_specs.append(pl.BlockSpec(memory_space=pl.ANY))
        extra = (before,)
        alias = {d.bits + 2: 0}
    return pl.pallas_call(
        functools.partial(place_body, d.bits),
        grid_spec=pltpu.PrefetchScalarGridSpec(
            num_scalar_prefetch=1,
            grid=(d.C,),
            in_specs=in_specs,
            out_specs=pl.BlockSpec((None, nm, rb, cols), lambda b, t: (layer, 0, b, 0)),
        ),
        out_shape=sds((LAYERS, nm, rows, cols), F32),
        input_output_aliases=alias,
        compiler_params=pltpu.CompilerParams(vmem_limit_bytes=VLIM),
        cost_estimate=cost(1e6, 12e6),
        name="place_" + name,
    )(table, *parts, *extra)


def swap(values, axis):
    return lax.ppermute(values, axis, [(0, 1), (1, 0)])


def cross(values, bit, size):
    return lax.ppermute(values, "ctx", [(i, i ^ (1 << bit)) for i in range(size)])


def total_over_ctx(d, keep, send):
    for bit in range(d.bits):
        got = cross(send, bit, d.C)
        half = keep.shape[0] // 2
        if half == 0:
            keep = (keep.astype(F32) + got.astype(F32)).astype(BF)
            break
        send = (keep[half:].astype(F32) + got[half:].astype(F32)).astype(BF)
        keep = (keep[:half].astype(F32) + got[:half].astype(F32)).astype(BF)
    parts = [keep]
    for bit in reversed(range(d.bits)):
        full = parts[0] if len(parts) == 1 else jnp.concatenate(parts, axis=0)
        parts.append(cross(full, bit, d.C))
    return parts


def shift_chunks(d, chunks):
    out = [chunks[0]]
    for o in range(1, d.C):
        out.append(lax.ppermute(chunks[o], "ctx", [(i, (i + o) % d.C) for i in range(d.C)]))
    return out


def key_table(d, parent_ids, depth_offsets):
    segs = parent_ids.shape[0] // lax.axis_size("fsdp")
    start = lax.axis_index("fsdp") * segs
    parents = lax.dynamic_slice_in_dim(parent_ids, start, segs) - start
    depths = lax.dynamic_slice_in_dim(depth_offsets, start, segs).astype(F32)
    ids = jnp.arange(segs, dtype=jnp.int32)
    reach = jnp.maximum(
        (parents[:, None] == ids[None, :]).astype(F32), (ids[:, None] == ids[None, :]).astype(F32)
    )
    for _ in range((segs - 1).bit_length()):
        reach = jnp.minimum(jnp.dot(reach, reach), 1.0)
    head = lax.axis_index("tp") * d.lh + lax.axis_index("ctx") // d.g
    slope = jnp.exp2(-(head + 1).astype(F32))
    level = jnp.where(reach > 0.5, slope * (depths[None, :] - depths[:, None]), MASKED)
    spots = slope * jnp.arange(SEG, dtype=jnp.int32).astype(F32)
    return (level[:, :, None] + spots[None, None, :]).reshape(segs, segs * SEG)


def gather_pieces(d, shard, axis, y):
    half = shard.shape[axis] // 2
    mine = lax.dynamic_slice_in_dim(shard, y * half, half, axis)
    first = swap(mine, "fsdp")
    return (first, cross(first, 0, d.C))


def on_device(tokens, qkv_weight, out_weight, up_weight, down_weight, qv_bias, up_bias,
              norm_gains, row_biases, parent_ids, depth_offsets, cotangent):
    d = Dims(tokens, qkv_weight, up_weight)
    x = lax.axis_index("fsdp")
    c = lax.axis_index("ctx")
    t = lax.axis_index("tp")
    y = c % 2
    sc = jnp.stack([x, y, c]).astype(jnp.int32)
    table = jnp.stack([reverse_bits(lax.bitwise_xor(c, b), d.bits) for b in range(d.C)])
    table = table.astype(jnp.int32)
    w_qkv = qkv_weight.transpose(0, 2, 1, 3)
    pieces = []
    for layer in range(LAYERS):
        pieces.append((
            gather_pieces(d, w_qkv[layer], 1, y),
            gather_pieces(d, out_weight[layer], 0, y),
            gather_pieces(d, up_weight[layer], 0, y),
            gather_pieces(d, down_weight[layer], 0, y),
        ))
    kb = key_table(d, parent_ids, depth_offsets)

    def both(rows):
        got = swap(rows, "tp")
        return jnp.where(
            t == 0,
            jnp.concatenate([rows, got], axis=0),
            jnp.concatenate([got, rows], axis=0),
        )

    def row(values):
        return values.reshape(1, -1)

    state = both(tokens)
    saved = []
    for layer in range(LAYERS):
        p_qkv, p_out, p_up, p_down = pieces[layer]
        res = qkv_forward(d, layer, sc, state, row(norm_gains[layer, 0]),
                          row(row_biases[layer, 0]), w_qkv, p_qkv, qv_bias[layer])
        hidden, normed, normed_s = res[:3]
        chunks = shift_chunks(d, res[3:])
        outs = shift_chunks(d, attend_forward(d, sc, kb, chunks))
        ctx, part = out_forward(d, layer, sc, out_weight, p_out, outs)
        middle, n2, n2_s, act, dg, part2 = ffn_forward(
            d, layer, sc, hidden, part, swap(part, "tp"), row(row_biases[layer, 1]),
            row(norm_gains[layer, 1]), row(row_biases[layer, 2]), up_weight, p_up,
            row(up_bias[layer]), down_weight, p_down)
        state = (middle, part2, swap(part2, "tp"), row(row_biases[layer, 3]))
        saved.append((hidden, normed, normed_s, chunks, ctx, middle, n2, n2_s, act, dg))
    own_rows = tokens.shape[0]

    def mine(values):
        return lax.dynamic_slice_in_dim(values, t * own_rows, own_rows, 0)

    output = mine(state[0]) + (
        (mine(state[1]).astype(F32) + mine(state[2]).astype(F32)) + state[3]
    )
    output = output.astype(BF)
    grad = both(cotangent)
    sums = [None] * LAYERS
    grads = [None] * 4
    for layer in reversed(range(LAYERS)):
        p_qkv, p_out, p_up, p_down = pieces[layer]
        hidden, normed, normed_s, chunks, ctx, middle, n2, n2_s, act, dg = saved[layer]
        db, db_s, dpre, usum, bsum, part = ffn_backward(
            d, layer, sc, grad, dg, up_weight, p_up, down_weight, p_down)
        other = swap(part, "tp")
        res = context_backward(d, layer, sc, grad, part, other, middle,
                               row(norm_gains[layer, 1]), out_weight, p_out)
        dmid, da, da_s, gsum2, ssum2, asum = res[:6]
        dchunks = shift_chunks(d, res[6:])
        dparts = shift_chunks(d, attend_backward(d, sc, kb, chunks, dchunks))
        dproj, qvsum, part = qkv_backward(d, layer, sc, w_qkv, p_qkv, dparts)
        other = swap(part, "tp")
        grad, gsum1, ssum1 = input_backward(d, dmid, part, other, hidden,
                                            row(norm_gains[layer, 0]))
        jobs = (
            ("qkv", normed, normed_s, dproj, dproj, 0),
            ("out", ctx, ctx, da, da_s, 1),
            ("up", n2, n2_s, dpre, dpre, 2),
            ("down", act, act, db, db_s, 3),
        )
        for kind, a, a_s, b, b_s, slot in reversed(jobs):
            keep, send = weight_grad(d, kind, sc, a, swap(a_s, "fsdp"), b, swap(b_s, "fsdp"))
            parts = total_over_ctx(d, keep, send)
            grads[slot] = place(d, layer, table, parts, grads[slot], kind)
        sums[layer] = (qvsum, usum, gsum1, gsum2, ssum1, asum, ssum2, bsum)
    flat = jnp.concatenate([v.reshape(-1) for layer in sums for v in layer]).reshape(-1, 128)
    flat = flat + swap(flat, "fsdp")
    for bit in range(d.bits):
        flat = flat + cross(flat, bit, d.C)
    flat = flat.reshape(LAYERS, -1)
    n_qv, n_up = 2 * d.W, d.F
    qv_grad = flat[:, :n_qv].reshape(LAYERS, 2, d.W)
    up_grad = flat[:, n_qv : n_qv + n_up]
    rest = flat[:, n_qv + n_up :].reshape(LAYERS, 6, d.D)
    g_qkv, g_out, g_up, g_down = grads
    return (
        output,
        mine(grad),
        g_qkv.transpose(0, 2, 1, 3),
        g_out.reshape(LAYERS, d.W, d.H),
        g_up.reshape(LAYERS, d.H, d.F),
        g_down.reshape(LAYERS, d.F, d.H),
        qv_grad,
        up_grad,
        rest[:, :2],
        rest[:, 2:],
    )


def solution(mesh):
    in_specs = (
        P(("fsdp", "ctx", "tp"), None),
        P(None, "fsdp", None, "tp"),
        P(None, "tp", "fsdp"),
        P(None, "fsdp", "tp"),
        P(None, "tp", "fsdp"),
        P(None, None, "tp"),
        P(None, "tp"),
        P(),
        P(),
        P(),
        P(),
        P(("fsdp", "ctx", "tp"), None),
    )
    out_specs = (
        P(("fsdp", "ctx", "tp"), None),
        P(("fsdp", "ctx", "tp"), None),
        P(None, "fsdp", None, "tp"),
        P(None, "tp", "fsdp"),
        P(None, "fsdp", "tp"),
        P(None, "tp", "fsdp"),
        P(None, None, "tp"),
        P(None, "tp"),
        P(),
        P(),
    )
    return jax.shard_map(
        on_device, mesh=mesh, in_specs=in_specs, out_specs=out_specs, check_vma=False
    )
```

time: 1760 us -> 956 us (0.54)
  waiting for transfers between devices: 1320 us -> 482 us
  starting transfers between devices: 1.53 us -> 207 us
  Pallas kernels: 0 us -> 199 us
  blocking collectives: 140 us -> 0 us
  matrix products: 131 us -> 0.54 us
  other arithmetic: 73.2 us -> 16.3 us
  local copies, waits for them, and re-layouts: 60.2 us -> 39.4 us
    reduce_scatter x18 -> x0, waiting for transfers between devices: 538 us -> none  [the longest x2 139 us: on_device(): lax.psum_scatter(key_terms.astype(jnp.bfloat16), 'ctx', scatter_dimension...]
    all_gather x12 -> x0, waiting for transfers between devices: 487 us -> none  [the longest x2 108 us: layer_weights(): lax.all_gather(down_weight[layer_index], 'fsdp', axis=1, tiled=True)]
    ppermute x0 -> x150, waiting for transfers between devices: none -> 482 us  [the longest x59 272 us: cross(): return lax.ppermute(values, 'ctx', [(i, i ^ 1 << bit) for i in range(size)])]
    psum x1 -> x0, waiting for transfers between devices: 297 us -> none  [reduce_weights(): lax.psum(shards[0].astype(jnp.bfloat16), 'ctx').astype(jnp.float32)]
    ppermute x0 -> x150, starting transfers between devices: none -> 207 us  [the longest x56 112 us: shift_chunks(): lax.ppermute(chunks[o], 'ctx', [(i, (i + o) % d.C) for i in range(d.C)])]
    pallas_call x0 -> x34, Pallas kernels: none -> 199 us  [the longest x8 53.5 us: place(): pl.pallas_call(functools.partial(place_body, d.bits), grid_spec=pltpu.Pre...]
    dot_general x36 -> x2, matrix products: 131 us -> 0.54 us  [key_table(): reach = jnp.minimum(jnp.dot(reach, reach), 1.0)]
    psum x2 -> x0, blocking collectives: 121 us -> none  [the longest x1 79.1 us: on_device(): lax.psum((jnp.stack(qv_parts), jnp.stack(up_parts)), ('fsdp', 'ctx'))]
  transfers between devices with their start and end apart: 31 -> 150, of which waited for: 29 -> 63; matrix products, arithmetic and copies ran while one was open for 7% -> 4% of each run, Pallas kernels for 0% -> 17%
where the time goes in v1:
time: 956 us; the launch traced here: 947 us
  waiting for transfers between devices  482 us (50%)
  starting transfers between devices  207 us (22%)
  Pallas kernels  199 us (21%)
  local copies, waits for them, and re-layouts  39.4 us (4%)
  other arithmetic  16.3 us (2%)
    ppermute x59, waiting for transfers between devices, cross(): return lax.ppermute(values, 'ctx', [(i, i ^ 1 << bit) for i in range(size)])  272 us
    ppermute x56, waiting for transfers between devices, shift_chunks(): lax.ppermute(chunks[o], 'ctx', [(i, (i + o) % d.C) for i in range(d.C)])  118 us
    ppermute x56, starting transfers between devices, shift_chunks(): lax.ppermute(chunks[o], 'ctx', [(i, (i + o) % d.C) for i in range(d.C)])  112 us
    ppermute x35, waiting for transfers between devices, swap(): return lax.ppermute(values, axis, [(0, 1), (1, 0)])  91.8 us
    ppermute x59, starting transfers between devices, cross(): return lax.ppermute(values, 'ctx', [(i, i ^ 1 << bit) for i in range(size)])  56.9 us
    pallas_call x8, Pallas kernels, place(): pl.pallas_call(functools.partial(place_body, d.bits), grid_spec=pltpu.Pre...  53.5 us
    ppermute x35, starting transfers between devices, swap(): return lax.ppermute(values, axis, [(0, 1), (1, 0)])  37.8 us
    pallas_call x8, Pallas kernels, weight_grad(): pl.pallas_call(functools.partial(wgrad_body, d, kind, nm, rows, cols), in...  36.3 us
  transfers between devices with their start and end apart: 150, of which 63 were waited for; matrix products, arithmetic and copies ran while one was open for 4% of the time, Pallas kernels for 17%

profile of v1, /device:TPU:0, one launch (start us, length us, event | category | flops | bytes accessed | tf_op | source)
XLA Modules:
  0.0 947.1 jit_solution(12014186118096431774)
XLA Ops:
  32.4 12.5 %collective-permute-done.2.refs_6_.refs_3_ = bf16[3,256,512]{2,1,0:T(8,128)(2,1)} collective-permute-done((bf16[3,256,512]{2,1,0:T(8,128)(2,1)}, bf16[3,256,512]{2,1,0:T(8,128)(2,1)}, u32[]{:S(2)}, u32[]{:S(2)}) %collective-permute-start.2) | collective-permute-done | bytes 786464 | tf_op jit(solution)/shard_map/ppermute | solution.py:659
  56.8 19.6 %collective-permute-done.22.w1 = bf16[1024,512]{1,0:T(8,128)(2,1)} collective-permute-done((bf16[1024,512]{1,0:T(8,128)(2,1)}, bf16[1024,512]{1,0:T(8,128)(2,1)}, u32[]{:S(2)}, u32[]{:S(2)}) %collective-permute-start.22) | collective-permute-done | bytes 1048608 | tf_op jit(solution)/shard_map/ppermute | solution.py:655
  106.5 32.0 %collective-permute-done.12.refs_5_ = bf16[128,128]{1,0:T(8,128)(2,1)S(1)} collective-permute-done((bf16[128,128]{1,0:T(8,128)(2,1)}, bf16[128,128]{1,0:T(8,128)(2,1)S(1)}, u32[]{:S(2)}, u32[]{:S(2)}) %collective-permute-start.12) | collective-permute-done | bytes 32800 | tf_op jit(solution)/shard_map/ppermute | solution.py:681
  166.8 10.7 %ffn_forward.2 = (f32[256,1024]{1,0:T(8,128)}, bf16[256,1024]{1,0:T(8,128)(2,1)}, bf16[256,512]{1,0:T(8,128)(2,1)}, bf16[256,2048]{1,0:T(8,128)(2,1)}, bf16[256,...) custom-call(s32[3]{0:T(128)} %pad_add_fusion.refs_0_.sc, f32[256,1024]{1,0:T(8,128)} %get-tuple-element.148.hid, ...), custom_call_target="tpu_custom_call" | custom-call | flops 2147483648 | bytes 14000000 | tf_op jit(solution)/shard_map/ffn_forward/pallas_call | solution.py:316
  191.0 14.4 %collective-permute-done.27.refs_2_.refs_7_ = bf16[256,512]{1,0:T(8,128)(2,1)S(1)} collective-permute-done((bf16[256,512]{1,0:T(8,128)(2,1)S(1)}, bf16[256,512]{1,0:T(8,128)(2,1)S(1)}, u32[]{:S(2)}, u32[]{:S(2)}) %collective-permute-start.27) | collective-permute-done | bytes 262176 | tf_op jit(solution)/shard_map/ppermute | solution.py:655
  217.6 7.8 collective-permute-start.34
  230.0 33.6 %collective-permute-done.35.refs_9_ = bf16[640,128]{1,0:T(8,128)(2,1)S(1)} collective-permute-done((bf16[640,128]{1,0:T(8,128)(2,1)}, bf16[640,128]{1,0:T(8,128)(2,1)S(1)}, u32[]{:S(2)}, u32[]{:S(2)}) %collective-permute-start.35) | collective-permute-done | bytes 163872 | tf_op jit(solution)/shard_map/ppermute | solution.py:681
  294.0 10.7 %ffn_forward.3 = (f32[256,1024]{1,0:T(8,128)}, bf16[256,1024]{1,0:T(8,128)(2,1)}, bf16[256,512]{1,0:T(8,128)(2,1)}, bf16[256,2048]{1,0:T(8,128)(2,1)}, bf16[256,...) custom-call(s32[3]{0:T(128)} %pad_add_fusion.refs_0_.sc, f32[256,1024]{1,0:T(8,128)} %get-tuple-element.168.hid, ...), custom_call_target="tpu_custom_call" | custom-call | flops 2147483648 | bytes 14000000 | tf_op jit(solution)/shard_map/ffn_forward/pallas_call | solution.py:316
  304.6 9.2 ffn_backward.2
  336.3 9.2 attend_backward.2
  357.5 15.8 %collective-permute-start.62 = (bf16[640,128]{1,0:T(8,128)(2,1)}, bf16[640,128]{1,0:T(8,128)(2,1)S(1)}, u32[]{:S(2)}, u32[]{:S(2)}) collective-permute-start(bf16[640,128]{1,0:T(8,128)(2,1)} %get-tuple-element.204), channel_id=1, source_target_pairs={{0,10},{2,12},{4,14},{6,0},{8,2},{10,4},{12,6},{14,8},{1,11},{3,13... | collective-permute-start | bytes 491528 | tf_op jit(solution)/shard_map/ppermute | solution.py:681
  406.7 9.4 ffn_backward.3
  416.1 16.2 %collective-permute-done.90.a2 = bf16[256,512]{1,0:T(8,128)(2,1)S(1)} collective-permute-done((bf16[256,512]{1,0:T(8,128)(2,1)S(1)}, bf16[256,512]{1,0:T(8,128)(2,1)S(1)}, u32[]{:S(2)}, u32[]{:S(2)}) %collective-permute-start.90) | collective-permute-done | bytes 262176 | tf_op jit(solution)/shard_map/ppermute | solution.py:655
  446.5 19.5 %collective-permute-done.122.a2 = bf16[256,512]{1,0:T(8,128)(2,1)S(1)} collective-permute-done((bf16[256,512]{1,0:T(8,128)(2,1)S(1)}, bf16[256,512]{1,0:T(8,128)(2,1)S(1)}, u32[]{:S(2)}, u32[]{:S(2)}) %collective-permute-start.122) | collective-permute-done | bytes 262176 | tf_op jit(solution)/shard_map/ppermute | solution.py:655
  487.8 8.9 collective-permute-done.73.refs_17_
  497.4 9.1 attend_backward.3
  568.8 12.2 %collective-permute-done.100 = bf16[4,1,64,512]{3,2,1,0:T(8,128)(2,1)S(1)} collective-permute-done((bf16[4,1,64,512]{3,2,1,0:T(8,128)(2,1)S(1)}, bf16[4,1,64,512]{3,2,1,0:T(8,128)(2,1)S(1)}, u32[]{:S(2)}, u32[]{:S(2)}) %collective-permute-start.100) | collective-permute-done | bytes 262176 | tf_op jit(solution)/shard_map/ppermute | solution.py:659
  596.6 11.2 %collective-permute-done.132 = bf16[4,1,256,512]{3,2,1,0:T(8,128)(2,1)S(1)} collective-permute-done((bf16[4,1,256,512]{3,2,1,0:T(8,128)(2,1)S(1)}, bf16[4,1,256,512]{3,2,1,0:T(8,128)(2,1)S(1)}, u32[]{:S(2)}, u32[]{:S(2)}) %collective-permute-start.132) | collective-permute-done | bytes 1048608 | tf_op jit(solution)/shard_map/ppermute | solution.py:659
  619.8 12.7 %collective-permute-done.141 = bf16[2,1,256,512]{3,2,1,0:T(8,128)(2,1)S(1)} collective-permute-done((bf16[2,1,256,512]{3,2,1,0:T(8,128)(2,1)S(1)}, bf16[2,1,256,512]{3,2,1,0:T(8,128)(2,1)S(1)}, u32[]{:S(2)}, u32[]{:S(2)}) %collective-permute-start.141) | collective-permute-done | bytes 524320 | tf_op jit(solution)/shard_map/ppermute | solution.py:659
  644.6 9.0 collective-permute-done.148
  661.7 13.9 %collective-permute-done.94 = bf16[1,3,64,512]{3,2,1,0:T(8,128)(2,1)S(1)} collective-permute-done((bf16[1,3,64,512]{3,2,1,0:T(8,128)(2,1)S(1)}, bf16[1,3,64,512]{3,2,1,0:T(8,128)(2,1)S(1)}, u32[]{:S(2)}, u32[]{:S(2)}) %collective-permute-start.94) | collective-permute-done | bytes 196640 | tf_op jit(solution)/shard_map/ppermute | solution.py:659
  678.1 12.7 %collective-permute-done.95.refs_1_ = bf16[1,3,64,512]{3,2,1,0:T(8,128)(2,1)S(1)} collective-permute-done((bf16[1,3,64,512]{3,2,1,0:T(8,128)(2,1)S(1)}, bf16[1,3,64,512]{3,2,1,0:T(8,128)(2,1)S(1)}, u32[]{:S(2)}, u32[]{:S(2)}) %collective-permute-start.95) | collective-permute-done | bytes 196640 | tf_op jit(solution)/shard_map/ppermute | solution.py:659
  693.9 13.3 %collective-permute-done.127.refs_1_ = bf16[1,1,64,2048]{3,2,1,0:T(8,128)(2,1)S(1)} collective-permute-done((bf16[1,1,64,2048]{3,2,1,0:T(8,128)(2,1)S(1)}, bf16[1,1,64,2048]{3,2,1,0:T(8,128)(2,1)S(1)}, u32[]{:S(2)}, u32[]{:S(2)}) %collective-permute-start.127) | collective-permute-done | bytes 262176 | tf_op jit(solution)/shard_map/ppermute | solution.py:659
  719.8 17.5 %collective-permute-done.117 = bf16[2,1,64,2048]{3,2,1,0:T(8,128)(2,1)S(1)} collective-permute-done((bf16[2,1,64,2048]{3,2,1,0:T(8,128)(2,1)S(1)}, bf16[2,1,64,2048]{3,2,1,0:T(8,128)(2,1)S(1)}, u32[]{:S(2)}, u32[]{:S(2)}) %collective-permute-start.117) | collective-permute-done | bytes 524320 | tf_op jit(solution)/shard_map/ppermute | solution.py:659
  739.6 26.0 %collective-permute-done.85 = bf16[2,3,64,512]{3,2,1,0:T(8,128)(2,1)S(1)} collective-permute-done((bf16[2,3,64,512]{3,2,1,0:T(8,128)(2,1)S(1)}, bf16[2,3,64,512]{3,2,1,0:T(8,128)(2,1)S(1)}, u32[]{:S(2)}, u32[]{:S(2)}) %collective-permute-start.85) | collective-permute-done | bytes 393248 | tf_op jit(solution)/shard_map/ppermute | solution.py:659
  768.8 13.8 %collective-permute-done.135.refs_1_ = bf16[1,1,256,512]{3,2,1,0:T(8,128)(2,1)S(1)} collective-permute-done((bf16[1,1,256,512]{3,2,1,0:T(8,128)(2,1)S(1)}, bf16[1,1,256,512]{3,2,1,0:T(8,128)(2,1)S(1)}, u32[]{:S(2)}, u32[]{:S(2)}) %collective-permute-start.135) | collective-permute-done | bytes 262176 | tf_op jit(solution)/shard_map/ppermute | solution.py:659
  796.0 8.6 collective-permute-done.87.refs_1_
  815.7 7.5 collective-permute-done.149
  858.5 7.1 place_down.2.refs_4_
  865.6 7.3 collective-permute-done.129.refs_3_
  880.0 15.4 %collective-permute-done.137.refs_3_ = bf16[4,1,256,512]{3,2,1,0:T(8,128)(2,1)} collective-permute-done((bf16[4,1,256,512]{3,2,1,0:T(8,128)(2,1)}, bf16[4,1,256,512]{3,2,1,0:T(8,128)(2,1)}, u32[]{:S(2)}, u32[]{:S(2)}) %collective-permute-start.137) | collective-permute-done | bytes 1048608 | tf_op jit(solution)/shard_map/ppermute | solution.py:659
  902.4 29.5 %collective-permute-done.89.refs_3_ = bf16[4,3,64,512]{3,2,1,0:T(8,128)(2,1)} collective-permute-done((bf16[4,3,64,512]{3,2,1,0:T(8,128)(2,1)}, bf16[4,3,64,512]{3,2,1,0:T(8,128)(2,1)}, u32[]{:S(2)}, u32[]{:S(2)}) %collective-permute-start.89) | collective-permute-done | bytes 786464 | tf_op jit(solution)/shard_map/ppermute | solution.py:659
  (729 shorter events, 488.2 us)
Async XLA Ops:
  9.5 44.9 %collective-permute-start.3 = (bf16[256,512]{1,0:T(8,128)(2,1)}, bf16[256,512]{1,0:T(8,128)(2,1)S(1)}, u32[]{:S(2)}, u32[]{:S(2)}) collective-permute-start(bf16[256,512]{1,0:T(8,128)(2,1)} %dynamic-slice_bitcast_fusion.7), channel_id=1, source_target_pairs={{0,16},{16,0},{1,17},{17,1},{2,18},{18,2},{3,19},{19,3},{4,20},{20... | collective-permute-start | bytes 786440 | tf_op jit(solution)/shard_map/ppermute | solution.py:655
  12.5 42.5 %collective-permute-start.20 = (bf16[256,2048]{1,0:T(8,128)(2,1)}, bf16[256,2048]{1,0:T(8,128)(2,1)S(1)}, u32[]{:S(2)}, u32[]{:S(2)}) collective-permute-start(bf16[256,2048]{1,0:T(8,128)(2,1)} %dynamic-slice_bitcast_fusion.3), channel_id=1, source_target_pairs={{0,16},{16,0},{1,17},{17,1},{2,18},{18,2},{3,19},{19,3},{4,20},{20... | collective-permute-start | bytes 3145736 | tf_op jit(solution)/shard_map/ppermute | solution.py:655
  20.7 55.7 %collective-permute-start.22 = (bf16[1024,512]{1,0:T(8,128)(2,1)}, bf16[1024,512]{1,0:T(8,128)(2,1)}, u32[]{:S(2)}, u32[]{:S(2)}) collective-permute-start(bf16[1024,512]{1,0:T(8,128)(2,1)} %dynamic-slice_bitcast_fusion.2), channel_id=1, source_target_pairs={{0,16},{16,0},{1,17},{17,1},{2,18},{18,2},{3,19},{19,3},{4,20},{20... | collective-permute-start | bytes 3145736 | tf_op jit(solution)/shard_map/ppermute | solution.py:655
  80.1 80.9 %collective-permute-start.25 = (bf16[3,256,512]{2,1,0:T(8,128)(2,1)}, bf16[3,256,512]{2,1,0:T(8,128)(2,1)}, u32[]{:S(2)}, u32[]{:S(2)}) collective-permute-start(bf16[3,256,512]{2,1,0:T(8,128)(2,1)} %dynamic-slice_bitcast_fusion.4), channel_id=1, source_target_pairs={{0,16},{16,0},{1,17},{17,1},{2,18},{18,2},{3,19},{19,3},{4,20},{20... | collective-permute-start | bytes 2359304 | tf_op jit(solution)/shard_map/ppermute | solution.py:655
  83.1 78.9 %collective-permute-start.21 = (bf16[256,2048]{1,0:T(8,128)(2,1)S(1)}, bf16[256,2048]{1,0:T(8,128)(2,1)S(1)}, u32[]{:S(2)}, u32[]{:S(2)}) collective-permute-start(bf16[256,2048]{1,0:T(8,128)(2,1)S(1)} %collective-permute-done.20.u1), channel_id=1, source_target_pairs={{0,2},{2,0},{4,6},{6,4},{8,10},{10,8},{12,14},{14,12},{1,3},{3,1},... | collective-permute-start | bytes 3145736 | tf_op jit(solution)/shard_map/ppermute | solution.py:659
  93.7 71.9 %collective-permute-start.23 = (bf16[1024,512]{1,0:T(8,128)(2,1)}, bf16[1024,512]{1,0:T(8,128)(2,1)S(1)}, u32[]{:S(2)}, u32[]{:S(2)}) collective-permute-start(bf16[1024,512]{1,0:T(8,128)(2,1)} %collective-permute-done.22.w1), channel_id=1, source_target_pairs={{0,2},{2,0},{4,6},{6,4},{8,10},{10,8},{12,14},{14,12},{1,3},{3,1},... | collective-permute-start | bytes 3145736 | tf_op jit(solution)/shard_map/ppermute | solution.py:659
  155.4 50.0 %collective-permute-start.44 = (bf16[256,2048]{1,0:T(8,128)(2,1)}, bf16[256,2048]{1,0:T(8,128)(2,1)S(1)}, u32[]{:S(2)}, u32[]{:S(2)}) collective-permute-start(bf16[256,2048]{1,0:T(8,128)(2,1)} %dynamic-slice_bitcast_fusion.1), channel_id=1, source_target_pairs={{0,16},{16,0},{1,17},{17,1},{2,18},{18,2},{3,19},{19,3},{4,20},{20... | collective-permute-start | bytes 3145736 | tf_op jit(solution)/shard_map/ppermute | solution.py:655
  161.0 46.6 %collective-permute-start.46 = (bf16[1024,512]{1,0:T(8,128)(2,1)}, bf16[1024,512]{1,0:T(8,128)(2,1)S(1)}, u32[]{:S(2)}, u32[]{:S(2)}) collective-permute-start(bf16[1024,512]{1,0:T(8,128)(2,1)} %dynamic-slice_bitcast_fusion), channel_id=1, source_target_pairs={{0,16},{16,0},{1,17},{17,1},{2,18},{18,2},{3,19},{19,3},{4,20},{20... | collective-permute-start | bytes 3145736 | tf_op jit(solution)/shard_map/ppermute | solution.py:655
  207.7 84.8 %collective-permute-start.45 = (bf16[256,2048]{1,0:T(8,128)(2,1)S(1)}, bf16[256,2048]{1,0:T(8,128)(2,1)S(1)}, u32[]{:S(2)}, u32[]{:S(2)}) collective-permute-start(bf16[256,2048]{1,0:T(8,128)(2,1)S(1)} %collective-permute-done.44.u1), channel_id=1, source_target_pairs={{0,2},{2,0},{4,6},{6,4},{8,10},{10,8},{12,14},{14,12},{1,3},{3,1},... | collective-permute-start | bytes 3145736 | tf_op jit(solution)/shard_map/ppermute | solution.py:659
  209.9 82.6 %collective-permute-start.47 = (bf16[1024,512]{1,0:T(8,128)(2,1)S(1)}, bf16[1024,512]{1,0:T(8,128)(2,1)S(1)}, u32[]{:S(2)}, u32[]{:S(2)}) collective-permute-start(bf16[1024,512]{1,0:T(8,128)(2,1)S(1)} %collective-permute-done.46.w1), channel_id=1, source_target_pairs={{0,2},{2,0},{4,6},{6,4},{8,10},{10,8},{12,14},{14,12},{1,3},{3,1},... | collective-permute-start | bytes 3145736 | tf_op jit(solution)/shard_map/ppermute | solution.py:659
  225.5 38.1 %collective-permute-start.35 = (bf16[640,128]{1,0:T(8,128)(2,1)}, bf16[640,128]{1,0:T(8,128)(2,1)S(1)}, u32[]{:S(2)}, u32[]{:S(2)}) collective-permute-start(bf16[640,128]{1,0:T(8,128)(2,1)} %get-tuple-element.176), channel_id=1, source_target_pairs={{0,14},{2,0},{4,2},{6,4},{8,6},{10,8},{12,10},{14,12},{1,15},{3,1}... | collective-permute-start | bytes 491528 | tf_op jit(solution)/shard_map/ppermute | solution.py:681
  227.5 45.6 %collective-permute-start.28 = (bf16[256,512]{1,0:T(8,128)(2,1)S(1)}, bf16[256,512]{1,0:T(8,128)(2,1)S(1)}, u32[]{:S(2)}, u32[]{:S(2)}) collective-permute-start(bf16[256,512]{1,0:T(8,128)(2,1)S(1)} %collective-permute-done.27.refs_2_.refs_7_), channel_id=1, source_target_pairs={{0,2},{2,0},{4,6},{6,4},{8,10},{10,8},{12,14},{14,12},{1,3},{3,1},... | collective-permute-start | bytes 786440 | tf_op jit(solution)/shard_map/ppermute | solution.py:659
  378.1 56.1 %collective-permute-start.130 = (bf16[256,2048]{1,0:T(8,128)(2,1)S(1)}, bf16[256,2048]{1,0:T(8,128)(2,1)S(1)}, u32[]{:S(2)}, u32[]{:S(2)}) collective-permute-start(bf16[256,2048]{1,0:T(8,128)(2,1)S(1)} %copy-done.115), channel_id=1, source_target_pairs={{0,16},{16,0},{1,17},{17,1},{2,18},{18,2},{3,19},{19,3},{4,20},{20... | collective-permute-start | bytes 3145736 | tf_op jit(solution)/shard_map/ppermute | solution.py:655
  390.8 75.3 %collective-permute-start.123 = (bf16[256,2048]{1,0:T(8,128)(2,1)S(1)}, bf16[256,2048]{1,0:T(8,128)(2,1)}, u32[]{:S(2)}, u32[]{:S(2)}) collective-permute-start(bf16[256,2048]{1,0:T(8,128)(2,1)S(1)} %copy-done.117), channel_id=1, source_target_pairs={{0,16},{16,0},{1,17},{17,1},{2,18},{18,2},{3,19},{19,3},{4,20},{20... | collective-permute-start | bytes 3145736 | tf_op jit(solution)/shard_map/ppermute | solution.py:655
  392.7 39.6 %collective-permute-start.90 = (bf16[256,512]{1,0:T(8,128)(2,1)S(1)}, bf16[256,512]{1,0:T(8,128)(2,1)S(1)}, u32[]{:S(2)}, u32[]{:S(2)}) collective-permute-start(bf16[256,512]{1,0:T(8,128)(2,1)S(1)} %copy-done.122), channel_id=1, source_target_pairs={{0,16},{16,0},{1,17},{17,1},{2,18},{18,2},{3,19},{19,3},{4,20},{20... | collective-permute-start | bytes 786440 | tf_op jit(solution)/shard_map/ppermute | solution.py:655
  399.3 38.7 %collective-permute-start.139 = (bf16[256,512]{1,0:T(8,128)(2,1)}, bf16[256,512]{1,0:T(8,128)(2,1)S(1)}, u32[]{:S(2)}, u32[]{:S(2)}) collective-permute-start(bf16[256,512]{1,0:T(8,128)(2,1)} %get-tuple-element.267), channel_id=1, source_target_pairs={{0,16},{16,0},{1,17},{17,1},{2,18},{18,2},{3,19},{19,3},{4,20},{20... | collective-permute-start | bytes 786440 | tf_op jit(solution)/shard_map/ppermute | solution.py:655
  432.3 74.2 %collective-permute-start.138 = (bf16[256,2048]{1,0:T(8,128)(2,1)S(1)}, bf16[256,2048]{1,0:T(8,128)(2,1)S(1)}, u32[]{:S(2)}, u32[]{:S(2)}) collective-permute-start(bf16[256,2048]{1,0:T(8,128)(2,1)S(1)} %copy-done.116), channel_id=1, source_target_pairs={{0,16},{16,0},{1,17},{17,1},{2,18},{18,2},{3,19},{19,3},{4,20},{20... | collective-permute-start | bytes 3145736 | tf_op jit(solution)/shard_map/ppermute | solution.py:655
  441.2 69.3 %collective-permute-start.91 = (bf16[3,256,512]{2,1,0:T(8,128)(2,1)}, bf16[3,256,512]{2,1,0:T(8,128)(2,1)S(1)}, u32[]{:S(2)}, u32[]{:S(2)}) collective-permute-start(bf16[3,256,512]{2,1,0:T(8,128)(2,1)} %get-tuple-element.237.b), channel_id=1, source_target_pairs={{0,16},{16,0},{1,17},{17,1},{2,18},{18,2},{3,19},{19,3},{4,20},{20... | collective-permute-start | bytes 2359304 | tf_op jit(solution)/shard_map/ppermute | solution.py:655
  478.7 87.2 %collective-permute-start.124 = (bf16[4,1,64,2048]{3,2,1,0:T(8,128)(2,1)}, bf16[4,1,64,2048]{3,2,1,0:T(8,128)(2,1)S(1)}, u32[]{:S(2)}, u32[]{:S(2)}) collective-permute-start(bf16[4,1,64,2048]{3,2,1,0:T(8,128)(2,1)} %get-tuple-element.259), channel_id=1, source_target_pairs={{0,2},{2,0},{4,6},{6,4},{8,10},{10,8},{12,14},{14,12},{1,3},{3,1},... | collective-permute-start | bytes 3145736 | tf_op jit(solution)/shard_map/ppermute | solution.py:659
  518.7 47.7 %collective-permute-start.140 = (bf16[4,1,256,512]{3,2,1,0:T(8,128)(2,1)}, bf16[4,1,256,512]{3,2,1,0:T(8,128)(2,1)S(1)}, u32[]{:S(2)}, u32[]{:S(2)}) collective-permute-start(bf16[4,1,256,512]{3,2,1,0:T(8,128)(2,1)} %get-tuple-element.269), channel_id=1, source_target_pairs={{0,2},{2,0},{4,6},{6,4},{8,10},{10,8},{12,14},{14,12},{1,3},{3,1},... | collective-permute-start | bytes 3145736 | tf_op jit(solution)/shard_map/ppermute | solution.py:659
  541.8 111.9 %collective-permute-start.82 = (bf16[256,512]{1,0:T(8,128)(2,1)}, bf16[256,512]{1,0:T(8,128)(2,1)}, u32[]{:S(2)}, u32[]{:S(2)}) collective-permute-start(bf16[256,512]{1,0:T(8,128)(2,1)} %get-tuple-element.231), channel_id=1, source_target_pairs={{0,16},{16,0},{1,17},{17,1},{2,18},{18,2},{3,19},{19,3},{4,20},{20... | collective-permute-start | bytes 786440 | tf_op jit(solution)/shard_map/ppermute | solution.py:655
  581.4 224.3 %collective-permute-start.48 = (bf16[256,1024]{1,0:T(8,128)(2,1)}, bf16[256,1024]{1,0:T(8,128)(2,1)}, u32[]{:S(2)}, u32[]{:S(2)}) collective-permute-start(bf16[256,1024]{1,0:T(8,128)(2,1)} %get-tuple-element.187), channel_id=1, source_target_pairs={{0,1},{1,0},{2,3},{3,2},{4,5},{5,4},{6,7},{7,6},{8,9},{9,8},{10,11... | collective-permute-start | bytes 1572872 | tf_op jit(solution)/shard_map/ppermute | solution.py:655
  587.7 66.0 %collective-permute-start.83 = (bf16[3,256,512]{2,1,0:T(8,128)(2,1)}, bf16[3,256,512]{2,1,0:T(8,128)(2,1)}, u32[]{:S(2)}, u32[]{:S(2)}) collective-permute-start(bf16[3,256,512]{2,1,0:T(8,128)(2,1)} %get-tuple-element.232.b), channel_id=1, source_target_pairs={{0,16},{16,0},{1,17},{17,1},{2,18},{18,2},{3,19},{19,3},{4,20},{20... | collective-permute-start | bytes 2359304 | tf_op jit(solution)/shard_map/ppermute | solution.py:655
  653.6 53.7 %collective-permute-start.116 = (bf16[4,1,64,2048]{3,2,1,0:T(8,128)(2,1)}, bf16[4,1,64,2048]{3,2,1,0:T(8,128)(2,1)S(1)}, u32[]{:S(2)}, u32[]{:S(2)}) collective-permute-start(bf16[4,1,64,2048]{3,2,1,0:T(8,128)(2,1)} %get-tuple-element.254), channel_id=1, source_target_pairs={{0,2},{2,0},{4,6},{6,4},{8,10},{10,8},{12,14},{14,12},{1,3},{3,1},... | collective-permute-start | bytes 3145736 | tf_op jit(solution)/shard_map/ppermute | solution.py:659
  653.7 37.2 %collective-permute-start.133 = (bf16[2,1,256,512]{3,2,1,0:T(8,128)(2,1)S(1)}, bf16[2,1,256,512]{3,2,1,0:T(8,128)(2,1)S(1)}, u32[]{:S(2)}, u32[]{:S(2)}) collective-permute-start(bf16[2,1,256,512]{3,2,1,0:T(8,128)(2,1)S(1)} %get-tuple-element.295), channel_id=1, source_target_pairs={{0,4},{2,6},{4,0},{6,2},{8,12},{10,14},{12,8},{14,10},{1,5},{3,7},... | collective-permute-start | bytes 1572872 | tf_op jit(solution)/shard_map/ppermute | solution.py:659
  675.6 42.1 %collective-permute-start.84 = (bf16[4,3,64,512]{3,2,1,0:T(8,128)(2,1)}, bf16[4,3,64,512]{3,2,1,0:T(8,128)(2,1)S(1)}, u32[]{:S(2)}, u32[]{:S(2)}) collective-permute-start(bf16[4,3,64,512]{3,2,1,0:T(8,128)(2,1)} %get-tuple-element.234), channel_id=1, source_target_pairs={{0,2},{2,0},{4,6},{6,4},{8,10},{10,8},{12,14},{14,12},{1,3},{3,1},... | collective-permute-start | bytes 2359304 | tf_op jit(solution)/shard_map/ppermute | solution.py:659
  717.3 90.6 %collective-permute-start.144 = (bf16[2,1,256,512]{3,2,1,0:T(8,128)(2,1)S(1)}, bf16[2,1,256,512]{3,2,1,0:T(8,128)(2,1)S(1)}, u32[]{:S(2)}, u32[]{:S(2)}) collective-permute-start(bf16[2,1,256,512]{3,2,1,0:T(8,128)(2,1)S(1)} %pad_maximum_fusion.9), channel_id=1, source_target_pairs={{0,4},{2,6},{4,0},{6,2},{8,12},{10,14},{12,8},{14,10},{1,5},{3,7},... | collective-permute-start | bytes 1572872 | tf_op jit(solution)/shard_map/ppermute | solution.py:659
  717.7 78.2 %collective-permute-start.128 = (bf16[2,1,64,2048]{3,2,1,0:T(8,128)(2,1)S(1)}, bf16[2,1,64,2048]{3,2,1,0:T(8,128)(2,1)S(1)}, u32[]{:S(2)}, u32[]{:S(2)}) collective-permute-start(bf16[2,1,64,2048]{3,2,1,0:T(8,128)(2,1)S(1)} %pad_maximum_fusion.7), channel_id=1, source_target_pairs={{0,4},{2,6},{4,0},{6,2},{8,12},{10,14},{12,8},{14,10},{1,5},{3,7},... | collective-permute-start | bytes 1572872 | tf_op jit(solution)/shard_map/ppermute | solution.py:659
  823.2 49.7 %collective-permute-start.129 = (bf16[4,1,64,2048]{3,2,1,0:T(8,128)(2,1)}, bf16[4,1,64,2048]{3,2,1,0:T(8,128)(2,1)}, u32[]{:S(2)}, u32[]{:S(2)}) collective-permute-start(bf16[4,1,64,2048]{3,2,1,0:T(8,128)(2,1)} %pad_maximum_fusion.1), channel_id=1, source_target_pairs={{0,2},{2,0},{4,6},{6,4},{8,10},{10,8},{12,14},{14,12},{1,3},{3,1},... | collective-permute-start | bytes 3145736 | tf_op jit(solution)/shard_map/ppermute | solution.py:659
  825.2 70.1 %collective-permute-start.137 = (bf16[4,1,256,512]{3,2,1,0:T(8,128)(2,1)}, bf16[4,1,256,512]{3,2,1,0:T(8,128)(2,1)}, u32[]{:S(2)}, u32[]{:S(2)}) collective-permute-start(bf16[4,1,256,512]{3,2,1,0:T(8,128)(2,1)} %pad_maximum_fusion.2), channel_id=1, source_target_pairs={{0,2},{2,0},{4,6},{6,4},{8,10},{10,8},{12,14},{14,12},{1,3},{3,1},... | collective-permute-start | bytes 3145736 | tf_op jit(solution)/shard_map/ppermute | solution.py:659
  830.3 108.5 %collective-permute-start.121 = (bf16[4,1,64,2048]{3,2,1,0:T(8,128)(2,1)}, bf16[4,1,64,2048]{3,2,1,0:T(8,128)(2,1)S(1)}, u32[]{:S(2)}, u32[]{:S(2)}) collective-permute-start(bf16[4,1,64,2048]{3,2,1,0:T(8,128)(2,1)} %pad_maximum_fusion), channel_id=1, source_target_pairs={{0,2},{2,0},{4,6},{6,4},{8,10},{10,8},{12,14},{14,12},{1,3},{3,1},... | collective-permute-start | bytes 3145736 | tf_op jit(solution)/shard_map/ppermute | solution.py:659
  832.3 99.7 %collective-permute-start.89 = (bf16[4,3,64,512]{3,2,1,0:T(8,128)(2,1)}, bf16[4,3,64,512]{3,2,1,0:T(8,128)(2,1)}, u32[]{:S(2)}, u32[]{:S(2)}) collective-permute-start(bf16[4,3,64,512]{3,2,1,0:T(8,128)(2,1)} %pad_maximum_fusion.4), channel_id=1, source_target_pairs={{0,2},{2,0},{4,6},{6,4},{8,10},{10,8},{12,14},{14,12},{1,3},{3,1},... | collective-permute-start | bytes 2359304 | tf_op jit(solution)/shard_map/ppermute | solution.py:659
  (282 other events, 5012.3 us)

commit v2 on v1

v2 whole, which is shorter than its diff:
```python
import functools

import jax
import jax.numpy as jnp
from jax import lax
from jax.experimental import pallas as pl
from jax.experimental.pallas import tpu as pltpu
from jax.sharding import PartitionSpec as P

HEAD_DIM = 128
LAYERS = 2
SEG = 128
EPSILON = 1e-05
MASKED = -1e30
SCALE = HEAD_DIM ** (-0.5)
GELU_A = 0.7978845608028654
GELU_B = 0.044715
BF = jnp.bfloat16
F32 = jnp.float32
VLIM = 56 * 1024 * 1024

NN = (((1,), (0,)), ((), ()))
NT = (((1,), (1,)), ((), ()))
TN = (((0,), (0,)), ((), ()))


def mm(a, b, dims=NN):
    return lax.dot_general(a, b, dims, preferred_element_type=F32)


def sds(shape, dtype):
    return jax.ShapeDtypeStruct(shape, dtype)


VSPEC = pl.BlockSpec(memory_space=pltpu.VMEM)
SSPEC = pl.BlockSpec(memory_space=pltpu.SMEM)


def cost(flops, nbytes):
    return pl.CostEstimate(flops=int(flops), bytes_accessed=int(nbytes), transcendentals=0)


def kernel_call(body, args, in_specs, out_specs, out_shape, name, scratch=(), grid=None,
                deps=(), work=None, aliases=None):
    count, extra = len(args), len(deps)

    def ordered(*refs):
        body(*refs[:count], *refs[count + extra :])

    kwargs = {} if grid is None else {"grid": grid}
    return pl.pallas_call(
        ordered,
        in_specs=list(in_specs) + [pl.BlockSpec(memory_space=pl.ANY)] * extra,
        out_specs=out_specs,
        out_shape=out_shape,
        scratch_shapes=list(scratch),
        input_output_aliases=aliases or {},
        compiler_params=pltpu.CompilerParams(vmem_limit_bytes=VLIM),
        cost_estimate=work,
        name=name,
        **kwargs,
    )(*args, *deps)


def norm_rows(v):
    centered = v - jnp.mean(v, axis=-1, keepdims=True)
    rstd = lax.rsqrt(jnp.mean(centered * centered, axis=-1, keepdims=True) + EPSILON)
    return centered * rstd, rstd


def norm_back(d, v, gain):
    xhat, rstd = norm_rows(v)
    dx = d * gain
    back = rstd * (
        dx
        - jnp.mean(dx, axis=-1, keepdims=True)
        - xhat * jnp.mean(dx * xhat, axis=-1, keepdims=True)
    )
    d_gain = jnp.sum(d * xhat, axis=0, keepdims=True)
    d_shift = jnp.sum(d, axis=0, keepdims=True)
    return back, d_gain, d_shift


class Dims:
    def __init__(self, tokens, qkv_weight, up_weight):
        self.tp = lax.axis_size("tp")
        self.C = lax.axis_size("ctx")
        self.T = tokens.shape[0] * self.tp
        self.D = tokens.shape[1]
        self.H = self.D // lax.axis_size("fsdp")
        self.Q = self.H // 2
        self.W = qkv_weight.shape[3]
        self.F = up_weight.shape[2]
        self.lh = self.W // HEAD_DIM
        self.g = self.C // self.lh
        self.rq = self.T // self.g
        self.chunk = self.rq + 2 * self.T
        self.bits = self.C.bit_length() - 1


def offs(sc, d):
    x = sc[0]
    y = sc[1]
    own = pl.multiple_of(x * d.H, d.H)
    oth = pl.multiple_of((1 - x) * d.H, d.H)
    first = pl.multiple_of((1 - x) * d.H + y * d.Q, d.Q)
    second = pl.multiple_of((1 - x) * d.H + (1 - y) * d.Q, d.Q)
    return own, oth, first, second


def spot_of(d, chip):
    row, head = (chip % d.g) * d.rq, (chip // d.g) * HEAD_DIM
    return slice(row, row + d.rq), slice(head, head + HEAD_DIM)


def qkv_body(d, first, *refs):
    if first:
        sc, hid, gain, shift, w, w1, w2, qvb = refs[:8]
        rest = refs[8:]
        hidden = hid[...].astype(F32)
    else:
        sc, mid, pa, pb, bias, gain, shift, w, w1, w2, qvb = refs[:11]
        rest = refs[11:]
        hidden = mid[...] + ((pa[...].astype(F32) + pb[...].astype(F32)) + bias[...])
    h_out, no_out, ns_out, chunks, n_out, scr = rest
    own, oth, p1, p2 = offs(sc, d)
    h_out[...] = hidden
    xhat, _ = norm_rows(hidden)
    n_out[...] = (xhat * gain[...] + shift[...]).astype(BF)
    ns_out[...] = n_out[:, pl.ds(oth, d.H)]
    a0 = n_out[:, pl.ds(own, d.H)]
    no_out[...] = a0
    a1 = n_out[:, pl.ds(p1, d.Q)]
    a2 = n_out[:, pl.ds(p2, d.Q)]
    for n in range(3):
        proj = mm(a0, w[n]) + mm(a1, w1[n]) + mm(a2, w2[n])
        if n == 0:
            proj = proj + qvb[0:1, :]
        if n == 2:
            proj = proj + qvb[1:2, :]
        scr[n] = proj.astype(BF)
    for to in range(d.C):
        row, col = spot_of(d, to)
        chunks[to, 0 : d.rq, :] = scr[0, row, col]
        chunks[to, d.rq : d.rq + d.T, :] = scr[1, :, col]
        chunks[to, d.rq + d.T :, :] = scr[2, :, col]


def whole(shape):
    return pl.BlockSpec(shape, lambda *_: (0,) * len(shape))


def piece_specs(shape, pieces, axis):
    if pieces[0] is not pieces[1]:
        return [whole(shape), whole(shape)]
    second = tuple(1 if k == axis else 0 for k in range(len(shape)))
    return [whole(shape), pl.BlockSpec(shape, lambda *_: second)]


def qkv_forward(d, layer, sc, hid, gain, shift, w, pieces, qvb, deps=()):
    first = not isinstance(hid, tuple)
    hid = (hid,) if first else hid
    wspec = pl.BlockSpec((None, 3, d.H, d.W), lambda i: (layer, 0, 0, 0))
    in_specs = [SSPEC] + [whole(a.shape) for a in hid]
    in_specs += [whole(gain.shape), whole(shift.shape), wspec]
    in_specs += piece_specs((3, d.Q, d.W), pieces, 1) + [whole(qvb.shape)]
    outs = [sds((d.T, d.D), F32), sds((d.T, d.H), BF), sds((d.T, d.H), BF)]
    outs += [sds((d.C, d.chunk, HEAD_DIM), BF)]
    return kernel_call(
        functools.partial(qkv_body, d, first),
        (sc, *hid, gain, shift, w, *pieces, qvb,),
        grid=(1,),
        in_specs=in_specs,
        out_specs=[whole(o.shape) for o in outs],
        out_shape=outs,
        scratch=[pltpu.VMEM((d.T, d.D), BF), pltpu.VMEM((3, d.T, d.W), BF)],
        work=cost(2 * d.T * d.D * 3 * d.W, 8e6),
        name="qkv_forward",
        deps=deps,
    )


def load_chunks(d, sc, chunks, qs, ks, vs):
    qs[...] = chunks[:, 0 : d.rq, :]
    ks[...] = chunks[:, d.rq : d.rq + d.T, :]
    vs[...] = chunks[:, d.rq + d.T :, :]


def score_block(d, sc, kb, q, k, s, ext):
    part = lax.rem(sc[2], d.g)
    seg = s * (d.T // SEG) + lax.div(part * d.rq, SEG)
    scores = mm(q, k, NT) * SCALE + kb[pl.ds(seg, 1), 0:ext]
    col = lax.broadcasted_iota(jnp.int32, (d.rq, ext), 1) - s * d.T
    row = lax.broadcasted_iota(jnp.int32, (d.rq, ext), 0) + part * d.rq
    return jnp.where(col <= row, scores, MASKED)


UNROLL = 8
SHIFT = 3


def each_source(d, one):
    if d.C <= UNROLL:
        for s in range(d.C):
            one(s, s + 1)
    else:
        lax.fori_loop(0, d.C, lambda s, carry: (one(s, d.C), carry)[1], 0)


def attend_body(d, *refs):
    sc, kb, chunks, cs, qs, ks, vs = refs
    load_chunks(d, sc, chunks, qs, ks, vs)
    def one(s, seen):
        ext = seen * d.T
        k = ks[0:seen].reshape(ext, HEAD_DIM)
        v = vs[0:seen].reshape(ext, HEAD_DIM)
        scores = score_block(d, sc, kb, qs[s], k, s, ext)
        e = jnp.exp(scores - jnp.max(scores, axis=-1, keepdims=True))
        total = jnp.sum(e, axis=-1, keepdims=True)
        cs[s] = (mm(e.astype(BF), v) / total).astype(BF)

    each_source(d, one)


def attend_forward(d, sc, kb, chunks, deps=()):
    return kernel_call(
        functools.partial(attend_body, d),
        (sc, kb, chunks,),
        in_specs=[SSPEC] + [VSPEC] * 2,
        out_specs=VSPEC,
        out_shape=sds((d.C, d.rq, HEAD_DIM), BF),
        scratch=[
            pltpu.VMEM((d.C, d.rq, HEAD_DIM), BF),
            pltpu.VMEM((d.C, d.T, HEAD_DIM), BF),
            pltpu.VMEM((d.C, d.T, HEAD_DIM), BF),
        ],
        work=cost(2 * d.C * d.rq * d.C * d.T * HEAD_DIM * 2, 3e6),
        name="attend_forward",
        deps=deps,
    )


def out_body(d, *refs):
    sc, w, w1, w2, chunks, ctx, part = refs
    for src in range(d.C):
        ctx[spot_of(d, src)] = chunks[src]
    own, oth, _, _ = offs(sc, d)
    half = d.W // 2
    k1 = pl.multiple_of(sc[1] * half, half)
    k2 = pl.multiple_of((1 - sc[1]) * half, half)
    part[:, pl.ds(own, d.H)] = mm(ctx[...], w[...]).astype(BF)
    part[:, pl.ds(oth, d.H)] = (
        mm(ctx[:, pl.ds(k1, half)], w1[...]) + mm(ctx[:, pl.ds(k2, half)], w2[...])
    ).astype(BF)


def out_forward(d, layer, sc, w, pieces, chunks, deps=()):
    wspec = pl.BlockSpec((None, d.W, d.H), lambda i: (layer, 0, 0))
    outs = [sds((d.T, d.W), BF), sds((d.T, d.D), BF)]
    return kernel_call(
        functools.partial(out_body, d),
        (sc, w, *pieces, chunks,),
        grid=(1,),
        in_specs=[SSPEC, wspec] + piece_specs((d.W // 2, d.H), pieces, 0)
        + [whole(chunks.shape)],
        out_specs=[whole(o.shape) for o in outs],
        out_shape=outs,
        work=cost(2 * d.T * d.D * d.W, 3e6),
        name="out_forward",
        deps=deps,
    )


FT = 512


def tile_of(f, sc, tiles, refs, use):
    half = tiles // 2
    mine = lax.rem(f, half) == sc[1]
    for number, (came, then) in enumerate((refs[:2], refs[2:])):
        here = lax.div(f, half) == number

        @pl.when(jnp.logical_and(here, mine))
        def _():
            use(came)

        @pl.when(jnp.logical_and(here, jnp.logical_not(mine)))
        def _():
            use(then)


def ffn_body(d, tiles, sc, hid, pa, pb, bias, gain, shift,
             u, u1, u2, u3, u4, ub, w, w1, w2, w3, w4,
             mid, no, act_p, act_q, dg, part, n2, acc, pre):
    f = pl.program_id(0)
    own, oth, _, _ = offs(sc, d)

    @pl.when(f == 0)
    def _():
        m = hid[...] + ((pa[...].astype(F32) + pb[...].astype(F32)) + bias[...])
        mid[...] = m
        xhat, _ = norm_rows(m)
        n2[...] = (xhat * gain[...] + shift[...]).astype(BF)
        no[...] = n2[:, pl.ds(own, d.H)]
        act_p[0] = n2[:, pl.ds(oth, d.H)]
        acc[...] = jnp.zeros_like(acc)

    def up(ref):
        pre[...] = mm(act_p[0], ref[...])

    tile_of(f, sc, tiles, (u1, u2, u3, u4), up)
    v = pre[...] + mm(no[...], u[...]) + ub[...]
    sq = v * v
    th = jnp.tanh(GELU_A * v * (1.0 + GELU_B * sq))
    half = 0.5 * (1.0 + th)
    a = (v * half).astype(BF)

    @pl.when(f < tiles // 2)
    def _():
        act_p[1 + f] = a

    @pl.when(f >= tiles // 2)
    def _():
        act_q[f - tiles // 2] = a

    dg[...] = (
        half + 0.5 * v * (1.0 - th * th) * (GELU_A * (1.0 + 3.0 * GELU_B * sq))
    ).astype(BF)
    acc[0] += mm(a, w[...])

    def down(ref):
        acc[1] += mm(a, ref[...])

    tile_of(f, sc, tiles, (w1, w2, w3, w4), down)

    @pl.when(f == tiles - 1)
    def _():
        part[:, pl.ds(own, d.H)] = acc[0].astype(BF)
        part[:, pl.ds(oth, d.H)] = acc[1].astype(BF)


def ffn_specs(d, layer):
    u = pl.BlockSpec((None, d.H, FT), lambda f: (layer, 0, f))
    w = pl.BlockSpec((None, FT, d.H), lambda f: (layer, f, 0))
    tile = whole((d.H, FT))
    low = pl.BlockSpec((None, FT, d.H), lambda f: (0, 0, 0))
    high = pl.BlockSpec((None, FT, d.H), lambda f: (1, 0, 0))
    return [u] + [tile] * 4, [w, low, low, high, high]


def ffn_forward(d, layer, sc, hid, pa, pb, bias, gain, shift,
                up_w, up_p, ub, dn_w, dn_p, deps=()):
    tiles = d.F // FT
    us, ws = ffn_specs(d, layer)
    side = whole((d.T, d.H))
    col = pl.BlockSpec((d.T, FT), lambda f: (0, f))
    row = whole((1, d.D))
    full = whole((d.T, d.D))
    act_p = sds((1 + tiles // 2, d.T, FT), BF)
    act_q = sds((tiles // 2, d.T, FT), BF)
    return kernel_call(
        functools.partial(ffn_body, d, tiles),
        (sc, hid, pa, pb, bias, gain, shift, up_w, *up_p, ub, dn_w, *dn_p),
        [SSPEC, full, full, full, row, row, row, *us,
         pl.BlockSpec((1, FT), lambda f: (0, f)), *ws],
        [full, side, whole(act_p.shape), whole(act_q.shape), col, full],
        [sds((d.T, d.D), F32), sds((d.T, d.H), BF), act_p, act_q,
         sds((d.T, d.F), BF), sds((d.T, d.D), BF)],
        "ffn_forward",
        scratch=[pltpu.VMEM((d.T, d.D), BF), pltpu.VMEM((2, d.T, d.H), F32),
                 pltpu.VMEM((d.T, FT), F32)],
        grid=(tiles,), deps=deps, work=cost(4 * d.T * d.D * d.F, 14e6))


def ffn_back_body(d, tiles, sc, grad, dg, u, u1, u2, u3, u4, w, w1, w2, w3, w4,
                  dbo, xba, xbb, usum, bsum, part, acc, dact):
    f = pl.program_id(0)
    own, oth, _, _ = offs(sc, d)

    @pl.when(f == 0)
    def _():
        dbo[...] = grad[:, pl.ds(own, d.H)].astype(BF)
        xba[0] = grad[:, pl.ds(oth, d.H)].astype(BF)
        bsum[...] = jnp.sum(grad[...].astype(BF).astype(F32), axis=0, keepdims=True)
        acc[...] = jnp.zeros_like(acc)

    def down(ref):
        dact[...] = mm(xba[0], ref[...], NT)

    tile_of(f, sc, tiles, (w1, w2, w3, w4), down)
    da = dact[...] + mm(dbo[...], w[...], NT)
    dp = (da * dg[...].astype(F32)).astype(BF)

    @pl.when(f == 0)
    def _():
        xba[1] = dp

    @pl.when(f > 0)
    def _():
        xbb[f - 1] = dp

    usum[...] = jnp.sum(dp.astype(F32), axis=0, keepdims=True)
    acc[0] += mm(dp, u[...], NT)

    def up(ref):
        acc[1] += mm(dp, ref[...], NT)

    tile_of(f, sc, tiles, (u1, u2, u3, u4), up)

    @pl.when(f == tiles - 1)
    def _():
        part[:, pl.ds(own, d.H)] = acc[0].astype(BF)
        part[:, pl.ds(oth, d.H)] = acc[1].astype(BF)


def ffn_backward(d, layer, sc, grad, dg, up_w, up_p, dn_w, dn_p, deps=()):
    tiles = d.F // FT
    us, ws = ffn_specs(d, layer)
    side = whole((d.T, d.H))
    col = pl.BlockSpec((d.T, FT), lambda f: (0, f))
    full = whole((d.T, d.D))
    xba = sds((2, d.T, FT), BF)
    xbb = sds((tiles - 1, d.T, FT), BF)
    return kernel_call(
        functools.partial(ffn_back_body, d, tiles),
        (sc, grad, dg, up_w, *up_p, dn_w, *dn_p),
        [SSPEC, full, col, *us, *ws],
        [side, whole(xba.shape), whole(xbb.shape),
         pl.BlockSpec((1, FT), lambda f: (0, f)), whole((1, d.D)), full],
        [sds((d.T, d.H), BF), xba, xbb,
         sds((1, d.F), F32), sds((1, d.D), F32), sds((d.T, d.D), BF)],
        "ffn_backward",
        scratch=[pltpu.VMEM((2, d.T, d.H), F32), pltpu.VMEM((d.T, FT), F32)],
        grid=(tiles,), deps=deps, work=cost(4 * d.T * d.D * d.F, 14e6))


def context_back_body(d, *refs):
    sc, grad, pa, pb, mid, gain, w, w1, w2 = refs[:9]
    dmid, dao, das, gsum, ssum, asum, chunks, da, dctx = refs[9:]
    own, oth, _, _ = offs(sc, d)
    back, g, s = norm_back(pa[...].astype(F32) + pb[...].astype(F32), mid[...], gain[...])
    gsum[...] = g
    ssum[...] = s
    total = grad[...].astype(F32) + back
    dmid[...] = total
    da[...] = total.astype(BF)
    dao[...] = da[:, pl.ds(own, d.H)]
    das[...] = da[:, pl.ds(oth, d.H)]
    asum[...] = jnp.sum(da[...].astype(F32), axis=0, keepdims=True)
    half = d.W // 2
    k1 = pl.multiple_of(sc[1] * half, half)
    k2 = pl.multiple_of((1 - sc[1]) * half, half)
    dctx[...] = mm(da[:, pl.ds(own, d.H)], w[...], NT)
    dctx[:, pl.ds(k1, half)] += mm(da[:, pl.ds(oth, d.H)], w1[...], NT)
    dctx[:, pl.ds(k2, half)] += mm(da[:, pl.ds(oth, d.H)], w2[...], NT)
    for to in range(d.C):
        chunks[to] = dctx[spot_of(d, to)].astype(BF)


def context_backward(d, layer, sc, grad, pa, pb, mid, gain, w, pieces, deps=()):
    wspec = pl.BlockSpec((None, d.W, d.H), lambda i: (layer, 0, 0))
    outs = [sds((d.T, d.D), F32), sds((d.T, d.H), BF), sds((d.T, d.H), BF)]
    outs += [sds((1, d.D), F32)] * 3 + [sds((d.C, d.rq, HEAD_DIM), BF)]
    return kernel_call(
        functools.partial(context_back_body, d),
        (sc, grad, pa, pb, mid, gain, w, *pieces,),
        grid=(1,),
        in_specs=[SSPEC] + [whole(a.shape) for a in (grad, pa, pb, mid, gain)]
        + [wspec] + piece_specs((d.W // 2, d.H), pieces, 0),
        out_specs=[whole(o.shape) for o in outs],
        out_shape=outs,
        scratch=[pltpu.VMEM((d.T, d.D), BF), pltpu.VMEM((d.T, d.W), F32)],
        work=cost(2 * d.T * d.D * d.W, 6e6),
        name="context_backward",
        deps=deps,
    )


def attend_back_body(d, *refs):
    sc, kb, chunks, cs, outs, qs, ks, vs, dks, dvs = refs
    load_chunks(d, sc, chunks, qs, ks, vs)
    dks[...] = jnp.zeros_like(dks)
    dvs[...] = jnp.zeros_like(dvs)
    def one(s, seen):
        ext = seen * d.T
        k = ks[0:seen].reshape(ext, HEAD_DIM)
        v = vs[0:seen].reshape(ext, HEAD_DIM)
        q = qs[s]
        dc = cs[s]
        scores = score_block(d, sc, kb, q, k, s, ext)
        e = jnp.exp(scores - jnp.max(scores, axis=-1, keepdims=True))
        p = e / jnp.sum(e, axis=-1, keepdims=True)
        dp = mm(dc, v, NT)
        ds = (p * (dp - jnp.sum(p * dp, axis=-1, keepdims=True))).astype(BF)
        outs[s, 0 : d.rq, :] = (mm(ds, k) * SCALE).astype(BF)
        dks[0:seen] += mm(ds, q, TN).reshape(seen, d.T, HEAD_DIM)
        dvs[0:seen] += mm(p.astype(BF), dc, TN).reshape(seen, d.T, HEAD_DIM)

    each_source(d, one)
    outs[:, d.rq : d.rq + d.T, :] = (dks[...] * SCALE).astype(BF)
    outs[:, d.rq + d.T :, :] = dvs[...].astype(BF)


def attend_backward(d, sc, kb, chunks, dchunks, deps=()):
    return kernel_call(
        functools.partial(attend_back_body, d),
        (sc, kb, chunks, dchunks,),
        in_specs=[SSPEC] + [VSPEC] * 3,
        out_specs=VSPEC,
        out_shape=sds((d.C, d.chunk, HEAD_DIM), BF),
        scratch=[
            pltpu.VMEM((d.C, d.rq, HEAD_DIM), BF),
            pltpu.VMEM((d.C, d.T, HEAD_DIM), BF),
            pltpu.VMEM((d.C, d.T, HEAD_DIM), BF),
            pltpu.VMEM((d.C, d.T, HEAD_DIM), F32),
            pltpu.VMEM((d.C, d.T, HEAD_DIM), F32),
        ],
        work=cost(5 * d.C * d.rq * d.C * d.T * HEAD_DIM * 2, 4e6),
        name="attend_backward",
        deps=deps,
    )


def qkv_back_body(d, sc, w, w1, w2, chunks, xb, qvsum, part, dk, dv):
    dk[...] = jnp.zeros_like(dk)
    dv[...] = jnp.zeros_like(dv)
    for src in range(d.C):
        row, col = spot_of(d, src)
        xb[0, row, col] = chunks[src, 0 : d.rq, :]
        dk[:, col] += chunks[src, d.rq : d.rq + d.T, :].astype(F32)
        dv[:, col] += chunks[src, d.rq + d.T :, :].astype(F32)
    xb[1] = dk[...].astype(BF)
    xb[2] = dv[...].astype(BF)
    qvsum[0:1, :] = jnp.sum(xb[0].astype(F32), axis=0, keepdims=True)
    qvsum[1:2, :] = jnp.sum(xb[2].astype(F32), axis=0, keepdims=True)
    own, _, p1, p2 = offs(sc, d)
    for ref, at, width in ((w, own, d.H), (w1, p1, d.Q), (w2, p2, d.Q)):
        total = mm(xb[0], ref[0], NT) + mm(xb[1], ref[1], NT) + mm(xb[2], ref[2], NT)
        part[:, pl.ds(at, width)] = total.astype(BF)


def qkv_backward(d, layer, sc, w, pieces, chunks, deps=()):
    wspec = pl.BlockSpec((None, 3, d.H, d.W), lambda i: (layer, 0, 0, 0))
    outs = [sds((3, d.T, d.W), BF), sds((2, d.W), F32), sds((d.T, d.D), BF)]
    return kernel_call(
        functools.partial(qkv_back_body, d),
        (sc, w, *pieces, chunks),
        [SSPEC, wspec] + [whole((3, d.Q, d.W))] * 2 + [whole(chunks.shape)],
        [whole(o.shape) for o in outs],
        outs,
        "qkv_backward",
        scratch=[pltpu.VMEM((d.T, d.W), F32)] * 2,
        grid=(1,), deps=deps, work=cost(2 * d.T * d.D * 3 * d.W, 7e6))


def input_back_body(dmid, pa, pb, hid, gain, grad, gsum, ssum):
    back, g, s = norm_back(pa[...].astype(F32) + pb[...].astype(F32), hid[...], gain[...])
    grad[...] = dmid[...] + back
    gsum[...] = g
    ssum[...] = s


def input_backward(d, dmid, pa, pb, hid, gain, deps=()):
    return kernel_call(
        input_back_body,
        (dmid, pa, pb, hid, gain,),
        in_specs=[VSPEC] * 5,
        out_specs=[VSPEC] * 3,
        out_shape=[sds((d.T, d.D), F32)] + [sds((1, d.D), F32)] * 2,
        work=cost(3e6, 5e6),
        name="input_backward",
        deps=deps,
    )


def spot_bits(value, shifts, bits):
    out = 0
    for k in range(bits):
        bit = lax.bitwise_and(lax.shift_right_logical(value, shifts[k]), 1)
        out = out + bit * (1 << (bits - 1 - k))
    return out


def wgrad_body(d, tiles, sc, *refs):
    ins = refs[:-2]
    keep, send = refs[-2:]
    c = sc[2]
    shifts = [sc[SHIFT + k] for k in range(d.bits)]
    rb = FT // d.C
    spots = [spot_bits(lax.bitwise_xor(c, b), shifts, d.bits) for b in range(d.C)]

    def pick(item):
        ref, at = item
        return ins[ref][...] if at is None else ins[ref][at]

    for m, (a, b, a2, b2) in enumerate(tiles):
        total = mm(pick(a), pick(b), TN) + mm(pick(a2), pick(b2), TN)
        total = total.astype(BF)
        for block, spot in enumerate(spots):
            piece = total[block * rb : (block + 1) * rb, :]

            @pl.when(spot < d.C // 2)
            def _():
                keep[spot, m] = piece

            @pl.when(spot >= d.C // 2)
            def _():
                send[spot - d.C // 2, m] = piece


def wgrad_plain_body(tiles, *refs):
    ins, out = refs[:-1], refs[-1]

    def pick(item):
        ref, at = item
        return ins[ref][...] if at is None else ins[ref][at]

    for m, (a, b, a2, b2) in enumerate(tiles):
        total = mm(pick(a), pick(b), TN) + mm(pick(a2), pick(b2), TN)
        out[m] = total.astype(BF)


def weight_grad_plain(d, name, ins, tiles, deps=()):
    return kernel_call(
        functools.partial(wgrad_plain_body, tiles), ins,
        [VSPEC] * len(ins), VSPEC, sds((len(tiles), FT, FT), BF), "weight_grad_" + name,
        deps=deps, work=cost(4 * d.T * len(tiles) * FT * FT, 8e6))


def weight_grad(d, name, sc, ins, tiles, deps=()):
    shape = (d.C // 2, len(tiles), FT // d.C, FT)
    return kernel_call(
        functools.partial(wgrad_body, d, tiles),
        (sc, *ins,),
        in_specs=[SSPEC] + [VSPEC] * len(ins),
        out_specs=[VSPEC] * 2,
        out_shape=[sds(shape, BF)] * 2,
        work=cost(4 * d.T * len(tiles) * FT * FT, 8e6),
        name="weight_grad_" + name,
        deps=deps,
    )


def place_body(d, wide, count_in, extra, layer, owner, plain, sc, *refs):
    ins = refs[:count_in]
    outs = refs[count_in + extra : -2]
    buf, sems = refs[-2:]
    rb = FT // d.C
    if plain:
        buf[...] = ins[0][...].astype(F32)
    else:
        r = 0
        for part in ins:
            for n in range(part.shape[0]):
                row = pl.multiple_of(owner(sc, r) * rb, rb)
                for m in range(part.shape[1]):
                    buf[m, pl.ds(row, rb), :] = part[n, m].astype(F32)
                r += 1
    copies = []
    m = 0
    for out, (kind, count) in zip(outs, wide):
        if kind == "cols":
            for k in range(count):
                copies.append((buf.at[m + k], out.at[layer, :, pl.ds(k * FT, FT)]))
        else:
            copies.append((buf.at[pl.ds(m, count)], out.at[layer]))
        m += count
    going = [pltpu.make_async_copy(a, b, sems.at[k]) for k, (a, b) in enumerate(copies)]
    for one in going:
        one.start()
    for one in going:
        one.wait()


def place(d, layer, sc, parts, before, wide, name, deps=()):
    plain = not isinstance(parts, list)
    parts = [parts] if plain else parts
    nt = parts[0].shape[0 if plain else 1]
    extra = tuple(before or ()) + tuple(deps)
    alias = {1 + len(parts) + k: k for k in range(len(before or ()))}
    shapes = [
        sds((LAYERS, FT, n * FT) if kind == "cols" else (LAYERS, n, FT, FT), F32)
        for kind, n in wide
    ]
    moves = sum(n if kind == "cols" else 1 for kind, n in wide)

    def owner(scalars, r):
        turned = 0
        for k in range(d.bits):
            if r >> (d.bits - 1 - k) & 1:
                turned = turned + lax.shift_left(jnp.int32(1), scalars[SHIFT + k])
        return lax.bitwise_xor(scalars[2], jnp.int32(turned))

    return pl.pallas_call(
        functools.partial(place_body, d, wide, len(parts), len(extra), layer, owner, plain),
        in_specs=[SSPEC] + [VSPEC] * len(parts) + [pl.BlockSpec(memory_space=pl.ANY)] * len(extra),
        out_specs=[pl.BlockSpec(memory_space=pl.ANY)] * len(wide),
        out_shape=shapes,
        scratch_shapes=[pltpu.VMEM((nt, FT, FT), F32), pltpu.SemaphoreType.DMA((moves,))],
        input_output_aliases=alias,
        compiler_params=pltpu.CompilerParams(vmem_limit_bytes=VLIM),
        name="place_" + name,
    )(sc, *parts, *extra)


def swap(values, axis):
    return lax.ppermute(values, axis, [(0, 1), (1, 0)])


def way(d, core, step):
    if step < 2 and d.bits > 1:
        return step if core == 0 else 1 - step
    return step


def cross(d, values, step):
    pairs = []
    for i in range(d.C):
        for core in range(d.tp):
            to = i ^ (1 << way(d, core, step))
            pairs.append((i * d.tp + core, to * d.tp + core))
    return lax.ppermute(values, ("ctx", "tp"), pairs)


def cross_all(d, values, step):
    return lax.ppermute(values, "ctx", [(i, i ^ (1 << step)) for i in range(d.C)])


def take_body(sc, w, *refs):
    refs[-1][...] = w[...]


def take(sc, w, block, index, shape, steps=1, deps=()):
    out_block = shape if steps == 1 else (None, *shape[1:])
    return pl.pallas_call(
        take_body,
        grid_spec=pltpu.PrefetchScalarGridSpec(
            num_scalar_prefetch=1,
            grid=(steps,),
            in_specs=[pl.BlockSpec(block, lambda n, s: index(n, s[1]))]
            + [pl.BlockSpec(memory_space=pl.ANY)] * len(deps),
            out_specs=pl.BlockSpec(out_block, lambda n, s: (n,) + (0,) * (len(shape) - 1)),
        ),
        out_shape=sds(shape, BF),
        compiler_params=pltpu.CompilerParams(vmem_limit_bytes=VLIM),
        name="take",
    )(sc, w, *deps)


def fold_body(keep, got, *outs):
    total = (keep[...].astype(F32) + got[...].astype(F32)).astype(BF)
    if len(outs) == 1:
        outs[0][...] = total
    else:
        half = total.shape[0] // 2
        outs[0][...] = total[:half]
        outs[1][...] = total[half:]


def fold(keep, got, deps=()):
    count = keep.shape[0]
    shapes = [keep.shape] if count == 1 else [(count // 2, *keep.shape[1:])] * 2
    return kernel_call(
        fold_body, (keep, got), [VSPEC] * 2, [VSPEC] * len(shapes),
        [sds(v, BF) for v in shapes], "fold", deps=deps, work=cost(1e6, 3e6))


def join_body(*refs):
    out = refs[-1]
    at = 0
    for ref in refs[:-1]:
        out[at : at + ref.shape[0]] = ref[...]
        at += ref.shape[0]


def join(parts, deps=()):
    if len(parts) == 1:
        return parts[0]
    count = sum(p.shape[0] for p in parts)
    return kernel_call(
        join_body, tuple(parts), [VSPEC] * len(parts), VSPEC,
        sds((count, *parts[0].shape[1:]), BF), "join", deps=deps, work=cost(1e5, 3e6))


class Sum:
    def __init__(self, d, keep, send):
        self.d = d
        self.keep = keep
        self.got = cross(d, send, 0)
        self.at = 0
        self.parts = None

    def step(self, *deps):
        self.at += 1
        n = self.d.bits
        if self.at < n:
            keep, send = fold(self.keep, self.got, deps)
            self.keep = keep
            self.got = cross(self.d, send, self.at)
            return keep
        if self.at == n:
            (keep,) = fold(self.keep, self.got, deps)
            self.parts = [keep]
            self.got = cross(self.d, keep, n - 1)
            return keep
        self.parts.append(self.got)
        if self.at < 2 * n:
            full = join(self.parts, deps)
            self.got = cross(self.d, full, 2 * n - 1 - self.at)
            return full
        return self.got

    def finish(self):
        while self.at < 2 * self.d.bits:
            self.step()
        return self.parts


def all_to_all(values):
    return lax.all_to_all(values, "ctx", 0, 0)


def key_table(d, parent_ids, depth_offsets):
    segs = parent_ids.shape[0] // lax.axis_size("fsdp")
    start = lax.axis_index("fsdp") * segs
    parents = lax.dynamic_slice_in_dim(parent_ids, start, segs) - start
    depths = lax.dynamic_slice_in_dim(depth_offsets, start, segs).astype(F32)
    ids = jnp.arange(segs, dtype=jnp.int32)
    reach = jnp.maximum(
        (parents[:, None] == ids[None, :]).astype(F32), (ids[:, None] == ids[None, :]).astype(F32)
    )
    for _ in range((segs - 1).bit_length()):
        reach = jnp.minimum(jnp.dot(reach, reach), 1.0)
    head = lax.axis_index("tp") * d.lh + lax.axis_index("ctx") // d.g
    slope = jnp.exp2(-(head + 1).astype(F32))
    level = jnp.where(reach > 0.5, slope * (depths[None, :] - depths[:, None]), MASKED)
    spots = slope * jnp.arange(SEG, dtype=jnp.int32).astype(F32)
    return (level[:, :, None] + spots[None, None, :]).reshape(segs, segs * SEG)


def on_device(tokens, qkv_weight, out_weight, up_weight, down_weight, qv_bias, up_bias,
              norm_gains, row_biases, parent_ids, depth_offsets, cotangent):
    d = Dims(tokens, qkv_weight, up_weight)
    x = lax.axis_index("fsdp")
    c = lax.axis_index("ctx")
    t = lax.axis_index("tp")
    first = [jnp.where(t == 0, way(d, 0, k), way(d, 1, k)) for k in range(d.bits)]
    bit = (c >> first[0]) % 2
    sc = jnp.stack([x, bit, c, *first]).astype(jnp.int32)
    w_qkv = qkv_weight.transpose(0, 2, 1, 3)
    tiles = d.F // FT
    half = tiles // 2

    class Pieces:
        def __init__(self, layer, deps):
            def over(values):
                first = swap(values, "fsdp")
                return first, cross(d, first, 0)

            tile = (None, FT, FT)
            qkv = take(sc, w_qkv, (None, 3, d.Q, d.W), lambda n, b: (layer, 0, b, 0),
                       (3, d.Q, d.W), deps=deps)
            out = take(sc, out_weight, (None, d.W // 2, d.H), lambda n, b: (layer, b, 0),
                       (d.W // 2, d.H), deps=(qkv,))
            up_a = take(sc, up_weight, tile, lambda n, b: (layer, 0, b), (FT, FT), deps=(out,))
            up_b = take(sc, up_weight, tile, lambda n, b: (layer, 0, half + b), (FT, FT),
                        deps=(up_a,))
            dn = take(sc, down_weight, tile, lambda n, b: (layer, n * half + b, 0),
                      (2, FT, FT), 2, deps=(up_b,))
            self.last = dn
            self.qkv, self.out, self.dn = over(qkv), over(out), over(dn)
            self.up_a, self.up_b = over(up_a), over(up_b)
            self.up = (*self.up_a, *self.up_b)
            self.down = (*self.dn, *self.dn)

    p0 = Pieces(0, ())
    p = [p0]
    kb = key_table(d, parent_ids, depth_offsets)

    def both(rows):
        got = swap(rows, "tp")
        return jnp.where(
            t == 0,
            jnp.concatenate([rows, got], axis=0),
            jnp.concatenate([got, rows], axis=0),
        )

    def row(values):
        return values.reshape(1, -1)

    def swapped(values):
        return swap(values, "tp")

    def fsdp(values):
        return swap(values, "fsdp")

    class Kept:
        pass

    def forward(layer, state, needs):
        k = kept[layer]
        before = [needs(n) for n in range(1)]
        k.hidden, k.n_o, n_s, chunks = qkv_forward(
            d, layer, sc, state, row(norm_gains[layer, 0]), row(row_biases[layer, 0]),
            w_qkv, p[layer].qkv, qv_bias[layer], deps=before[0])
        k.n_r = fsdp(n_s)
        if layer == 0:
            p.append(Pieces(1, (k.hidden,)))
        before += [needs(n) for n in range(1, 3)]
        k.chunks = all_to_all(chunks)
        outs = all_to_all(attend_forward(d, sc, kb, k.chunks, deps=before[1]))
        k.ctx, part = out_forward(d, layer, sc, out_weight, p[layer].out, outs, deps=before[2])
        k.ctx_r = fsdp(k.ctx)
        before.append(needs(3))
        k.middle, k.n2_o, k.act_p, k.act_q, k.dg, part2 = ffn_forward(
            d, layer, sc, k.hidden, part, swapped(part), row(row_biases[layer, 1]),
            row(norm_gains[layer, 1]), row(row_biases[layer, 2]), up_weight,
            p[layer].up, row(up_bias[layer]), down_weight, p[layer].down, deps=before[3])
        state = (k.middle, part2, swapped(part2), row(row_biases[layer, 3]))
        k.act_pr, k.act_qr = fsdp(k.act_p), fsdp(k.act_q)
        return state

    state = both(tokens)
    p0 = p[0]
    kept = [Kept() for _ in range(LAYERS)]
    k0, k1 = kept
    state = forward(0, state, lambda n: (
        (p0.out[0], p0.up_a[0], p0.last) if n == 0
        else (p0.out[1], p0.up_a[1], p0.up_b[0], p0.dn[0]) if n == 1
        else (p[1].qkv[0], p[1].out[0], p[1].last) if n == 2
        else ()
    ))
    p1 = p[1]
    state = forward(1, state, lambda n: (
        (p1.up_a[0], p1.up_b[0]) if n == 0
        else (p1.out[1], p1.up_a[1], p1.dn[0], k1.n_r) if n == 1
        else (k0.act_pr,) if n == 2
        else ()
    ))
    own_rows = tokens.shape[0]

    def mine(values):
        return lax.dynamic_slice_in_dim(values, t * own_rows, own_rows, 0)

    output = mine(state[0]) + (
        (mine(state[1]).astype(F32) + mine(state[2]).astype(F32)) + state[3]
    )
    output = output.astype(BF)
    grad = both(cotangent)
    sums = [None] * LAYERS
    def grad_ffn(k, more, deps=()):
        ins = (k.n2_o, k.act_p, k.act_pr, k.act_q, k.act_qr, k.xba, k.xba_r, k.xbb, k.xbb_r,
               k.db_o)
        jobs = []
        for f in range(tiles):
            at = (5, 1) if f == 0 else (7, f - 1)
            jobs.append(((0, None), at, (2, 0), (at[0] + 1, at[1])))
        for f in range(tiles):
            at = (1, 1 + f) if f < half else (3, f - half)
            jobs.append((at, (9, None), (at[0] + 1, at[1]), (6, 0)))
        if more:
            ins += (k.ctx, k.ctx_r, k.da_o, k.da_r)
            jobs += [((10, None), (12, None), (11, None), (13, None))]
        return Sum(d, *weight_grad(d, "ffn", sc, ins, jobs, deps))

    def grad_qkv(k, more, deps=()):
        ins = (k.n_o, k.n_r, k.xc, k.xc_r)
        jobs = [((0, None), (2, n), (1, None), (3, n)) for n in range(3)]
        if more:
            ins += (k.ctx, k.da_o, k.ctx_r, k.da_r)
            jobs += [((4, None), (5, None), (6, None), (7, None))]
        return Sum(d, *weight_grad(d, "qkv", sc, ins, jobs, deps))

    def back_ffn(layer, k, grad, deps=()):
        k.db_o, k.xba, k.xbb, k.usum, k.bsum, part = ffn_backward(
            d, layer, sc, grad, k.dg, up_weight, p[layer].up, down_weight, p[layer].down,
            deps=deps)
        k.xba_r, k.xbb_r = fsdp(k.xba), fsdp(k.xbb)
        return part

    def back_context(layer, k, grad, part, deps=()):
        k.dmid, k.da_o, k.da_s, k.gsum2, k.ssum2, k.asum, dchunks = context_backward(
            d, layer, sc, grad, part, swapped(part), k.middle, row(norm_gains[layer, 1]),
            out_weight, p[layer].out, deps=deps)
        k.da_r = fsdp(k.da_s)
        return dchunks

    def back_qkv(layer, k, dparts, deps=()):
        k.xc, k.qvsum, part = qkv_backward(
            d, layer, sc, w_qkv, p[layer].qkv, dparts, deps=deps)
        k.xc_r = fsdp(k.xc)
        return part

    def back_input(layer, k, part, deps=()):
        grad, k.gsum1, k.ssum1 = input_backward(
            d, k.dmid, part, swapped(part), k.hidden, row(norm_gains[layer, 0]), deps=deps)
        sums[layer] = (k.qvsum, k.usum, k.gsum1, k.gsum2, k.ssum1, k.asum, k.ssum2, k.bsum)
        return grad

    def small_sums():
        return jnp.concatenate(
            [v.reshape(-1) for layer in sums for v in layer]
        ).reshape(-1, 128)

    part = back_ffn(1, k1, grad, (k0.act_qr, k1.ctx_r))
    dchunks = back_context(1, k1, grad, part, (state[2],))
    dback = attend_backward(d, sc, kb, k1.chunks, all_to_all(dchunks),
                            deps=(k1.act_pr, k1.act_qr))
    dparts = all_to_all(dback)
    f1 = grad_ffn(k1, False, (dback,))
    part = back_qkv(1, k1, dparts, (f1.keep, k0.n_r, k0.ctx_r))
    grad = back_input(1, k1, part)
    part = back_ffn(0, k0, grad)
    a = f1.step(part)
    dchunks = back_context(0, k0, grad, part, (a, k1.xc_r, k1.da_r))
    q1 = grad_qkv(k1, True, (dchunks,))
    a = f1.step(q1.keep)
    dback = attend_backward(d, sc, kb, k0.chunks, all_to_all(dchunks), deps=(a, k0.xba_r))
    dparts = all_to_all(dback)
    f0 = grad_ffn(k0, True, (dback,))
    part = back_qkv(0, k0, dparts, (f0.keep,))
    grad = back_input(0, k0, part)
    flat = small_sums()
    flat = flat + swap(flat, "fsdp")
    a = q1.step(grad)
    a = f1.step(a)
    a = f0.step(a, flat)
    q0 = grad_qkv(k0, False, (a,))
    a = q1.step(q0.keep)
    a = q0.step(a)
    a = f0.step(a)
    a = f1.step(a)
    flat = flat + cross_all(d, flat, 0)
    a = q1.step(a, flat)
    a = q0.step(a)
    a = f1.step(a)
    a = q1.step(a)
    flats = list(range(1, d.bits))
    while f1.at < 2 * d.bits - 1:
        a = f1.step(a)
    while any(u.at < 2 * d.bits - 1 for u in (q1, q0, f0)):
        for unit in (f0, q1, q0):
            if unit.at < 2 * d.bits - 1:
                if unit is f0 and flats:
                    flat = flat + cross_all(d, flat, flats.pop(0))
                a = unit.step(a, flat) if unit is f0 else unit.step(a)
    for step in flats:
        flat = flat + cross_all(d, flat, step)
    ffn_kinds = (("cols", tiles), ("mats", tiles))
    g_ffn = place(d, 1, sc, f1.finish(), None, ffn_kinds, "ffn", (a,))
    g_qkv = place(d, 1, sc, q1.finish(), None, (("mats", 3), ("mats", 1)), "qkv", (g_ffn[0],))
    g_up, g_down, g_out = place(d, 0, sc, f0.finish(), (*g_ffn, g_qkv[1]),
                                (*ffn_kinds, ("mats", 1)), "ffn", (a,))
    (g_qkv,) = place(d, 0, sc, q0.finish(), (g_qkv[0],), (("mats", 3),), "qkv", (g_up,))
    flat = flat.reshape(LAYERS, -1)
    n_qv, n_up = 2 * d.W, d.F
    qv_grad = flat[:, :n_qv].reshape(LAYERS, 2, d.W)
    up_grad = flat[:, n_qv : n_qv + n_up]
    rest = flat[:, n_qv + n_up :].reshape(LAYERS, 6, d.D)
    return (
        output,
        mine(grad),
        g_qkv.transpose(0, 2, 1, 3),
        g_out.reshape(LAYERS, d.W, d.H),
        g_up.reshape(LAYERS, d.H, d.F),
        g_down.reshape(LAYERS, d.F, d.H),
        qv_grad,
        up_grad,
        rest[:, :2],
        rest[:, 2:],
    )


def solution(mesh):
    in_specs = (
        P(("fsdp", "ctx", "tp"), None),
        P(None, "fsdp", None, "tp"),
        P(None, "tp", "fsdp"),
        P(None, "fsdp", "tp"),
        P(None, "tp", "fsdp"),
        P(None, None, "tp"),
        P(None, "tp"),
        P(),
        P(),
        P(),
        P(),
        P(("fsdp", "ctx", "tp"), None),
    )
    out_specs = (
        P(("fsdp", "ctx", "tp"), None),
        P(("fsdp", "ctx", "tp"), None),
        P(None, "fsdp", None, "tp"),
        P(None, "tp", "fsdp"),
        P(None, "fsdp", "tp"),
        P(None, "tp", "fsdp"),
        P(None, None, "tp"),
        P(None, "tp"),
        P(),
        P(),
    )
    return jax.shard_map(
        on_device, mesh=mesh, in_specs=in_specs, out_specs=out_specs, check_vma=False
    )
```

time: 956 us -> 791 us (0.83)
  waiting for transfers between devices: 482 us -> 360 us
  starting transfers between devices: 207 us -> 124 us
  Pallas kernels: 199 us -> 237 us
    ppermute x115 -> x37, waiting for transfers between devices: 390 us -> 181 us  [the longest x34 142 us: cross(): return lax.ppermute(values, ('ctx', 'tp'), pairs)]
    ppermute x115 -> x37, starting transfers between devices: 169 us -> 52.9 us  [the longest x34 46.2 us: cross(): return lax.ppermute(values, ('ctx', 'tp'), pairs)]
    ppermute x35 -> x37, waiting for transfers between devices: 91.8 us -> 172 us  [swap(): return lax.ppermute(values, axis, [(0, 1), (1, 0)])]
    all_to_all x0 -> x8, starting transfers between devices: none -> 40.3 us  [all_to_all(): return lax.all_to_all(values, 'ctx', 0, 0)]
    pallas_call x34 -> x56, Pallas kernels: 199 us -> 237 us  [the longest x42 191 us: kernel_call(): pl.pallas_call(ordered, in_specs=list(in_specs) + [pl.BlockSpec(memory_sp...]
    unnamed x345 -> x249, local copies, waits for them, and re-layouts: 14.7 us -> 40.9 us
    slice x6 -> x2, local copies, waits for them, and re-layouts: 11.2 us -> 1.24 us  [the longest x1 0.62 us: forward(): state = (k.middle, part2, swapped(part2), row(row_biases[layer, 3]))]
    ppermute x35 -> x37, starting transfers between devices: 37.8 us -> 31 us  [swap(): return lax.ppermute(values, axis, [(0, 1), (1, 0)])]
  transfers between devices with their start and end apart: 150 -> 82, of which waited for: 63 -> 30; matrix products, arithmetic and copies ran while one was open for 4% -> 2% of each run, Pallas kernels for 17% -> 24%
where the time goes in v2:
time: 791 us; the launch traced here: 781 us
  waiting for transfers between devices  360 us (46%)
  Pallas kernels  237 us (30%)
  starting transfers between devices  124 us (16%)
  local copies, waits for them, and re-layouts  48.5 us (6%)
  other arithmetic  8.21 us (1%)
    pallas_call x42, Pallas kernels, kernel_call(): pl.pallas_call(ordered, in_specs=list(in_specs) + [pl.BlockSpec(memory_sp...  191 us
    ppermute x37, waiting for transfers between devices, swap(): return lax.ppermute(values, axis, [(0, 1), (1, 0)])  172 us
    ppermute x34, waiting for transfers between devices, cross(): return lax.ppermute(values, ('ctx', 'tp'), pairs)  142 us
    ppermute x34, starting transfers between devices, cross(): return lax.ppermute(values, ('ctx', 'tp'), pairs)  46.2 us
    unnamed x249, local copies, waits for them, and re-layouts  40.9 us
    all_to_all x8, starting transfers between devices, all_to_all(): return lax.all_to_all(values, 'ctx', 0, 0)  40.3 us
    ppermute x3, waiting for transfers between devices, cross_all(): return lax.ppermute(values, 'ctx', [(i, i ^ 1 << step) for i in range(d.C)])  39 us
    ppermute x37, starting transfers between devices, swap(): return lax.ppermute(values, axis, [(0, 1), (1, 0)])  31 us
  transfers between devices with their start and end apart: 82, of which 30 were waited for; matrix products, arithmetic and copies ran while one was open for 2% of the time, Pallas kernels for 24%

profile of v2, /device:TPU:0, one launch (start us, length us, event | category | flops | bytes accessed | tf_op | source)
XLA Modules:
  0.0 780.7 jit_solution(4636408026302922975)
XLA Ops:
  13.9 11.7 %collective-permute-done.1.refs_5_.refs_2_ = bf16[3,256,512]{2,1,0:T(8,128)(2,1)S(1)} collective-permute-done((bf16[3,256,512]{2,1,0:T(8,128)(2,1)}, bf16[3,256,512]{2,1,0:T(8,128)(2,1)S(1)}, u32[]{:S(2)}, u32[]{:S(2)}) %collective-permute-start.1) | collective-permute-done | bytes 786464 | tf_op jit(solution)/shard_map/ppermute | solution.py:707
  35.8 5.8 collective-permute-done.4.refs_9_.refs_8_.refs_4_
  47.2 6.2 all-to-all-start
  63.3 27.6 %collective-permute-done.8.refs_6_.refs_14_.refs_16_.refs_9_.refs_11_ = bf16[2,512,512]{2,1,0:T(8,128)(2,1)S(1)} collective-permute-done((bf16[2,512,512]{2,1,0:T(8,128)(2,1)S(1)}, bf16[2,512,512]{2,1,0:T(8,128)(2,1)S(1)}, u32[]{:S(2)}, u32[]{:S(2)}) %collective-permute-start.8) | collective-permute-done | bytes 1048608 | tf_op jit(solution)/shard_map/ppermute | solution.py:707
  125.6 12.1 %ffn_forward.2 = (f32[256,1024]{1,0:T(8,128)}, bf16[256,512]{1,0:T(8,128)(2,1)}, bf16[3,256,512]{2,1,0:T(8,128)(2,1)}, bf16[2,256,512]{2,1,0:T(8,128)(2,1)}, bf1...) custom-call(s32[6]{0:T(128)} %stack.24.sc.refs_0_, f32[256,1024]{1,0:T(8,128)} %get-tuple-element.103.refs_0_.refs_1_.refs_3_, ...), custom_call_target="tpu_custom_call" | custom-call | flops 2147483648 | bytes 14000000 | tf_op jit(solution)/shard_map/ffn_forward/pallas_call | solution.py:51
  138.9 8.9 %collective-permute-done.17.refs_12_.refs_10_.refs_6_ = bf16[512,512]{1,0:T(8,128)(2,1)S(1)} collective-permute-done((bf16[512,512]{1,0:T(8,128)(2,1)S(1)}, bf16[512,512]{1,0:T(8,128)(2,1)S(1)}, u32[]{:S(2)}, u32[]{:S(2)}) %collective-permute-start.17) | collective-permute-done | bytes 524320 | tf_op jit(solution)/shard_map/ppermute | solution.py:707
  164.4 21.4 %collective-permute-done.20.refs_5_.refs_14_.refs_16_.refs_9_.refs_11_ = bf16[2,512,512]{2,1,0:T(8,128)(2,1)S(1)} collective-permute-done((bf16[2,512,512]{2,1,0:T(8,128)(2,1)S(1)}, bf16[2,512,512]{2,1,0:T(8,128)(2,1)S(1)}, u32[]{:S(2)}, u32[]{:S(2)}) %collective-permute-start.20) | collective-permute-done | bytes 1048608 | tf_op jit(solution)/shard_map/ppermute | solution.py:707
  197.4 5.6 all-to-all-start.3
  207.1 6.0 all-to-all-done.3.refs_4_
  221.5 12.0 %ffn_forward.3 = (f32[256,1024]{1,0:T(8,128)}, bf16[256,512]{1,0:T(8,128)(2,1)}, bf16[3,256,512]{2,1,0:T(8,128)(2,1)}, bf16[2,256,512]{2,1,0:T(8,128)(2,1)}, bf1...) custom-call(s32[6]{0:T(128)} %stack.24.sc.refs_0_, f32[256,1024]{1,0:T(8,128)} %get-tuple-element.108.refs_1_.refs_3_, ...), custom_call_target="tpu_custom_call" | custom-call | flops 2147483648 | bytes 14000000 | tf_op jit(solution)/shard_map/ffn_forward/pallas_call | solution.py:51
  237.1 10.3 %ffn_backward.2 = (bf16[256,512]{1,0:T(8,128)(2,1)}, bf16[2,256,512]{2,1,0:T(8,128)(2,1)}, bf16[3,256,512]{2,1,0:T(8,128)(2,1)}, f32[1,2048]{1,0:T(1,128)}, f32[...) custom-call(s32[6]{0:T(128)} %stack.24.sc.refs_0_, bf16[256,1024]{1,0:T(8,128)(2,1)} %maximum_select_fusion.1.refs_1_, ...), custom_call_target="tpu_custom_call" | custom-call | flops 2147483648 | bytes 14000000 | tf_op jit(solution)/shard_map/ffn_backward/pallas_call | solution.py:51
  258.6 20.1 %collective-permute-done.32.refs_5_ = bf16[2,256,512]{2,1,0:T(8,128)(2,1)S(1)} collective-permute-done((bf16[2,256,512]{2,1,0:T(8,128)(2,1)S(1)}, bf16[2,256,512]{2,1,0:T(8,128)(2,1)S(1)}, u32[]{:S(2)}, u32[]{:S(2)}) %collective-permute-start.32) | collective-permute-done | bytes 524320 | tf_op jit(solution)/shard_map/ppermute | solution.py:707
  280.5 8.9 %attend_backward.2.refs_11_ = bf16[8,640,128]{2,1,0:T(8,128)(2,1)} custom-call(s32[6]{0:T(128)} %stack.24.sc.refs_0_, f32[16,2048]{1,0:T(8,128)} %bitcast_add_fusion.refs_1_, bf16[8,640,128]{2,1,0:T(8,128)(2,1)} %all-to-all-done.2.refs_2_, bf16[8,128,128]{2,1,0:T(8,128)(2,1)} %copy-done.68, bf16[3,256,512]{2,1,0:T(8,128)(2,1)} %copy-done.95, ...), custom_call_target="tpu_custom_call" | custom-call | flops 2684354560 | bytes 4000000 | tf_op jit(solution)/shard_map/attend_backward/pallas_call | solution.py:51
  295.3 28.3 %collective-permute-done.33.refs_7_ = bf16[2,256,512]{2,1,0:T(8,128)(2,1)S(1)} collective-permute-done((bf16[2,256,512]{2,1,0:T(8,128)(2,1)S(1)}, bf16[2,256,512]{2,1,0:T(8,128)(2,1)S(1)}, u32[]{:S(2)}, u32[]{:S(2)}) %collective-permute-start.33) | collective-permute-done | bytes 524320 | tf_op jit(solution)/shard_map/ppermute | solution.py:707
  324.7 9.2 %weight_grad_ffn.2 = (bf16[4,8,64,512]{3,2,1,0:T(8,128)(2,1)}, bf16[4,8,64,512]{3,2,1,0:T(8,128)(2,1)}) custom-call(s32[6]{0:T(128)} %stack.24.sc.refs_0_, bf16[256,512]{1,0:T(8,128)(2,1)} %get-tuple-element.123.refs_1_, bf16[3,256,512]{2,1,0:T(8,128)(2,1)} %get-tuple-element.121.refs_2_, bf16[3,256,512]{2,1,0:T(8,128)(2,1)} %copy-done.95, ...), custom_call_target="tpu_custom_call" | custom-call | flops 2147483648 | bytes 8000000 | tf_op jit(solution)/shard_map/weight_grad_ffn/pallas_call | solution.py:51
  337.5 7.2 collective-permute-done.35.refs_6_.refs_2_
  359.3 10.5 %ffn_backward.3 = (bf16[256,512]{1,0:T(8,128)(2,1)}, bf16[2,256,512]{2,1,0:T(8,128)(2,1)}, bf16[3,256,512]{2,1,0:T(8,128)(2,1)}, f32[1,2048]{1,0:T(1,128)}, f32[...) custom-call(s32[6]{0:T(128)} %stack.24.sc.refs_0_, f32[256,1024]{1,0:T(8,128)} %get-tuple-element.131.refs_1_, ...), custom_call_target="tpu_custom_call" | custom-call | flops 2147483648 | bytes 14000000 | tf_op jit(solution)/shard_map/ffn_backward/pallas_call | solution.py:51
  378.4 7.1 collective-permute-done.41.refs_11_.refs_8_
  395.7 5.6 weight_grad_qkv.2
  405.7 8.9 %attend_backward.3.refs_15_ = bf16[8,640,128]{2,1,0:T(8,128)(2,1)} custom-call(s32[6]{0:T(128)} %stack.24.sc.refs_0_, f32[16,2048]{1,0:T(8,128)} %bitcast_add_fusion.refs_1_, bf16[8,640,128]{2,1,0:T(8,128)(2,1)} %all-to-all-done.refs_2_, bf16[8,128,128]{2,1,0:T(8,128)(2,1)} %copy-done.67, bf16[1,8,64,512]{3,2,1,0:T(8,128)(2,1)} %get-tuple-element.144.refs_4_.refs_0_, ...), custom_call_target="tpu_custom_call" | custom-call | flops 2684354560 | bytes 4000000 | tf_op jit(solution)/shard_map/attend_backward/pallas_call | solution.py:51
  414.7 6.1 all-to-all-start.7
  422.9 18.4 %collective-permute-done.44.refs_9_ = bf16[3,256,512]{2,1,0:T(8,128)(2,1)S(1)} collective-permute-done((bf16[3,256,512]{2,1,0:T(8,128)(2,1)S(1)}, bf16[3,256,512]{2,1,0:T(8,128)(2,1)S(1)}, u32[]{:S(2)}, u32[]{:S(2)}) %collective-permute-start.44) | collective-permute-done | bytes 786464 | tf_op jit(solution)/shard_map/ppermute | solution.py:707
  445.0 10.3 %weight_grad_ffn.3 = (bf16[4,9,64,512]{3,2,1,0:T(8,128)(2,1)}, bf16[4,9,64,512]{3,2,1,0:T(8,128)(2,1)}) custom-call(s32[6]{0:T(128)} %stack.24.sc.refs_0_, bf16[256,512]{1,0:T(8,128)(2,1)} %get-tuple-element.146.refs_1_, bf16[3,256,512]{2,1,0:T(8,128)(2,1)} %get-tuple-element.111.refs_2_, bf16[3,256,512]{2,1,0:T(8,128)(2,1)} %collective-permute-done.22.refs_5_.refs_3_, ...), custom_call_target="tpu_custom_call" | custom-call | flops 2415919104 | bytes 8000000 | tf_op jit(solution)/shard_map/weight_grad_ffn/pallas_call | solution.py:51
  474.3 26.8 %collective-permute-done.50.refs_1_ = bf16[4,4,64,512]{3,2,1,0:T(8,128)(2,1)S(1)} collective-permute-done((bf16[4,4,64,512]{3,2,1,0:T(8,128)(2,1)S(1)}, bf16[4,4,64,512]{3,2,1,0:T(8,128)(2,1)S(1)}, u32[]{:S(2)}, u32[]{:S(2)}) %collective-permute-start.50) | collective-permute-done | bytes 1048608 | tf_op jit(solution)/shard_map/ppermute | solution.py:722
  525.1 29.5 %collective-permute-done.53.refs_1_ = bf16[2,4,64,512]{3,2,1,0:T(8,128)(2,1)S(1)} collective-permute-done((bf16[2,4,64,512]{3,2,1,0:T(8,128)(2,1)S(1)}, bf16[2,4,64,512]{3,2,1,0:T(8,128)(2,1)S(1)}, u32[]{:S(2)}, u32[]{:S(2)}) %collective-permute-start.53) | collective-permute-done | bytes 524320 | tf_op jit(solution)/shard_map/ppermute | solution.py:722
  577.8 28.8 %collective-permute-done.55.refs_1_ = bf16[1,4,64,512]{3,2,1,0:T(8,128)(2,1)S(1)} collective-permute-done((bf16[1,4,64,512]{3,2,1,0:T(8,128)(2,1)S(1)}, bf16[1,4,64,512]{3,2,1,0:T(8,128)(2,1)S(1)}, u32[]{:S(2)}, u32[]{:S(2)}) %collective-permute-start.55) | collective-permute-done | bytes 262176 | tf_op jit(solution)/shard_map/ppermute | solution.py:722
  636.4 33.2 %collective-permute-done.67 = f32[144,128]{1,0:T(8,128)S(1)} collective-permute-done((f32[144,128]{1,0:T(8,128)S(1)}, f32[144,128]{1,0:T(8,128)S(1)}, u32[]{:S(2)}, u32[]{:S(2)}) %collective-permute-start.67) | collective-permute-done | bytes 73760 | tf_op jit(solution)/shard_map/ppermute | solution.py:726
  681.3 14.7 %collective-permute-done.65.refs_1_ = bf16[1,3,64,512]{3,2,1,0:T(8,128)(2,1)S(1)} collective-permute-done((bf16[1,3,64,512]{3,2,1,0:T(8,128)(2,1)S(1)}, bf16[1,3,64,512]{3,2,1,0:T(8,128)(2,1)S(1)}, u32[]{:S(2)}, u32[]{:S(2)}) %collective-permute-start.65) | collective-permute-done | bytes 196640 | tf_op jit(solution)/shard_map/ppermute | solution.py:722
  708.1 9.4 %collective-permute-done.68.refs_2_ = bf16[2,3,64,512]{3,2,1,0:T(8,128)(2,1)S(1)} collective-permute-done((bf16[2,3,64,512]{3,2,1,0:T(8,128)(2,1)S(1)}, bf16[2,3,64,512]{3,2,1,0:T(8,128)(2,1)S(1)}, u32[]{:S(2)}, u32[]{:S(2)}) %collective-permute-start.68) | collective-permute-done | bytes 393248 | tf_op jit(solution)/shard_map/ppermute | solution.py:722
  728.0 27.1 %collective-permute-done.72.refs_3_ = bf16[4,8,64,512]{3,2,1,0:T(8,128)(2,1)} collective-permute-done((bf16[4,8,64,512]{3,2,1,0:T(8,128)(2,1)S(1)}, bf16[4,8,64,512]{3,2,1,0:T(8,128)(2,1)}, u32[]{:S(2)}, u32[]{:S(2)}) %collective-permute-start.72) | collective-permute-done | bytes 2097184 | tf_op jit(solution)/shard_map/ppermute | solution.py:722
  755.0 6.2 place_ffn.2
  770.2 6.7 place_ffn.3
  (467 shorter events, 327.7 us)
Async XLA Ops:
  47.2 46.5 %all-to-all-start = ((bf16[8,640,128]{2,1,0:T(8,128)(2,1)}), bf16[8,640,128]{2,1,0:T(8,128)(2,1)}, u32[]{:S(2)}, u32[]{:S(2)}) async-start(bf16[8,640,128]{2,1,0:T(8,128)(2,1)} %get-tuple-element.104), calls=%async_computation | async-start | bytes 2621440 | tf_op jit(solution)/shard_map/all_to_all | solution.py:820
  53.4 39.6 %collective-permute-start.7 = (bf16[512,512]{1,0:T(8,128)(2,1)}, bf16[512,512]{1,0:T(8,128)(2,1)S(1)}, u32[]{:S(2)}, u32[]{:S(2)}) collective-permute-start(bf16[512,512]{1,0:T(8,128)(2,1)} %take.13.refs_0_), channel_id=1, source_target_pairs={{0,16},{16,0},{1,17},{17,1},{2,18},{18,2},{3,19},{19,3},{4,20},{20... | collective-permute-start | bytes 1572872 | tf_op jit(solution)/shard_map/ppermute | solution.py:707
  54.9 36.1 %collective-permute-start.8 = (bf16[2,512,512]{2,1,0:T(8,128)(2,1)S(1)}, bf16[2,512,512]{2,1,0:T(8,128)(2,1)S(1)}, u32[]{:S(2)}, u32[]{:S(2)}) collective-permute-start(bf16[2,512,512]{2,1,0:T(8,128)(2,1)S(1)} %copy-done.21), channel_id=1, source_target_pairs={{0,16},{16,0},{1,17},{17,1},{2,18},{18,2},{3,19},{19,3},{4,20},{20... | collective-permute-start | bytes 3145736 | tf_op jit(solution)/shard_map/ppermute | solution.py:707
  56.2 37.5 %collective-permute-start.6 = (bf16[512,512]{1,0:T(8,128)(2,1)}, bf16[512,512]{1,0:T(8,128)(2,1)}, u32[]{:S(2)}, u32[]{:S(2)}) collective-permute-start(bf16[512,512]{1,0:T(8,128)(2,1)} %collective-permute-done.4.refs_9_.refs_8_.refs_4_), channel_id=1, source_target_pairs={{0,2},{1,5},{2,0},{3,7},{4,6},{5,1},{6,4},{7,3},{8,10},{9,13},{10,... | collective-permute-start | bytes 1572872 | tf_op jit(solution)/shard_map/ppermute | solution.py:722
  58.3 34.7 %collective-permute-start.5 = (bf16[256,512]{1,0:T(8,128)(2,1)}, bf16[256,512]{1,0:T(8,128)(2,1)S(1)}, u32[]{:S(2)}, u32[]{:S(2)}) collective-permute-start(bf16[256,512]{1,0:T(8,128)(2,1)} %collective-permute-done.3.refs_8_.refs_2_.refs_7_), channel_id=1, source_target_pairs={{0,2},{1,5},{2,0},{3,7},{4,6},{5,1},{6,4},{7,3},{8,10},{9,13},{10,... | collective-permute-start | bytes 786440 | tf_op jit(solution)/shard_map/ppermute | solution.py:722
  61.1 57.2 %collective-permute-start.9 = (bf16[3,256,512]{2,1,0:T(8,128)(2,1)}, bf16[3,256,512]{2,1,0:T(8,128)(2,1)S(1)}, u32[]{:S(2)}, u32[]{:S(2)}) collective-permute-start(bf16[3,256,512]{2,1,0:T(8,128)(2,1)} %take.15.refs_0_), channel_id=1, source_target_pairs={{0,16},{16,0},{1,17},{17,1},{2,18},{18,2},{3,19},{19,3},{4,20},{20... | collective-permute-start | bytes 2359304 | tf_op jit(solution)/shard_map/ppermute | solution.py:707
  91.0 33.5 %collective-permute-start.13 = (bf16[2,512,512]{2,1,0:T(8,128)(2,1)S(1)}, bf16[2,512,512]{2,1,0:T(8,128)(2,1)S(1)}, u32[]{:S(2)}, u32[]{:S(2)}) collective-permute-start(bf16[2,512,512]{2,1,0:T(8,128)(2,1)S(1)} %collective-permute-done.8.refs_6_.refs_14_.refs_16_.refs_9_.refs_11_), channel_id=1, source_target_pairs={{0,2},{1,5},{2,0},{3,7},{4,6},{5,1},{6,4},{7,3},{8,10},{9,13},{10,... | collective-permute-start | bytes 3145736 | tf_op jit(solution)/shard_map/ppermute | solution.py:722
  154.3 37.7 %all-to-all-start.2 = ((bf16[8,640,128]{2,1,0:T(8,128)(2,1)}), bf16[8,640,128]{2,1,0:T(8,128)(2,1)}, u32[]{:S(2)}, u32[]{:S(2)}) async-start(bf16[8,640,128]{2,1,0:T(8,128)(2,1)} %get-tuple-element.109), calls=%async_computation.2 | async-start | bytes 2621440 | tf_op jit(solution)/shard_map/all_to_all | solution.py:820
  163.9 43.2 %collective-permute-start.22 = (bf16[3,256,512]{2,1,0:T(8,128)(2,1)}, bf16[3,256,512]{2,1,0:T(8,128)(2,1)}, u32[]{:S(2)}, u32[]{:S(2)}) collective-permute-start(bf16[3,256,512]{2,1,0:T(8,128)(2,1)} %get-tuple-element.111.refs_2_), channel_id=1, source_target_pairs={{0,16},{16,0},{1,17},{17,1},{2,18},{18,2},{3,19},{19,3},{4,20},{20... | collective-permute-start | bytes 2359304 | tf_op jit(solution)/shard_map/ppermute | solution.py:707
  185.8 34.3 %collective-permute-start.25 = (bf16[2,512,512]{2,1,0:T(8,128)(2,1)S(1)}, bf16[2,512,512]{2,1,0:T(8,128)(2,1)S(1)}, u32[]{:S(2)}, u32[]{:S(2)}) collective-permute-start(bf16[2,512,512]{2,1,0:T(8,128)(2,1)S(1)} %collective-permute-done.20.refs_5_.refs_14_.refs_16_.refs_9_.refs_11_), channel_id=1, source_target_pairs={{0,2},{1,5},{2,0},{3,7},{4,6},{5,1},{6,4},{7,3},{8,10},{9,13},{10,... | collective-permute-start | bytes 3145736 | tf_op jit(solution)/shard_map/ppermute | solution.py:722
  289.5 58.1 %all-to-all-start.5 = ((bf16[8,640,128]{2,1,0:T(8,128)(2,1)}), bf16[8,640,128]{2,1,0:T(8,128)(2,1)S(1)}, u32[]{:S(2)}, u32[]{:S(2)}) async-start(bf16[8,640,128]{2,1,0:T(8,128)(2,1)} %attend_backward.2.refs_11_), calls=%async_computation.5 | async-start | bytes 2621440 | tf_op jit(solution)/shard_map/all_to_all | solution.py:820
  333.9 35.9 %collective-permute-start.39 = (bf16[4,8,64,512]{3,2,1,0:T(8,128)(2,1)}, bf16[4,8,64,512]{3,2,1,0:T(8,128)(2,1)S(1)}, u32[]{:S(2)}, u32[]{:S(2)}) collective-permute-start(bf16[4,8,64,512]{3,2,1,0:T(8,128)(2,1)} %get-tuple-element.134), channel_id=1, source_target_pairs={{0,2},{1,5},{2,0},{3,7},{4,6},{5,1},{6,4},{7,3},{8,10},{9,13},{10,... | collective-permute-start | bytes 6291464 | tf_op jit(solution)/shard_map/ppermute | solution.py:722
  414.7 40.6 %all-to-all-start.7 = ((bf16[8,640,128]{2,1,0:T(8,128)(2,1)}), bf16[8,640,128]{2,1,0:T(8,128)(2,1)S(1)}, u32[]{:S(2)}, u32[]{:S(2)}) async-start(bf16[8,640,128]{2,1,0:T(8,128)(2,1)} %attend_backward.3.refs_15_), calls=%async_computation.7 | async-start | bytes 2621440 | tf_op jit(solution)/shard_map/all_to_all | solution.py:820
  460.8 47.5 %collective-permute-start.48 = (bf16[4,9,64,512]{3,2,1,0:T(8,128)(2,1)}, bf16[4,9,64,512]{3,2,1,0:T(8,128)(2,1)S(1)}, u32[]{:S(2)}, u32[]{:S(2)}) collective-permute-start(bf16[4,9,64,512]{3,2,1,0:T(8,128)(2,1)} %get-tuple-element.156), channel_id=1, source_target_pairs={{0,2},{1,5},{2,0},{3,7},{4,6},{5,1},{6,4},{7,3},{8,10},{9,13},{10,... | collective-permute-start | bytes 7077896 | tf_op jit(solution)/shard_map/ppermute | solution.py:722
  462.6 38.6 %collective-permute-start.50 = (bf16[4,4,64,512]{3,2,1,0:T(8,128)(2,1)S(1)}, bf16[4,4,64,512]{3,2,1,0:T(8,128)(2,1)S(1)}, u32[]{:S(2)}, u32[]{:S(2)}) collective-permute-start(bf16[4,4,64,512]{3,2,1,0:T(8,128)(2,1)S(1)} %copy-done.91), channel_id=1, source_target_pairs={{0,2},{1,5},{2,0},{3,7},{4,6},{5,1},{6,4},{7,3},{8,10},{9,13},{10,... | collective-permute-start | bytes 3145736 | tf_op jit(solution)/shard_map/ppermute | solution.py:722
  462.9 41.9 %collective-permute-start.49 = (bf16[1,8,64,512]{3,2,1,0:T(8,128)(2,1)S(1)}, bf16[1,8,64,512]{3,2,1,0:T(8,128)(2,1)S(1)}, u32[]{:S(2)}, u32[]{:S(2)}) collective-permute-start(bf16[1,8,64,512]{3,2,1,0:T(8,128)(2,1)S(1)} %copy-done.100), channel_id=1, source_target_pairs={{0,8},{1,9},{2,10},{3,11},{4,12},{5,13},{6,14},{7,15},{8,0},{9,1},... | collective-permute-start | bytes 1572872 | tf_op jit(solution)/shard_map/ppermute | solution.py:722
  465.5 50.0 %collective-permute-start.47 = (bf16[3,256,512]{2,1,0:T(8,128)(2,1)}, bf16[3,256,512]{2,1,0:T(8,128)(2,1)S(1)}, u32[]{:S(2)}, u32[]{:S(2)}) collective-permute-start(bf16[3,256,512]{2,1,0:T(8,128)(2,1)} %get-tuple-element.155.refs_3_), channel_id=1, source_target_pairs={{0,16},{16,0},{1,17},{17,1},{2,18},{18,2},{3,19},{19,3},{4,20},{20... | collective-permute-start | bytes 2359304 | tf_op jit(solution)/shard_map/ppermute | solution.py:707
  472.8 34.9 %collective-permute-start.51 = (f32[144,128]{1,0:T(8,128)S(1)}, f32[144,128]{1,0:T(8,128)S(1)}, u32[]{:S(2)}, u32[]{:S(2)}) collective-permute-start(f32[144,128]{1,0:T(8,128)S(1)} %bitcast.75), channel_id=1, source_target_pairs={{0,16},{16,0},{1,17},{17,1},{2,18},{18,2},{3,19},{19,3},{4,20},{20... | collective-permute-start | bytes 221192 | tf_op jit(solution)/shard_map/ppermute | solution.py:707
  513.8 47.0 %collective-permute-start.57 = (bf16[2,9,64,512]{3,2,1,0:T(8,128)(2,1)}, bf16[2,9,64,512]{3,2,1,0:T(8,128)(2,1)S(1)}, u32[]{:S(2)}, u32[]{:S(2)}) collective-permute-start(bf16[2,9,64,512]{3,2,1,0:T(8,128)(2,1)} %get-tuple-element.184), channel_id=1, source_target_pairs={{0,4},{1,3},{2,6},{3,1},{4,0},{5,7},{6,2},{7,5},{8,12},{9,11},{10,... | collective-permute-start | bytes 3538952 | tf_op jit(solution)/shard_map/ppermute | solution.py:722
  520.7 36.8 %collective-permute-start.52 = (bf16[4,3,64,512]{3,2,1,0:T(8,128)(2,1)}, bf16[4,3,64,512]{3,2,1,0:T(8,128)(2,1)S(1)}, u32[]{:S(2)}, u32[]{:S(2)}) collective-permute-start(bf16[4,3,64,512]{3,2,1,0:T(8,128)(2,1)} %get-tuple-element.178), channel_id=1, source_target_pairs={{0,2},{1,5},{2,0},{3,7},{4,6},{5,1},{6,4},{7,3},{8,10},{9,13},{10,... | collective-permute-start | bytes 2359304 | tf_op jit(solution)/shard_map/ppermute | solution.py:722
  522.7 41.8 %collective-permute-start.56 = (bf16[1,8,64,512]{3,2,1,0:T(8,128)(2,1)S(1)}, bf16[1,8,64,512]{3,2,1,0:T(8,128)(2,1)S(1)}, u32[]{:S(2)}, u32[]{:S(2)}) collective-permute-start(bf16[1,8,64,512]{3,2,1,0:T(8,128)(2,1)S(1)} %copy-done.4), channel_id=1, source_target_pairs={{0,8},{1,9},{2,10},{3,11},{4,12},{5,13},{6,14},{7,15},{8,0},{9,1},... | collective-permute-start | bytes 1572872 | tf_op jit(solution)/shard_map/ppermute | solution.py:722
  567.6 52.6 %collective-permute-start.61 = (bf16[2,8,64,512]{3,2,1,0:T(8,128)(2,1)}, bf16[2,8,64,512]{3,2,1,0:T(8,128)(2,1)S(1)}, u32[]{:S(2)}, u32[]{:S(2)}) collective-permute-start(bf16[2,8,64,512]{3,2,1,0:T(8,128)(2,1)} %join.8.refs_2_), channel_id=1, source_target_pairs={{0,4},{1,3},{2,6},{3,1},{4,0},{5,7},{6,2},{7,5},{8,12},{9,11},{10,... | collective-permute-start | bytes 3145736 | tf_op jit(solution)/shard_map/ppermute | solution.py:722
  567.7 59.2 %collective-permute-start.63 = (bf16[1,9,64,512]{3,2,1,0:T(8,128)(2,1)S(1)}, bf16[1,9,64,512]{3,2,1,0:T(8,128)(2,1)S(1)}, u32[]{:S(2)}, u32[]{:S(2)}) collective-permute-start(bf16[1,9,64,512]{3,2,1,0:T(8,128)(2,1)S(1)} %copy-done.98), channel_id=1, source_target_pairs={{0,8},{1,9},{2,10},{3,11},{4,12},{5,13},{6,14},{7,15},{8,0},{9,1},... | collective-permute-start | bytes 1769480 | tf_op jit(solution)/shard_map/ppermute | solution.py:722
  574.1 43.5 %collective-permute-start.54 = (bf16[2,3,64,512]{3,2,1,0:T(8,128)(2,1)S(1)}, bf16[2,3,64,512]{3,2,1,0:T(8,128)(2,1)S(1)}, u32[]{:S(2)}, u32[]{:S(2)}) collective-permute-start(bf16[2,3,64,512]{3,2,1,0:T(8,128)(2,1)S(1)} %copy-done.107), channel_id=1, source_target_pairs={{0,4},{1,3},{2,6},{3,1},{4,0},{5,7},{6,2},{7,5},{8,12},{9,11},{10,... | collective-permute-start | bytes 1179656 | tf_op jit(solution)/shard_map/ppermute | solution.py:722
  629.9 45.9 %collective-permute-start.66 = (bf16[1,9,64,512]{3,2,1,0:T(8,128)(2,1)}, bf16[1,9,64,512]{3,2,1,0:T(8,128)(2,1)S(1)}, u32[]{:S(2)}, u32[]{:S(2)}) collective-permute-start(bf16[1,9,64,512]{3,2,1,0:T(8,128)(2,1)} %fold.22.refs_3_.refs_0_), channel_id=1, source_target_pairs={{0,8},{1,9},{2,10},{3,11},{4,12},{5,13},{6,14},{7,15},{8,0},{9,1},... | collective-permute-start | bytes 1769480 | tf_op jit(solution)/shard_map/ppermute | solution.py:722
  633.4 36.9 %collective-permute-start.62 = (bf16[2,4,64,512]{3,2,1,0:T(8,128)(2,1)S(1)}, bf16[2,4,64,512]{3,2,1,0:T(8,128)(2,1)S(1)}, u32[]{:S(2)}, u32[]{:S(2)}) collective-permute-start(bf16[2,4,64,512]{3,2,1,0:T(8,128)(2,1)S(1)} %copy-done.35), channel_id=1, source_target_pairs={{0,4},{1,3},{2,6},{3,1},{4,0},{5,7},{6,2},{7,5},{8,12},{9,11},{10,... | collective-permute-start | bytes 1572872 | tf_op jit(solution)/shard_map/ppermute | solution.py:722
  633.5 39.9 %collective-permute-start.59 = (bf16[1,3,64,512]{3,2,1,0:T(8,128)(2,1)S(1)}, bf16[1,3,64,512]{3,2,1,0:T(8,128)(2,1)S(1)}, u32[]{:S(2)}, u32[]{:S(2)}) collective-permute-start(bf16[1,3,64,512]{3,2,1,0:T(8,128)(2,1)S(1)} %copy-done.114), channel_id=1, source_target_pairs={{0,8},{1,9},{2,10},{3,11},{4,12},{5,13},{6,14},{7,15},{8,0},{9,1},... | collective-permute-start | bytes 589832 | tf_op jit(solution)/shard_map/ppermute | solution.py:722
  635.2 34.5 %collective-permute-start.67 = (f32[144,128]{1,0:T(8,128)S(1)}, f32[144,128]{1,0:T(8,128)S(1)}, u32[]{:S(2)}, u32[]{:S(2)}) collective-permute-start(f32[144,128]{1,0:T(8,128)S(1)} %copy-done.51), channel_id=1, source_target_pairs={{0,8},{2,10},{4,12},{6,14},{8,0},{10,2},{12,4},{14,6},{1,9},{3,11}... | collective-permute-start | bytes 221192 | tf_op jit(solution)/shard_map/ppermute | solution.py:726
  703.4 66.7 %collective-permute-start.73 = (bf16[4,9,64,512]{3,2,1,0:T(8,128)(2,1)}, bf16[4,9,64,512]{3,2,1,0:T(8,128)(2,1)}, u32[]{:S(2)}, u32[]{:S(2)}) collective-permute-start(bf16[4,9,64,512]{3,2,1,0:T(8,128)(2,1)} %join.14.refs_3_), channel_id=1, source_target_pairs={{0,2},{1,5},{2,0},{3,7},{4,6},{5,1},{6,4},{7,3},{8,10},{9,13},{10,... | collective-permute-start | bytes 7077896 | tf_op jit(solution)/shard_map/ppermute | solution.py:722
  704.5 50.5 %collective-permute-start.72 = (bf16[4,8,64,512]{3,2,1,0:T(8,128)(2,1)S(1)}, bf16[4,8,64,512]{3,2,1,0:T(8,128)(2,1)}, u32[]{:S(2)}, u32[]{:S(2)}) collective-permute-start(bf16[4,8,64,512]{3,2,1,0:T(8,128)(2,1)S(1)} %copy-done.5), channel_id=1, source_target_pairs={{0,2},{1,5},{2,0},{3,7},{4,6},{5,1},{6,4},{7,3},{8,10},{9,13},{10,... | collective-permute-start | bytes 6291464 | tf_op jit(solution)/shard_map/ppermute | solution.py:722
  707.0 59.3 %collective-permute-start.71 = (bf16[4,4,64,512]{3,2,1,0:T(8,128)(2,1)S(1)}, bf16[4,4,64,512]{3,2,1,0:T(8,128)(2,1)}, u32[]{:S(2)}, u32[]{:S(2)}) collective-permute-start(bf16[4,4,64,512]{3,2,1,0:T(8,128)(2,1)S(1)} %copy-done.20), channel_id=1, source_target_pairs={{0,2},{1,5},{2,0},{3,7},{4,6},{5,1},{6,4},{7,3},{8,10},{9,13},{10,... | collective-permute-start | bytes 3145736 | tf_op jit(solution)/shard_map/ppermute | solution.py:722
  720.4 56.4 %collective-permute-start.70 = (bf16[4,3,64,512]{3,2,1,0:T(8,128)(2,1)}, bf16[4,3,64,512]{3,2,1,0:T(8,128)(2,1)}, u32[]{:S(2)}, u32[]{:S(2)}) collective-permute-start(bf16[4,3,64,512]{3,2,1,0:T(8,128)(2,1)} %join.15.refs_4_.refs_7_), channel_id=1, source_target_pairs={{0,2},{1,5},{2,0},{3,7},{4,6},{5,1},{6,4},{7,3},{8,10},{9,13},{10,... | collective-permute-start | bytes 2359304 | tf_op jit(solution)/shard_map/ppermute | solution.py:722
  (166 other events, 1501.2 us)

commit v3 on v2

--- a/solution.py
+++ b/solution.py
@@ -342,10 +342,7 @@
 def ffn_specs(d, layer):
     u = pl.BlockSpec((None, d.H, FT), lambda f: (layer, 0, f))
     w = pl.BlockSpec((None, FT, d.H), lambda f: (layer, f, 0))
-    tile = whole((d.H, FT))
-    low = pl.BlockSpec((None, FT, d.H), lambda f: (0, 0, 0))
-    high = pl.BlockSpec((None, FT, d.H), lambda f: (1, 0, 0))
-    return [u] + [tile] * 4, [w, low, low, high, high]
+    return [u] + [whole((d.H, FT))] * 4, [w] + [whole((FT, d.H))] * 4
 
 
 def ffn_forward(d, layer, sc, hid, pa, pb, bias, gain, shift,
@@ -581,81 +578,92 @@
     return out
 
 
-def wgrad_body(d, tiles, sc, *refs):
+EXTRA = 16
+
+
+def shift_at(d, mix):
+    return SHIFT if mix else SHIFT + d.bits
+
+
+def wgrad_body(d, tiles, mix, flat, sc, *refs):
     ins = refs[:-2]
     keep, send = refs[-2:]
     c = sc[2]
-    shifts = [sc[SHIFT + k] for k in range(d.bits)]
+    shifts = [sc[shift_at(d, mix) + k] for k in range(d.bits)]
     rb = FT // d.C
     spots = [spot_bits(lax.bitwise_xor(c, b), shifts, d.bits) for b in range(d.C)]
 
     def pick(item):
         ref, at = item
         return ins[ref][...] if at is None else ins[ref][at]
+
+    def put(spot, low, piece):
+        @pl.when(spot < d.C // 2)
+        def _():
+            keep[spot, low : low + piece.shape[0]] = piece
+
+        @pl.when(spot >= d.C // 2)
+        def _():
+            send[spot - d.C // 2, low : low + piece.shape[0]] = piece
 
     for m, (a, b, a2, b2) in enumerate(tiles):
         total = mm(pick(a), pick(b), TN) + mm(pick(a2), pick(b2), TN)
         total = total.astype(BF)
         for block, spot in enumerate(spots):
-            piece = total[block * rb : (block + 1) * rb, :]
-
-            @pl.when(spot < d.C // 2)
-            def _():
-                keep[spot, m] = piece
-
-            @pl.when(spot >= d.C // 2)
-            def _():
-                send[spot - d.C // 2, m] = piece
-
-
-def wgrad_plain_body(tiles, *refs):
-    ins, out = refs[:-1], refs[-1]
-
-    def pick(item):
-        ref, at = item
-        return ins[ref][...] if at is None else ins[ref][at]
-
-    for m, (a, b, a2, b2) in enumerate(tiles):
-        total = mm(pick(a), pick(b), TN) + mm(pick(a2), pick(b2), TN)
-        out[m] = total.astype(BF)
-
-
-def weight_grad_plain(d, name, ins, tiles, deps=()):
+            put(spot, m * rb, total[block * rb : (block + 1) * rb, :])
+    if flat is not None:
+        for block, spot in enumerate(spots):
+            put(spot, len(tiles) * rb, ins[flat][block].astype(BF))
+
+
+def weight_grad(d, name, sc, ins, tiles, mix, flat=None, deps=()):
+    rows = len(tiles) * (FT // d.C)
+    if flat is not None:
+        ins = (*ins, flat)
+        rows += EXTRA
     return kernel_call(
-        functools.partial(wgrad_plain_body, tiles), ins,
-        [VSPEC] * len(ins), VSPEC, sds((len(tiles), FT, FT), BF), "weight_grad_" + name,
+        functools.partial(wgrad_body, d, tiles, mix, None if flat is None else len(ins) - 1),
+        (sc, *ins),
+        [SSPEC] + [VSPEC] * len(ins),
+        [VSPEC] * 2,
+        [sds((d.C // 2, rows, FT), BF)] * 2,
+        "weight_grad_" + name,
         deps=deps, work=cost(4 * d.T * len(tiles) * FT * FT, 8e6))
 
 
-def weight_grad(d, name, sc, ins, tiles, deps=()):
-    shape = (d.C // 2, len(tiles), FT // d.C, FT)
-    return kernel_call(
-        functools.partial(wgrad_body, d, tiles),
-        (sc, *ins,),
-        in_specs=[SSPEC] + [VSPEC] * len(ins),
-        out_specs=[VSPEC] * 2,
-        out_shape=[sds(shape, BF)] * 2,
-        work=cost(4 * d.T * len(tiles) * FT * FT, 8e6),
-        name="weight_grad_" + name,
-        deps=deps,
-    )
-
-
-def place_body(d, wide, count_in, extra, layer, owner, plain, sc, *refs):
+def small_rows(d):
+    return (2, 1, 2, 4), (d.W // FT, d.F // FT, d.D // FT, d.D // FT)
+
+
+def place_body(d, wide, count_in, extra, layer, owner, flat, sc, *refs):
     ins = refs[:count_in]
-    outs = refs[count_in + extra : -2]
-    buf, sems = refs[-2:]
+    outs = refs[count_in + extra : -3]
+    buf, small, sems = refs[-3:]
     rb = FT // d.C
-    if plain:
-        buf[...] = ins[0][...].astype(F32)
-    else:
-        r = 0
-        for part in ins:
-            for n in range(part.shape[0]):
-                row = pl.multiple_of(owner(sc, r) * rb, rb)
-                for m in range(part.shape[1]):
-                    buf[m, pl.ds(row, rb), :] = part[n, m].astype(F32)
-                r += 1
+    nt = buf.shape[0]
+    r = 0
+    for part in ins:
+        for n in range(part.shape[0]):
+            block = owner(sc, r)
+            row = pl.multiple_of(block * rb, rb)
+            for m in range(nt):
+                buf[m, pl.ds(row, rb), :] = part[n, m * rb : (m + 1) * rb].astype(F32)
+            if flat:
+                small[block] = part[n, nt * rb :].astype(F32)
+            r += 1
+    if flat:
+        at = 0
+        for k in range(LAYERS):
+            for out, rows, pieces in zip(outs[len(wide) :], *small_rows(d)):
+                for row in range(rows):
+                    for piece in range(pieces):
+                        line = small[at // EXTRA, at % EXTRA : at % EXTRA + 1, :]
+                        lanes = slice(piece * FT, (piece + 1) * FT)
+                        if rows == 1:
+                            out[k : k + 1, lanes] = line
+                        else:
+                            out[k, row : row + 1, lanes] = line
+                        at += 1
     copies = []
     m = 0
     for out, (kind, count) in zip(outs, wide):
@@ -672,31 +680,42 @@
         one.wait()
 
 
-def place(d, layer, sc, parts, before, wide, name, deps=()):
-    plain = not isinstance(parts, list)
-    parts = [parts] if plain else parts
-    nt = parts[0].shape[0 if plain else 1]
+def place(d, layer, sc, unit, before, wide, name, deps=()):
+    parts = unit.finish()
+    nt = sum(n for _, n in wide)
+    flat = parts[0].shape[1] > nt * (FT // d.C)
     extra = tuple(before or ()) + tuple(deps)
     alias = {1 + len(parts) + k: k for k in range(len(before or ()))}
     shapes = [
         sds((LAYERS, FT, n * FT) if kind == "cols" else (LAYERS, n, FT, FT), F32)
         for kind, n in wide
     ]
+    specs = [pl.BlockSpec(memory_space=pl.ANY)] * len(wide)
+    if flat:
+        for rows, pieces in zip(*small_rows(d)):
+            one = (rows, pieces * FT) if rows > 1 else (pieces * FT,)
+            shapes.append(sds((LAYERS, *one), F32))
+            specs.append(VSPEC)
     moves = sum(n if kind == "cols" else 1 for kind, n in wide)
+    at = shift_at(d, unit.mix)
 
     def owner(scalars, r):
         turned = 0
         for k in range(d.bits):
             if r >> (d.bits - 1 - k) & 1:
-                turned = turned + lax.shift_left(jnp.int32(1), scalars[SHIFT + k])
+                turned = turned + lax.shift_left(jnp.int32(1), scalars[at + k])
         return lax.bitwise_xor(scalars[2], jnp.int32(turned))
 
     return pl.pallas_call(
-        functools.partial(place_body, d, wide, len(parts), len(extra), layer, owner, plain),
+        functools.partial(place_body, d, wide, len(parts), len(extra), layer, owner, flat),
         in_specs=[SSPEC] + [VSPEC] * len(parts) + [pl.BlockSpec(memory_space=pl.ANY)] * len(extra),
-        out_specs=[pl.BlockSpec(memory_space=pl.ANY)] * len(wide),
+        out_specs=specs,
         out_shape=shapes,
-        scratch_shapes=[pltpu.VMEM((nt, FT, FT), F32), pltpu.SemaphoreType.DMA((moves,))],
+        scratch_shapes=[
+            pltpu.VMEM((nt, FT, FT), F32),
+            pltpu.VMEM((d.C, EXTRA, FT), F32),
+            pltpu.SemaphoreType.DMA((moves,)),
+        ],
         input_output_aliases=alias,
         compiler_params=pltpu.CompilerParams(vmem_limit_bytes=VLIM),
         name="place_" + name,
@@ -707,23 +726,19 @@
     return lax.ppermute(values, axis, [(0, 1), (1, 0)])
 
 
-def way(d, core, step):
-    if step < 2 and d.bits > 1:
+def way(d, core, step, mix=True):
+    if mix and step < 2 and d.bits > 1:
         return step if core == 0 else 1 - step
     return step
 
 
-def cross(d, values, step):
+def cross(d, values, step, mix=True):
     pairs = []
     for i in range(d.C):
         for core in range(d.tp):
-            to = i ^ (1 << way(d, core, step))
+            to = i ^ (1 << way(d, core, step, mix))
             pairs.append((i * d.tp + core, to * d.tp + core))
     return lax.ppermute(values, ("ctx", "tp"), pairs)
-
-
-def cross_all(d, values, step):
-    return lax.ppermute(values, "ctx", [(i, i ^ (1 << step)) for i in range(d.C)])
 
 
 def take_body(sc, w, *refs):
@@ -783,10 +798,10 @@
 
 
 class Sum:
-    def __init__(self, d, keep, send):
-        self.d = d
+    def __init__(self, d, mix, keep, send):
+        self.d, self.mix = d, mix
         self.keep = keep
-        self.got = cross(d, send, 0)
+        self.got = cross(d, send, 0, mix)
         self.at = 0
         self.parts = None
 
@@ -796,17 +811,17 @@
         if self.at < n:
             keep, send = fold(self.keep, self.got, deps)
             self.keep = keep
-            self.got = cross(self.d, send, self.at)
+            self.got = cross(self.d, send, self.at, self.mix)
             return keep
         if self.at == n:
             (keep,) = fold(self.keep, self.got, deps)
             self.parts = [keep]
-            self.got = cross(self.d, keep, n - 1)
+            self.got = cross(self.d, keep, n - 1, self.mix)
             return keep
         self.parts.append(self.got)
         if self.at < 2 * n:
             full = join(self.parts, deps)
-            self.got = cross(self.d, full, 2 * n - 1 - self.at)
+            self.got = cross(self.d, full, 2 * n - 1 - self.at, self.mix)
             return full
         return self.got
 
@@ -846,7 +861,7 @@
     t = lax.axis_index("tp")
     first = [jnp.where(t == 0, way(d, 0, k), way(d, 1, k)) for k in range(d.bits)]
     bit = (c >> first[0]) % 2
-    sc = jnp.stack([x, bit, c, *first]).astype(jnp.int32)
+    sc = jnp.stack([x, bit, c, *first, *range(d.bits)]).astype(jnp.int32)
     w_qkv = qkv_weight.transpose(0, 2, 1, 3)
     tiles = d.F // FT
     half = tiles // 2
@@ -865,13 +880,15 @@
             up_a = take(sc, up_weight, tile, lambda n, b: (layer, 0, b), (FT, FT), deps=(out,))
             up_b = take(sc, up_weight, tile, lambda n, b: (layer, 0, half + b), (FT, FT),
                         deps=(up_a,))
-            dn = take(sc, down_weight, tile, lambda n, b: (layer, n * half + b, 0),
-                      (2, FT, FT), 2, deps=(up_b,))
-            self.last = dn
-            self.qkv, self.out, self.dn = over(qkv), over(out), over(dn)
+            dn_a = take(sc, down_weight, tile, lambda n, b: (layer, b, 0), (FT, FT), deps=(up_b,))
+            dn_b = take(sc, down_weight, tile, lambda n, b: (layer, half + b, 0), (FT, FT),
+                        deps=(dn_a,))
+            self.last = dn_b
+            self.qkv, self.out = over(qkv), over(out)
+            self.dn_a, self.dn_b = over(dn_a), over(dn_b)
             self.up_a, self.up_b = over(up_a), over(up_b)
             self.up = (*self.up_a, *self.up_b)
-            self.down = (*self.dn, *self.dn)
+            self.down = (*self.dn_a, *self.dn_b)
 
     p0 = Pieces(0, ())
     p = [p0]
@@ -926,15 +943,15 @@
     k0, k1 = kept
     state = forward(0, state, lambda n: (
         (p0.out[0], p0.up_a[0], p0.last) if n == 0
-        else (p0.out[1], p0.up_a[1], p0.up_b[0], p0.dn[0]) if n == 1
-        else (p[1].qkv[0], p[1].out[0], p[1].last) if n == 2
+        else (p0.out[1], p0.up_a[1], p0.up_b[0], p0.dn_a[0], p[1].last) if n == 1
+        else (p0.dn_b[0], p[1].qkv[0], p[1].out[0]) if n == 2
         else ()
     ))
     p1 = p[1]
     state = forward(1, state, lambda n: (
-        (p1.up_a[0], p1.up_b[0]) if n == 0
-        else (p1.out[1], p1.up_a[1], p1.dn[0], k1.n_r) if n == 1
-        else (k0.act_pr,) if n == 2
+        (p1.up_a[0],) if n == 0
+        else (p1.out[1], p1.up_a[1], p1.up_b[0], p1.dn_a[0]) if n == 1
+        else (p1.dn_b[0], k1.n_r, k0.act_pr) if n == 2
         else ()
     ))
     own_rows = tokens.shape[0]
@@ -948,7 +965,7 @@
     output = output.astype(BF)
     grad = both(cotangent)
     sums = [None] * LAYERS
-    def grad_ffn(k, more, deps=()):
+    def grad_ffn(k, more, mix, deps=()):
         ins = (k.n2_o, k.act_p, k.act_pr, k.act_q, k.act_qr, k.xba, k.xba_r, k.xbb, k.xbb_r,
                k.db_o)
         jobs = []
@@ -961,15 +978,15 @@
         if more:
             ins += (k.ctx, k.ctx_r, k.da_o, k.da_r)
             jobs += [((10, None), (12, None), (11, None), (13, None))]
-        return Sum(d, *weight_grad(d, "ffn", sc, ins, jobs, deps))
-
-    def grad_qkv(k, more, deps=()):
+        return Sum(d, mix, *weight_grad(d, "ffn", sc, ins, jobs, mix, deps=deps))
+
+    def grad_qkv(k, more, mix, flat=None, deps=()):
         ins = (k.n_o, k.n_r, k.xc, k.xc_r)
         jobs = [((0, None), (2, n), (1, None), (3, n)) for n in range(3)]
         if more:
             ins += (k.ctx, k.da_o, k.ctx_r, k.da_r)
             jobs += [((4, None), (5, None), (6, None), (7, None))]
-        return Sum(d, *weight_grad(d, "qkv", sc, ins, jobs, deps))
+        return Sum(d, mix, *weight_grad(d, "qkv", sc, ins, jobs, mix, flat, deps))
 
     def back_ffn(layer, k, grad, deps=()):
         k.db_o, k.xba, k.xbb, k.usum, k.bsum, part = ffn_backward(
@@ -997,66 +1014,53 @@
         sums[layer] = (k.qvsum, k.usum, k.gsum1, k.gsum2, k.ssum1, k.asum, k.ssum2, k.bsum)
         return grad
 
+    total = LAYERS * (2 * d.W + d.F + 6 * d.D)
+
     def small_sums():
-        return jnp.concatenate(
-            [v.reshape(-1) for layer in sums for v in layer]
-        ).reshape(-1, 128)
+        flat = jnp.concatenate([v.reshape(-1) for layer in sums for v in layer])
+        return jnp.pad(flat, (0, d.C * EXTRA * FT - total)).reshape(d.C, EXTRA, FT)
 
     part = back_ffn(1, k1, grad, (k0.act_qr, k1.ctx_r))
     dchunks = back_context(1, k1, grad, part, (state[2],))
     dback = attend_backward(d, sc, kb, k1.chunks, all_to_all(dchunks),
                             deps=(k1.act_pr, k1.act_qr))
     dparts = all_to_all(dback)
-    f1 = grad_ffn(k1, False, (dback,))
-    part = back_qkv(1, k1, dparts, (f1.keep, k0.n_r, k0.ctx_r))
+    f1 = grad_ffn(k1, False, True, (dback,))
+    part = back_qkv(1, k1, dparts, (f1.keep,))
     grad = back_input(1, k1, part)
     part = back_ffn(0, k0, grad)
     a = f1.step(part)
-    dchunks = back_context(0, k0, grad, part, (a, k1.xc_r, k1.da_r))
-    q1 = grad_qkv(k1, True, (dchunks,))
+    dchunks = back_context(0, k0, grad, part, (a, k1.xc_r))
+    q1 = grad_qkv(k1, True, True, None, (dchunks,))
     a = f1.step(q1.keep)
-    dback = attend_backward(d, sc, kb, k0.chunks, all_to_all(dchunks), deps=(a, k0.xba_r))
+    dback = attend_backward(d, sc, kb, k0.chunks, all_to_all(dchunks),
+                            deps=(a, k0.xba_r, k0.ctx_r, k0.n_r))
     dparts = all_to_all(dback)
-    f0 = grad_ffn(k0, True, (dback,))
+    f0 = grad_ffn(k0, True, True, (dback,))
     part = back_qkv(0, k0, dparts, (f0.keep,))
     grad = back_input(0, k0, part)
     flat = small_sums()
     flat = flat + swap(flat, "fsdp")
-    a = q1.step(grad)
-    a = f1.step(a)
-    a = f0.step(a, flat)
-    q0 = grad_qkv(k0, False, (a,))
-    a = q1.step(q0.keep)
-    a = q0.step(a)
-    a = f0.step(a)
-    a = f1.step(a)
-    flat = flat + cross_all(d, flat, 0)
-    a = q1.step(a, flat)
-    a = q0.step(a)
-    a = f1.step(a)
-    a = q1.step(a)
-    flats = list(range(1, d.bits))
-    while f1.at < 2 * d.bits - 1:
+    q0 = grad_qkv(k0, False, False, flat, (grad,))
+    a = q0.keep
+    ffn_kinds = (("cols", tiles), ("mats", tiles))
+    qkv_kinds = (("mats", 3), ("mats", 1))
+    last = 2 * d.bits - 1
+    for unit in (f1, f0, q1, q0, f1, f0, q1, f1, q0, f0, q1, q0, f0, q1, q0):
+        if unit.at < last:
+            a = unit.step(a)
+    while f1.at < last:
         a = f1.step(a)
-    while any(u.at < 2 * d.bits - 1 for u in (q1, q0, f0)):
-        for unit in (f0, q1, q0):
-            if unit.at < 2 * d.bits - 1:
-                if unit is f0 and flats:
-                    flat = flat + cross_all(d, flat, flats.pop(0))
-                a = unit.step(a, flat) if unit is f0 else unit.step(a)
-    for step in flats:
-        flat = flat + cross_all(d, flat, step)
-    ffn_kinds = (("cols", tiles), ("mats", tiles))
-    g_ffn = place(d, 1, sc, f1.finish(), None, ffn_kinds, "ffn", (a,))
-    g_qkv = place(d, 1, sc, q1.finish(), None, (("mats", 3), ("mats", 1)), "qkv", (g_ffn[0],))
-    g_up, g_down, g_out = place(d, 0, sc, f0.finish(), (*g_ffn, g_qkv[1]),
-                                (*ffn_kinds, ("mats", 1)), "ffn", (a,))
-    (g_qkv,) = place(d, 0, sc, q0.finish(), (g_qkv[0],), (("mats", 3),), "qkv", (g_up,))
-    flat = flat.reshape(LAYERS, -1)
-    n_qv, n_up = 2 * d.W, d.F
-    qv_grad = flat[:, :n_qv].reshape(LAYERS, 2, d.W)
-    up_grad = flat[:, n_qv : n_qv + n_up]
-    rest = flat[:, n_qv + n_up :].reshape(LAYERS, 6, d.D)
+    g_ffn = place(d, 1, sc, f1, None, ffn_kinds, "ffn", (a,))
+    a = g_ffn[0]
+    for unit in (q1, q0, f0):
+        while unit.at < last:
+            a = unit.step(a)
+    g_qkv = place(d, 1, sc, q1, None, qkv_kinds, "qkv", (a,))
+    a = g_qkv[0]
+    g_up, g_down, g_out = place(d, 0, sc, f0, (*g_ffn, g_qkv[1]), (*ffn_kinds, ("mats", 1)),
+                                "ffn", (a,))
+    g_qkv, qv_grad, up_grad, gain_grad, bias_grad = place(d, 0, sc, q0, (g_qkv[0],), (("mats", 3),), "qkv", (g_up,))
     return (
         output,
         mine(grad),
@@ -1066,8 +1070,8 @@
         g_down.reshape(LAYERS, d.F, d.H),
         qv_grad,
         up_grad,
-        rest[:, :2],
-        rest[:, 2:],
+        gain_grad,
+        bias_grad,
     )
 
 

time: 791 us -> 744 us (0.941)
  waiting for transfers between devices: 360 us -> 316 us
    ppermute x37 -> x39, waiting for transfers between devices: 172 us -> 132 us  [swap(): return lax.ppermute(values, axis, [(0, 1), (1, 0)])]
    ppermute x3 -> x0, waiting for transfers between devices: 39 us -> none  [cross_all(): return lax.ppermute(values, 'ctx', [(i, i ^ 1 << step) for i in range(d.C)])]
    ppermute x34 -> x36, waiting for transfers between devices: 142 us -> 174 us  [cross(): return lax.ppermute(values, ('ctx', 'tp'), pairs)]
    pallas_call x10 -> x12, Pallas kernels: 26 us -> 30.8 us  [take(): pl.pallas_call(take_body, grid_spec=pltpu.PrefetchScalarGridSpec(num_scal...]
    ppermute x37 -> x39, starting transfers between devices: 31 us -> 33.6 us  [swap(): return lax.ppermute(values, axis, [(0, 1), (1, 0)])]
    ppermute x34 -> x36, starting transfers between devices: 46.2 us -> 45 us  [cross(): return lax.ppermute(values, ('ctx', 'tp'), pairs)]
    unnamed x249 -> x253, local copies, waits for them, and re-layouts: 40.9 us -> 42 us
  transfers between devices with their start and end apart: 82 -> 83, of which waited for: 30 -> 36; matrix products, arithmetic and copies ran while one was open for 2% -> 2% of each run, Pallas kernels for 24% -> 26%
where the time goes in v3:
time: 744 us; the launch traced here: 734 us
  waiting for transfers between devices  316 us (42%)
  Pallas kernels  243 us (33%)
  starting transfers between devices  119 us (16%)
  local copies, waits for them, and re-layouts  47.2 us (6%)
    pallas_call x42, Pallas kernels, kernel_call(): pl.pallas_call(ordered, in_specs=list(in_specs) + [pl.BlockSpec(memory_sp...  191 us
    ppermute x36, waiting for transfers between devices, cross(): return lax.ppermute(values, ('ctx', 'tp'), pairs)  174 us
    ppermute x39, waiting for transfers between devices, swap(): return lax.ppermute(values, axis, [(0, 1), (1, 0)])  132 us
    ppermute x36, starting transfers between devices, cross(): return lax.ppermute(values, ('ctx', 'tp'), pairs)  45 us
    unnamed x253, local copies, waits for them, and re-layouts  42 us
    all_to_all x8, starting transfers between devices, all_to_all(): return lax.all_to_all(values, 'ctx', 0, 0)  40.9 us
    ppermute x39, starting transfers between devices, swap(): return lax.ppermute(values, axis, [(0, 1), (1, 0)])  33.6 us
    pallas_call x12, Pallas kernels, take(): pl.pallas_call(take_body, grid_spec=pltpu.PrefetchScalarGridSpec(num_scal...  30.8 us
  transfers between devices with their start and end apart: 83, of which 36 were waited for; matrix products, arithmetic and copies ran while one was open for 2% of the time, Pallas kernels for 26%

profile of v3, /device:TPU:0, one launch (start us, length us, event | category | flops | bytes accessed | tf_op | source)
XLA Modules:
  0.0 733.6 jit_solution(17226403965417121103)
XLA Ops:
  13.9 11.7 %collective-permute-done.1.refs_5_.refs_2_ = bf16[3,256,512]{2,1,0:T(8,128)(2,1)S(1)} collective-permute-done((bf16[3,256,512]{2,1,0:T(8,128)(2,1)}, bf16[3,256,512]{2,1,0:T(8,128)(2,1)S(1)}, u32[]{:S(2)}, u32[]{:S(2)}) %collective-permute-start.1) | collective-permute-done | bytes 786464 | tf_op jit(solution)/shard_map/ppermute | solution.py:726
  47.3 6.2 all-to-all-start
  98.0 10.0 %collective-permute-done.9.refs_5_.refs_16_.refs_11_ = bf16[512,512]{1,0:T(8,128)(2,1)} collective-permute-done((bf16[512,512]{1,0:T(8,128)(2,1)}, bf16[512,512]{1,0:T(8,128)(2,1)}, u32[]{:S(2)}, u32[]{:S(2)}) %collective-permute-start.9) | collective-permute-done | bytes 524320 | tf_op jit(solution)/shard_map/ppermute | solution.py:726
  120.9 12.0 %ffn_forward.2 = (f32[256,1024]{1,0:T(8,128)}, bf16[256,512]{1,0:T(8,128)(2,1)}, bf16[3,256,512]{2,1,0:T(8,128)(2,1)}, bf16[2,256,512]{2,1,0:T(8,128)(2,1)}, bf1...) custom-call(s32[9]{0:T(128)} %stack.24.sc.refs_0_, f32[256,1024]{1,0:T(8,128)} %get-tuple-element.108.refs_0_.refs_1_.refs_3_, ...), custom_call_target="tpu_custom_call" | custom-call | flops 2147483648 | bytes 14000000 | tf_op jit(solution)/shard_map/ffn_forward/pallas_call | solution.py:51
  151.8 20.6 %collective-permute-done.19.refs_3_.refs_8_ = bf16[256,512]{1,0:T(8,128)(2,1)S(1)} collective-permute-done((bf16[256,512]{1,0:T(8,128)(2,1)S(1)}, bf16[256,512]{1,0:T(8,128)(2,1)S(1)}, u32[]{:S(2)}, u32[]{:S(2)}) %collective-permute-start.19) | collective-permute-done | bytes 262176 | tf_op jit(solution)/shard_map/ppermute | solution.py:741
  173.3 5.9 all-to-all-done.2.refs_2_
  189.2 12.0 %collective-permute-done.23.refs_5_.refs_16_.refs_11_ = bf16[512,512]{1,0:T(8,128)(2,1)S(1)} collective-permute-done((bf16[512,512]{1,0:T(8,128)(2,1)S(1)}, bf16[512,512]{1,0:T(8,128)(2,1)S(1)}, u32[]{:S(2)}, u32[]{:S(2)}) %collective-permute-start.23) | collective-permute-done | bytes 524320 | tf_op jit(solution)/shard_map/ppermute | solution.py:726
  216.1 5.6 collective-permute-done.27.refs_11_.refs_7_
  222.7 12.0 %ffn_forward.3 = (f32[256,1024]{1,0:T(8,128)}, bf16[256,512]{1,0:T(8,128)(2,1)}, bf16[3,256,512]{2,1,0:T(8,128)(2,1)}, bf16[2,256,512]{2,1,0:T(8,128)(2,1)}, bf1...) custom-call(s32[9]{0:T(128)} %stack.24.sc.refs_0_, f32[256,1024]{1,0:T(8,128)} %get-tuple-element.113.refs_1_.refs_3_, ...), custom_call_target="tpu_custom_call" | custom-call | flops 2147483648 | bytes 14000000 | tf_op jit(solution)/shard_map/ffn_forward/pallas_call | solution.py:51
  235.7 10.4 %ffn_backward.2 = (bf16[256,512]{1,0:T(8,128)(2,1)}, bf16[2,256,512]{2,1,0:T(8,128)(2,1)}, bf16[3,256,512]{2,1,0:T(8,128)(2,1)}, f32[1,2048]{1,0:T(1,128)}, f32[...) custom-call(s32[9]{0:T(128)} %stack.24.sc.refs_0_, bf16[256,1024]{1,0:T(8,128)(2,1)} %maximum_select_fusion.1.refs_1_, ...), custom_call_target="tpu_custom_call" | custom-call | flops 2147483648 | bytes 14000000 | tf_op jit(solution)/shard_map/ffn_backward/pallas_call | solution.py:51
  253.9 6.4 all-to-all-start.4
  260.3 17.1 %collective-permute-done.36.refs_5_ = bf16[2,256,512]{2,1,0:T(8,128)(2,1)S(1)} collective-permute-done((bf16[2,256,512]{2,1,0:T(8,128)(2,1)S(1)}, bf16[2,256,512]{2,1,0:T(8,128)(2,1)S(1)}, u32[]{:S(2)}, u32[]{:S(2)}) %collective-permute-start.36) | collective-permute-done | bytes 524320 | tf_op jit(solution)/shard_map/ppermute | solution.py:726
  279.2 8.9 %attend_backward.2.refs_11_ = bf16[8,640,128]{2,1,0:T(8,128)(2,1)} custom-call(s32[9]{0:T(128)} %stack.24.sc.refs_0_, f32[16,2048]{1,0:T(8,128)} %bitcast_add_fusion.refs_1_, bf16[8,640,128]{2,1,0:T(8,128)(2,1)} %all-to-all-done.2.refs_2_, bf16[8,128,128]{2,1,0:T(8,128)(2,1)} %copy-done.70, bf16[3,256,512]{2,1,0:T(8,128)(2,1)} %copy-done.97, ...), custom_call_target="tpu_custom_call" | custom-call | flops 2684354560 | bytes 4000000 | tf_op jit(solution)/shard_map/attend_backward/pallas_call | solution.py:51
  288.2 6.1 all-to-all-start.5
  296.4 27.6 %collective-permute-done.37.refs_7_ = bf16[2,256,512]{2,1,0:T(8,128)(2,1)S(1)} collective-permute-done((bf16[2,256,512]{2,1,0:T(8,128)(2,1)S(1)}, bf16[2,256,512]{2,1,0:T(8,128)(2,1)S(1)}, u32[]{:S(2)}, u32[]{:S(2)}) %collective-permute-start.37) | collective-permute-done | bytes 524320 | tf_op jit(solution)/shard_map/ppermute | solution.py:726
  325.1 9.2 %weight_grad_ffn.2 = (bf16[4,512,512]{2,1,0:T(8,128)(2,1)}, bf16[4,512,512]{2,1,0:T(8,128)(2,1)}) custom-call(s32[9]{0:T(128)} %stack.24.sc.refs_0_, bf16[256,512]{1,0:T(8,128)(2,1)} %get-tuple-element.128.refs_1_, bf16[3,256,512]{2,1,0:T(8,128)(2,1)} %get-tuple-element.126.refs_2_, bf16[3,256,512]{2,1,0:T(8,128)(2,1)} %copy-done.97, ...), custom_call_target="tpu_custom_call" | custom-call | flops 2147483648 | bytes 8000000 | tf_op jit(solution)/shard_map/weight_grad_ffn/pallas_call | solution.py:51
  347.6 10.4 %ffn_backward.3 = (bf16[256,512]{1,0:T(8,128)(2,1)}, bf16[2,256,512]{2,1,0:T(8,128)(2,1)}, bf16[3,256,512]{2,1,0:T(8,128)(2,1)}, f32[1,2048]{1,0:T(1,128)}, f32[...) custom-call(s32[9]{0:T(128)} %stack.24.sc.refs_0_, f32[256,1024]{1,0:T(8,128)} %get-tuple-element.134.refs_1_, ...), custom_call_target="tpu_custom_call" | custom-call | flops 2147483648 | bytes 14000000 | tf_op jit(solution)/shard_map/ffn_backward/pallas_call | solution.py:51
  381.8 6.5 collective-permute-done.44.refs_8_
  389.0 5.6 weight_grad_qkv.2
  399.7 8.9 %attend_backward.3.refs_15_ = bf16[8,640,128]{2,1,0:T(8,128)(2,1)} custom-call(s32[9]{0:T(128)} %stack.24.sc.refs_0_, f32[16,2048]{1,0:T(8,128)} %bitcast_add_fusion.refs_1_, bf16[8,640,128]{2,1,0:T(8,128)(2,1)} %copy-done.5, bf16[8,128,128]{2,1,0:T(8,128)(2,1)} %copy-done.69, bf16[1,512,512]{2,1,0:T(8,128)(2,1)} %get-tuple-element.147.refs_4_.refs_0_, ...), custom_call_target="tpu_custom_call" | custom-call | flops 2684354560 | bytes 4000000 | tf_op jit(solution)/shard_map/attend_backward/pallas_call | solution.py:51
  408.6 5.5 all-to-all-start.7
  416.3 18.4 %collective-permute-done.48.refs_9_ = bf16[3,256,512]{2,1,0:T(8,128)(2,1)S(1)} collective-permute-done((bf16[3,256,512]{2,1,0:T(8,128)(2,1)S(1)}, bf16[3,256,512]{2,1,0:T(8,128)(2,1)S(1)}, u32[]{:S(2)}, u32[]{:S(2)}) %collective-permute-start.48) | collective-permute-done | bytes 786464 | tf_op jit(solution)/shard_map/ppermute | solution.py:726
  438.2 10.3 %weight_grad_ffn.3 = (bf16[4,576,512]{2,1,0:T(8,128)(2,1)}, bf16[4,576,512]{2,1,0:T(8,128)(2,1)}) custom-call(s32[9]{0:T(128)} %stack.24.sc.refs_0_, bf16[256,512]{1,0:T(8,128)(2,1)} %get-tuple-element.151.refs_1_, bf16[3,256,512]{2,1,0:T(8,128)(2,1)} %get-tuple-element.116.refs_2_, bf16[3,256,512]{2,1,0:T(8,128)(2,1)} %collective-permute-done.25.refs_7_.refs_3_, ...), custom_call_target="tpu_custom_call" | custom-call | flops 2415919104 | bytes 8000000 | tf_op jit(solution)/shard_map/weight_grad_ffn/pallas_call | solution.py:51
  467.5 14.2 %collective-permute-done.52 = f32[8,16,512]{2,1,0:T(8,128)S(1)} collective-permute-done((f32[8,16,512]{2,1,0:T(8,128)S(1)}, f32[8,16,512]{2,1,0:T(8,128)S(1)}, u32[]{:S(2)}, u32[]{:S(2)}) %collective-permute-start.52) | collective-permute-done | bytes 262176 | tf_op jit(solution)/shard_map/ppermute | solution.py:726
  503.4 9.1 %collective-permute-done.53.refs_1_ = bf16[4,208,512]{2,1,0:T(8,128)(2,1)S(1)} collective-permute-done((bf16[4,208,512]{2,1,0:T(8,128)(2,1)}, bf16[4,208,512]{2,1,0:T(8,128)(2,1)S(1)}, u32[]{:S(2)}, u32[]{:S(2)}) %collective-permute-start.53) | collective-permute-done | bytes 852000 | tf_op jit(solution)/shard_map/ppermute | solution.py:741
  521.0 7.8 %collective-permute-done.61.refs_1_ = bf16[2,576,512]{2,1,0:T(8,128)(2,1)S(1)} collective-permute-done((bf16[2,576,512]{2,1,0:T(8,128)(2,1)}, bf16[2,576,512]{2,1,0:T(8,128)(2,1)S(1)}, u32[]{:S(2)}, u32[]{:S(2)}) %collective-permute-start.61) | collective-permute-done | bytes 1179680 | tf_op jit(solution)/shard_map/ppermute | solution.py:741
  533.2 20.9 %collective-permute-done.60.refs_1_ = bf16[2,256,512]{2,1,0:T(8,128)(2,1)S(1)} collective-permute-done((bf16[2,256,512]{2,1,0:T(8,128)(2,1)S(1)}, bf16[2,256,512]{2,1,0:T(8,128)(2,1)S(1)}, u32[]{:S(2)}, u32[]{:S(2)}) %collective-permute-start.60) | collective-permute-done | bytes 524320 | tf_op jit(solution)/shard_map/ppermute | solution.py:741
  577.7 41.3 %collective-permute-done.63.refs_1_ = bf16[1,256,512]{2,1,0:T(8,128)(2,1)S(1)} collective-permute-done((bf16[1,256,512]{2,1,0:T(8,128)(2,1)S(1)}, bf16[1,256,512]{2,1,0:T(8,128)(2,1)S(1)}, u32[]{:S(2)}, u32[]{:S(2)}) %collective-permute-start.63) | collective-permute-done | bytes 262176 | tf_op jit(solution)/shard_map/ppermute | solution.py:741
  631.2 19.6 %collective-permute-done.66.refs_1_ = bf16[1,256,512]{2,1,0:T(8,128)(2,1)S(1)} collective-permute-done((bf16[1,256,512]{2,1,0:T(8,128)(2,1)S(1)}, bf16[1,256,512]{2,1,0:T(8,128)(2,1)S(1)}, u32[]{:S(2)}, u32[]{:S(2)}) %collective-permute-start.66) | collective-permute-done | bytes 262176 | tf_op jit(solution)/shard_map/ppermute | solution.py:741
  659.3 6.2 place_ffn.2
  685.2 32.4 %collective-permute-done.72.refs_3_ = bf16[4,256,512]{2,1,0:T(8,128)(2,1)S(1)} collective-permute-done((bf16[4,256,512]{2,1,0:T(8,128)(2,1)S(1)}, bf16[4,256,512]{2,1,0:T(8,128)(2,1)S(1)}, u32[]{:S(2)}, u32[]{:S(2)}) %collective-permute-start.72) | collective-permute-done | bytes 1048608 | tf_op jit(solution)/shard_map/ppermute | solution.py:741
  722.4 6.7 place_ffn.3
  (466 shorter events, 325.8 us)
Async XLA Ops:
  7.0 30.3 %collective-permute-start = (bf16[128,1024]{1,0:T(8,128)(2,1)S(1)}, bf16[128,1024]{1,0:T(8,128)(2,1)S(1)}, u32[]{:S(2)}, u32[]{:S(2)}) collective-permute-start(bf16[128,1024]{1,0:T(8,128)(2,1)S(1)} %copy-done.71), channel_id=1, source_target_pairs={{0,1},{1,0},{2,3},{3,2},{4,5},{5,4},{6,7},{7,6},{8,9},{9,8},{10,11... | collective-permute-start | bytes 786440 | tf_op jit(solution)/shard_map/ppermute | solution.py:726
  9.3 28.9 %collective-permute-start.3 = (bf16[256,512]{1,0:T(8,128)(2,1)}, bf16[256,512]{1,0:T(8,128)(2,1)S(1)}, u32[]{:S(2)}, u32[]{:S(2)}) collective-permute-start(bf16[256,512]{1,0:T(8,128)(2,1)} %take.13.refs_0_), channel_id=1, source_target_pairs={{0,16},{16,0},{1,17},{17,1},{2,18},{18,2},{3,19},{19,3},{4,20},{20... | collective-permute-start | bytes 786440 | tf_op jit(solution)/shard_map/ppermute | solution.py:726
  12.0 29.6 %collective-permute-start.4 = (bf16[512,512]{1,0:T(8,128)(2,1)}, bf16[512,512]{1,0:T(8,128)(2,1)S(1)}, u32[]{:S(2)}, u32[]{:S(2)}) collective-permute-start(bf16[512,512]{1,0:T(8,128)(2,1)} %take.14.refs_0_), channel_id=1, source_target_pairs={{0,16},{16,0},{1,17},{17,1},{2,18},{18,2},{3,19},{19,3},{4,20},{20... | collective-permute-start | bytes 1572872 | tf_op jit(solution)/shard_map/ppermute | solution.py:726
  47.3 37.1 %all-to-all-start = ((bf16[8,640,128]{2,1,0:T(8,128)(2,1)}), bf16[8,640,128]{2,1,0:T(8,128)(2,1)S(1)}, u32[]{:S(2)}, u32[]{:S(2)}) async-start(bf16[8,640,128]{2,1,0:T(8,128)(2,1)} %get-tuple-element.109), calls=%async_computation | async-start | bytes 2621440 | tf_op jit(solution)/shard_map/all_to_all | solution.py:835
  61.2 50.0 %collective-permute-start.10 = (bf16[3,256,512]{2,1,0:T(8,128)(2,1)}, bf16[3,256,512]{2,1,0:T(8,128)(2,1)S(1)}, u32[]{:S(2)}, u32[]{:S(2)}) collective-permute-start(bf16[3,256,512]{2,1,0:T(8,128)(2,1)} %take.18.refs_0_), channel_id=1, source_target_pairs={{0,16},{16,0},{1,17},{17,1},{2,18},{18,2},{3,19},{19,3},{4,20},{20... | collective-permute-start | bytes 2359304 | tf_op jit(solution)/shard_map/ppermute | solution.py:726
  77.6 30.5 %collective-permute-start.9 = (bf16[512,512]{1,0:T(8,128)(2,1)}, bf16[512,512]{1,0:T(8,128)(2,1)}, u32[]{:S(2)}, u32[]{:S(2)}) collective-permute-start(bf16[512,512]{1,0:T(8,128)(2,1)} %take.17.refs_10_), channel_id=1, source_target_pairs={{0,16},{16,0},{1,17},{17,1},{2,18},{18,2},{3,19},{19,3},{4,20},{20... | collective-permute-start | bytes 1572872 | tf_op jit(solution)/shard_map/ppermute | solution.py:726
  142.2 36.9 %all-to-all-start.2 = ((bf16[8,640,128]{2,1,0:T(8,128)(2,1)}), bf16[8,640,128]{2,1,0:T(8,128)(2,1)}, u32[]{:S(2)}, u32[]{:S(2)}) async-start(bf16[8,640,128]{2,1,0:T(8,128)(2,1)} %get-tuple-element.114), calls=%async_computation.2 | async-start | bytes 2621440 | tf_op jit(solution)/shard_map/all_to_all | solution.py:835
  151.1 52.3 %collective-permute-start.25 = (bf16[3,256,512]{2,1,0:T(8,128)(2,1)}, bf16[3,256,512]{2,1,0:T(8,128)(2,1)}, u32[]{:S(2)}, u32[]{:S(2)}) collective-permute-start(bf16[3,256,512]{2,1,0:T(8,128)(2,1)} %get-tuple-element.116.refs_2_), channel_id=1, source_target_pairs={{0,16},{16,0},{1,17},{17,1},{2,18},{18,2},{3,19},{19,3},{4,20},{20... | collective-permute-start | bytes 2359304 | tf_op jit(solution)/shard_map/ppermute | solution.py:726
  172.4 28.9 %collective-permute-start.23 = (bf16[512,512]{1,0:T(8,128)(2,1)S(1)}, bf16[512,512]{1,0:T(8,128)(2,1)S(1)}, u32[]{:S(2)}, u32[]{:S(2)}) collective-permute-start(bf16[512,512]{1,0:T(8,128)(2,1)S(1)} %copy-done.40), channel_id=1, source_target_pairs={{0,16},{16,0},{1,17},{17,1},{2,18},{18,2},{3,19},{19,3},{4,20},{20... | collective-permute-start | bytes 1572872 | tf_op jit(solution)/shard_map/ppermute | solution.py:726
  246.6 30.8 %collective-permute-start.35 = (bf16[3,256,512]{2,1,0:T(8,128)(2,1)S(1)}, bf16[3,256,512]{2,1,0:T(8,128)(2,1)S(1)}, u32[]{:S(2)}, u32[]{:S(2)}) collective-permute-start(bf16[3,256,512]{2,1,0:T(8,128)(2,1)S(1)} %copy-done.95), channel_id=1, source_target_pairs={{0,16},{16,0},{1,17},{17,1},{2,18},{18,2},{3,19},{19,3},{4,20},{20... | collective-permute-start | bytes 2359304 | tf_op jit(solution)/shard_map/ppermute | solution.py:726
  247.4 30.1 %collective-permute-start.36 = (bf16[2,256,512]{2,1,0:T(8,128)(2,1)S(1)}, bf16[2,256,512]{2,1,0:T(8,128)(2,1)S(1)}, u32[]{:S(2)}, u32[]{:S(2)}) collective-permute-start(bf16[2,256,512]{2,1,0:T(8,128)(2,1)S(1)} %copy-done.103), channel_id=1, source_target_pairs={{0,16},{16,0},{1,17},{17,1},{2,18},{18,2},{3,19},{19,3},{4,20},{20... | collective-permute-start | bytes 1572872 | tf_op jit(solution)/shard_map/ppermute | solution.py:726
  288.2 47.8 %all-to-all-start.5 = ((bf16[8,640,128]{2,1,0:T(8,128)(2,1)}), bf16[8,640,128]{2,1,0:T(8,128)(2,1)S(1)}, u32[]{:S(2)}, u32[]{:S(2)}) async-start(bf16[8,640,128]{2,1,0:T(8,128)(2,1)} %attend_backward.2.refs_11_), calls=%async_computation.5 | async-start | bytes 2621440 | tf_op jit(solution)/shard_map/all_to_all | solution.py:835
  294.3 29.7 %collective-permute-start.38 = (bf16[3,256,512]{2,1,0:T(8,128)(2,1)S(1)}, bf16[3,256,512]{2,1,0:T(8,128)(2,1)S(1)}, u32[]{:S(2)}, u32[]{:S(2)}) collective-permute-start(bf16[3,256,512]{2,1,0:T(8,128)(2,1)S(1)} %copy-done.96), channel_id=1, source_target_pairs={{0,16},{16,0},{1,17},{17,1},{2,18},{18,2},{3,19},{19,3},{4,20},{20... | collective-permute-start | bytes 2359304 | tf_op jit(solution)/shard_map/ppermute | solution.py:726
  295.1 28.9 %collective-permute-start.37 = (bf16[2,256,512]{2,1,0:T(8,128)(2,1)S(1)}, bf16[2,256,512]{2,1,0:T(8,128)(2,1)S(1)}, u32[]{:S(2)}, u32[]{:S(2)}) collective-permute-start(bf16[2,256,512]{2,1,0:T(8,128)(2,1)S(1)} %copy-done.104), channel_id=1, source_target_pairs={{0,16},{16,0},{1,17},{17,1},{2,18},{18,2},{3,19},{19,3},{4,20},{20... | collective-permute-start | bytes 1572872 | tf_op jit(solution)/shard_map/ppermute | solution.py:726
  365.6 28.9 %collective-permute-start.43 = (bf16[2,512,512]{2,1,0:T(8,128)(2,1)}, bf16[2,512,512]{2,1,0:T(8,128)(2,1)S(1)}, u32[]{:S(2)}, u32[]{:S(2)}) collective-permute-start(bf16[2,512,512]{2,1,0:T(8,128)(2,1)} %get-tuple-element.142), channel_id=1, source_target_pairs={{0,4},{1,3},{2,6},{3,1},{4,0},{5,7},{6,2},{7,5},{8,12},{9,11},{10,... | collective-permute-start | bytes 3145736 | tf_op jit(solution)/shard_map/ppermute | solution.py:741
  367.3 31.4 %collective-permute-start.45 = (bf16[2,256,512]{2,1,0:T(8,128)(2,1)}, bf16[2,256,512]{2,1,0:T(8,128)(2,1)S(1)}, u32[]{:S(2)}, u32[]{:S(2)}) collective-permute-start(bf16[2,256,512]{2,1,0:T(8,128)(2,1)} %get-tuple-element.148.refs_6_), channel_id=1, source_target_pairs={{0,16},{16,0},{1,17},{17,1},{2,18},{18,2},{3,19},{19,3},{4,20},{20... | collective-permute-start | bytes 1572872 | tf_op jit(solution)/shard_map/ppermute | solution.py:726
  408.6 39.9 %all-to-all-start.7 = ((bf16[8,640,128]{2,1,0:T(8,128)(2,1)}), bf16[8,640,128]{2,1,0:T(8,128)(2,1)S(1)}, u32[]{:S(2)}, u32[]{:S(2)}) async-start(bf16[8,640,128]{2,1,0:T(8,128)(2,1)} %attend_backward.3.refs_15_), calls=%async_computation.7 | async-start | bytes 2621440 | tf_op jit(solution)/shard_map/all_to_all | solution.py:835
  453.9 39.7 %collective-permute-start.55 = (bf16[4,576,512]{2,1,0:T(8,128)(2,1)}, bf16[4,576,512]{2,1,0:T(8,128)(2,1)S(1)}, u32[]{:S(2)}, u32[]{:S(2)}) collective-permute-start(bf16[4,576,512]{2,1,0:T(8,128)(2,1)} %get-tuple-element.180), channel_id=1, source_target_pairs={{0,2},{1,5},{2,0},{3,7},{4,6},{5,1},{6,4},{7,3},{8,10},{9,13},{10,... | collective-permute-start | bytes 7077896 | tf_op jit(solution)/shard_map/ppermute | solution.py:741
  464.6 35.2 %collective-permute-start.54 = (bf16[4,256,512]{2,1,0:T(8,128)(2,1)}, bf16[4,256,512]{2,1,0:T(8,128)(2,1)S(1)}, u32[]{:S(2)}, u32[]{:S(2)}) collective-permute-start(bf16[4,256,512]{2,1,0:T(8,128)(2,1)} %get-tuple-element.179), channel_id=1, source_target_pairs={{0,2},{1,5},{2,0},{3,7},{4,6},{5,1},{6,4},{7,3},{8,10},{9,13},{10,... | collective-permute-start | bytes 3145736 | tf_op jit(solution)/shard_map/ppermute | solution.py:741
  499.0 29.8 %collective-permute-start.61 = (bf16[2,576,512]{2,1,0:T(8,128)(2,1)}, bf16[2,576,512]{2,1,0:T(8,128)(2,1)S(1)}, u32[]{:S(2)}, u32[]{:S(2)}) collective-permute-start(bf16[2,576,512]{2,1,0:T(8,128)(2,1)} %get-tuple-element.187), channel_id=1, source_target_pairs={{0,4},{1,3},{2,6},{3,1},{4,0},{5,7},{6,2},{7,5},{8,12},{9,11},{10,... | collective-permute-start | bytes 3538952 | tf_op jit(solution)/shard_map/ppermute | solution.py:741
  519.0 38.0 %collective-permute-start.59 = (bf16[2,512,512]{2,1,0:T(8,128)(2,1)}, bf16[2,512,512]{2,1,0:T(8,128)(2,1)S(1)}, u32[]{:S(2)}, u32[]{:S(2)}) collective-permute-start(bf16[2,512,512]{2,1,0:T(8,128)(2,1)} %join.8.refs_2_), channel_id=1, source_target_pairs={{0,4},{1,3},{2,6},{3,1},{4,0},{5,7},{6,2},{7,5},{8,12},{9,11},{10,... | collective-permute-start | bytes 3145736 | tf_op jit(solution)/shard_map/ppermute | solution.py:741
  520.7 33.4 %collective-permute-start.60 = (bf16[2,256,512]{2,1,0:T(8,128)(2,1)S(1)}, bf16[2,256,512]{2,1,0:T(8,128)(2,1)S(1)}, u32[]{:S(2)}, u32[]{:S(2)}) collective-permute-start(bf16[2,256,512]{2,1,0:T(8,128)(2,1)S(1)} %copy-done.106), channel_id=1, source_target_pairs={{0,4},{1,3},{2,6},{3,1},{4,0},{5,7},{6,2},{7,5},{8,12},{9,11},{10,... | collective-permute-start | bytes 1572872 | tf_op jit(solution)/shard_map/ppermute | solution.py:741
  532.6 37.5 %collective-permute-start.64 = (bf16[1,576,512]{2,1,0:T(8,128)(2,1)}, bf16[1,576,512]{2,1,0:T(8,128)(2,1)S(1)}, u32[]{:S(2)}, u32[]{:S(2)}) collective-permute-start(bf16[1,576,512]{2,1,0:T(8,128)(2,1)} %get-tuple-element.193), channel_id=1, source_target_pairs={{0,8},{1,9},{2,10},{3,11},{4,12},{5,13},{6,14},{7,15},{8,0},{9,1},... | collective-permute-start | bytes 1769480 | tf_op jit(solution)/shard_map/ppermute | solution.py:741
  532.6 34.8 %collective-permute-start.57 = (bf16[2,208,512]{2,1,0:T(8,128)(2,1)S(1)}, bf16[2,208,512]{2,1,0:T(8,128)(2,1)S(1)}, u32[]{:S(2)}, u32[]{:S(2)}) collective-permute-start(bf16[2,208,512]{2,1,0:T(8,128)(2,1)S(1)} %copy-done.108), channel_id=1, source_target_pairs={{0,4},{1,5},{2,6},{3,7},{4,0},{5,1},{6,2},{7,3},{8,12},{9,13},{10,... | collective-permute-start | bytes 1277960 | tf_op jit(solution)/shard_map/ppermute | solution.py:741
  561.0 97.1 %collective-permute-start.70 = (bf16[4,512,512]{2,1,0:T(8,128)(2,1)}, bf16[4,512,512]{2,1,0:T(8,128)(2,1)S(1)}, u32[]{:S(2)}, u32[]{:S(2)}) collective-permute-start(bf16[4,512,512]{2,1,0:T(8,128)(2,1)} %join.9.refs_2_), channel_id=1, source_target_pairs={{0,2},{1,5},{2,0},{3,7},{4,6},{5,1},{6,4},{7,3},{8,10},{9,13},{10,... | collective-permute-start | bytes 6291464 | tf_op jit(solution)/shard_map/ppermute | solution.py:741
  573.2 51.9 %collective-permute-start.67 = (bf16[1,576,512]{2,1,0:T(8,128)(2,1)}, bf16[1,576,512]{2,1,0:T(8,128)(2,1)S(1)}, u32[]{:S(2)}, u32[]{:S(2)}) collective-permute-start(bf16[1,576,512]{2,1,0:T(8,128)(2,1)} %fold.21.refs_2_.refs_0_), channel_id=1, source_target_pairs={{0,8},{1,9},{2,10},{3,11},{4,12},{5,13},{6,14},{7,15},{8,0},{9,1},... | collective-permute-start | bytes 1769480 | tf_op jit(solution)/shard_map/ppermute | solution.py:741
  574.7 44.2 %collective-permute-start.63 = (bf16[1,256,512]{2,1,0:T(8,128)(2,1)S(1)}, bf16[1,256,512]{2,1,0:T(8,128)(2,1)S(1)}, u32[]{:S(2)}, u32[]{:S(2)}) collective-permute-start(bf16[1,256,512]{2,1,0:T(8,128)(2,1)S(1)} %copy-done.114), channel_id=1, source_target_pairs={{0,8},{1,9},{2,10},{3,11},{4,12},{5,13},{6,14},{7,15},{8,0},{9,1},... | collective-permute-start | bytes 786440 | tf_op jit(solution)/shard_map/ppermute | solution.py:741
  576.1 46.6 %collective-permute-start.62 = (bf16[1,208,512]{2,1,0:T(8,128)(2,1)}, bf16[1,208,512]{2,1,0:T(8,128)(2,1)S(1)}, u32[]{:S(2)}, u32[]{:S(2)}) collective-permute-start(bf16[1,208,512]{2,1,0:T(8,128)(2,1)} %get-tuple-element.191), channel_id=1, source_target_pairs={{0,8},{1,9},{2,10},{3,11},{4,12},{5,13},{6,14},{7,15},{8,0},{9,1},... | collective-permute-start | bytes 638984 | tf_op jit(solution)/shard_map/ppermute | solution.py:741
  628.3 44.4 %collective-permute-start.73 = (bf16[2,576,512]{2,1,0:T(8,128)(2,1)}, bf16[2,576,512]{2,1,0:T(8,128)(2,1)S(1)}, u32[]{:S(2)}, u32[]{:S(2)}) collective-permute-start(bf16[2,576,512]{2,1,0:T(8,128)(2,1)} %join.10.refs_2_), channel_id=1, source_target_pairs={{0,4},{1,3},{2,6},{3,1},{4,0},{5,7},{6,2},{7,5},{8,12},{9,11},{10,... | collective-permute-start | bytes 3538952 | tf_op jit(solution)/shard_map/ppermute | solution.py:741
  676.9 45.5 %collective-permute-start.74 = (bf16[4,576,512]{2,1,0:T(8,128)(2,1)}, bf16[4,576,512]{2,1,0:T(8,128)(2,1)}, u32[]{:S(2)}, u32[]{:S(2)}) collective-permute-start(bf16[4,576,512]{2,1,0:T(8,128)(2,1)} %join.15.refs_4_), channel_id=1, source_target_pairs={{0,2},{1,5},{2,0},{3,7},{4,6},{5,1},{6,4},{7,3},{8,10},{9,13},{10,... | collective-permute-start | bytes 7077896 | tf_op jit(solution)/shard_map/ppermute | solution.py:741
  679.2 38.3 %collective-permute-start.72 = (bf16[4,256,512]{2,1,0:T(8,128)(2,1)S(1)}, bf16[4,256,512]{2,1,0:T(8,128)(2,1)S(1)}, u32[]{:S(2)}, u32[]{:S(2)}) collective-permute-start(bf16[4,256,512]{2,1,0:T(8,128)(2,1)S(1)} %copy-done.16), channel_id=1, source_target_pairs={{0,2},{1,5},{2,0},{3,7},{4,6},{5,1},{6,4},{7,3},{8,10},{9,13},{10,... | collective-permute-start | bytes 3145736 | tf_op jit(solution)/shard_map/ppermute | solution.py:741
  679.3 49.8 %collective-permute-start.71 = (bf16[4,208,512]{2,1,0:T(8,128)(2,1)S(1)}, bf16[4,208,512]{2,1,0:T(8,128)(2,1)}, u32[]{:S(2)}, u32[]{:S(2)}) collective-permute-start(bf16[4,208,512]{2,1,0:T(8,128)(2,1)S(1)} %copy-done.17), channel_id=1, source_target_pairs={{0,2},{1,3},{2,0},{3,1},{4,6},{5,7},{6,4},{7,5},{8,10},{9,11},{10,... | collective-permute-start | bytes 2555912 | tf_op jit(solution)/shard_map/ppermute | solution.py:741
  (169 other events, 1494.0 us)

commit v4 on v3

--- a/solution.py
+++ b/solution.py
@@ -684,8 +684,9 @@
     parts = unit.finish()
     nt = sum(n for _, n in wide)
     flat = parts[0].shape[1] > nt * (FT // d.C)
-    extra = tuple(before or ()) + tuple(deps)
-    alias = {1 + len(parts) + k: k for k in range(len(before or ()))}
+    held = [k for k, one in enumerate(before) if one is not None]
+    extra = tuple(before[k] for k in held) + tuple(deps)
+    alias = {1 + len(parts) + n: k for n, k in enumerate(held)}
     shapes = [
         sds((LAYERS, FT, n * FT) if kind == "cols" else (LAYERS, n, FT, FT), F32)
         for kind, n in wide
@@ -1041,26 +1042,30 @@
     grad = back_input(0, k0, part)
     flat = small_sums()
     flat = flat + swap(flat, "fsdp")
-    q0 = grad_qkv(k0, False, False, flat, (grad,))
+    a = f1.step(grad)
+    q0 = grad_qkv(k0, False, False, flat, (a,))
     a = q0.keep
     ffn_kinds = (("cols", tiles), ("mats", tiles))
     qkv_kinds = (("mats", 3), ("mats", 1))
     last = 2 * d.bits - 1
-    for unit in (f1, f0, q1, q0, f1, f0, q1, f1, q0, f0, q1, q0, f0, q1, q0):
+    for unit in (f0, q1, q0, f1, f0, q1, f1, q0, q1, q0, f0, q1, q0):
         if unit.at < last:
             a = unit.step(a)
     while f1.at < last:
         a = f1.step(a)
-    g_ffn = place(d, 1, sc, f1, None, ffn_kinds, "ffn", (a,))
+    g_ffn = place(d, 1, sc, f1, (), ffn_kinds, "ffn", (a,))
     a = g_ffn[0]
-    for unit in (q1, q0, f0):
+    for unit in (q1, q0):
         while unit.at < last:
             a = unit.step(a)
-    g_qkv = place(d, 1, sc, q1, None, qkv_kinds, "qkv", (a,))
-    a = g_qkv[0]
-    g_up, g_down, g_out = place(d, 0, sc, f0, (*g_ffn, g_qkv[1]), (*ffn_kinds, ("mats", 1)),
+    while f0.at < last - 1:
+        a = f0.step(a)
+    g_qkv, g_out = place(d, 1, sc, q1, (), qkv_kinds, "qkv", (a,))
+    g_qkv, qv_grad, up_grad, gain_grad, bias_grad = place(
+        d, 0, sc, q0, (g_qkv,), (("mats", 3),), "qkv", (g_out,))
+    a = f0.step(g_qkv)
+    g_up, g_down, g_out = place(d, 0, sc, f0, (*g_ffn, g_out), (*ffn_kinds, ("mats", 1)),
                                 "ffn", (a,))
-    g_qkv, qv_grad, up_grad, gain_grad, bias_grad = place(d, 0, sc, q0, (g_qkv[0],), (("mats", 3),), "qkv", (g_up,))
     return (
         output,
         mine(grad),

time: 744 us -> 777 us (1.044)
  the two profiles are of different devices: /device:TPU:0 before, /device:TPU:25 now
where the time goes in v4:
time: 777 us; the launch traced here: 767 us
  waiting for transfers between devices  351 us (45%)
  Pallas kernels  243 us (31%)
  starting transfers between devices  116 us (15%)
  local copies, waits for them, and re-layouts  48.7 us (6%)
    ppermute x36, waiting for transfers between devices, cross(): return lax.ppermute(values, ('ctx', 'tp'), pairs)  242 us
    pallas_call x42, Pallas kernels, kernel_call(): pl.pallas_call(ordered, in_specs=list(in_specs) + [pl.BlockSpec(memory_sp...  192 us
    ppermute x39, waiting for transfers between devices, swap(): return lax.ppermute(values, axis, [(0, 1), (1, 0)])  109 us
    all_to_all x8, starting transfers between devices, all_to_all(): return lax.all_to_all(values, 'ctx', 0, 0)  45.9 us
    ppermute x39, starting transfers between devices, swap(): return lax.ppermute(values, axis, [(0, 1), (1, 0)])  44.6 us
    unnamed x257, local copies, waits for them, and re-layouts  44.6 us
    pallas_call x12, Pallas kernels, take(): pl.pallas_call(take_body, grid_spec=pltpu.PrefetchScalarGridSpec(num_scal...  30.6 us
    ppermute x36, starting transfers between devices, cross(): return lax.ppermute(values, ('ctx', 'tp'), pairs)  25.3 us
  transfers between devices with their start and end apart: 83, of which 33 were waited for; matrix products, arithmetic and copies ran while one was open for 1% of the time, Pallas kernels for 24%

profile of v4, /device:TPU:25, one launch (start us, length us, event | category | flops | bytes accessed | tf_op | source)
XLA Modules:
  0.0 766.7 jit_solution(11868398428261428607)
XLA Ops:
  12.6 10.1 %collective-permute-done.1.refs_5_.refs_2_ = bf16[3,256,512]{2,1,0:T(8,128)(2,1)S(1)} collective-permute-done((bf16[3,256,512]{2,1,0:T(8,128)(2,1)}, bf16[3,256,512]{2,1,0:T(8,128)(2,1)S(1)}, u32[]{:S(2)}, u32[]{:S(2)}) %collective-permute-start.1) | collective-permute-done | bytes 786464 | tf_op jit(solution)/shard_map/ppermute | solution.py:727
  33.5 6.1 collective-permute-done.4.refs_9_.refs_8_.refs_4_
  45.3 5.6 all-to-all-start
  71.9 10.0 %collective-permute-done.5.refs_3_.refs_8_ = bf16[256,512]{1,0:T(8,128)(2,1)S(1)} collective-permute-done((bf16[256,512]{1,0:T(8,128)(2,1)S(1)}, bf16[256,512]{1,0:T(8,128)(2,1)S(1)}, u32[]{:S(2)}, u32[]{:S(2)}) %collective-permute-start.5) | collective-permute-done | bytes 262176 | tf_op jit(solution)/shard_map/ppermute | solution.py:742
  90.4 5.9 all-to-all-start.1
  119.7 12.0 %ffn_forward.2 = (f32[256,1024]{1,0:T(8,128)}, bf16[256,512]{1,0:T(8,128)(2,1)}, bf16[3,256,512]{2,1,0:T(8,128)(2,1)}, bf16[2,256,512]{2,1,0:T(8,128)(2,1)}, bf1...) custom-call(s32[9]{0:T(128)} %stack.24.sc.refs_0_, f32[256,1024]{1,0:T(8,128)} %get-tuple-element.108.refs_0_.refs_1_.refs_3_, ...), custom_call_target="tpu_custom_call" | custom-call | flops 2147483648 | bytes 14000000 | tf_op jit(solution)/shard_map/ffn_forward/pallas_call | solution.py:51
  140.0 5.9 all-to-all-start.2
  149.4 27.6 %collective-permute-done.19.refs_3_.refs_8_ = bf16[256,512]{1,0:T(8,128)(2,1)S(1)} collective-permute-done((bf16[256,512]{1,0:T(8,128)(2,1)S(1)}, bf16[256,512]{1,0:T(8,128)(2,1)S(1)}, u32[]{:S(2)}, u32[]{:S(2)}) %collective-permute-start.19) | collective-permute-done | bytes 262176 | tf_op jit(solution)/shard_map/ppermute | solution.py:742
  184.0 6.0 all-to-all-start.3
  191.0 7.5 collective-permute-done.23.refs_5_.refs_16_.refs_11_
  212.5 5.6 collective-permute-done.27.refs_11_.refs_7_
  219.1 12.1 %ffn_forward.3 = (f32[256,1024]{1,0:T(8,128)}, bf16[256,512]{1,0:T(8,128)(2,1)}, bf16[3,256,512]{2,1,0:T(8,128)(2,1)}, bf16[2,256,512]{2,1,0:T(8,128)(2,1)}, bf1...) custom-call(s32[9]{0:T(128)} %stack.24.sc.refs_0_, f32[256,1024]{1,0:T(8,128)} %get-tuple-element.113.refs_1_.refs_3_, ...), custom_call_target="tpu_custom_call" | custom-call | flops 2147483648 | bytes 14000000 | tf_op jit(solution)/shard_map/ffn_forward/pallas_call | solution.py:51
  232.1 10.4 %ffn_backward.2 = (bf16[256,512]{1,0:T(8,128)(2,1)}, bf16[2,256,512]{2,1,0:T(8,128)(2,1)}, bf16[3,256,512]{2,1,0:T(8,128)(2,1)}, f32[1,2048]{1,0:T(1,128)}, f32[...) custom-call(s32[9]{0:T(128)} %stack.24.sc.refs_0_, bf16[256,1024]{1,0:T(8,128)(2,1)} %maximum_select_fusion.1.refs_1_, ...), custom_call_target="tpu_custom_call" | custom-call | flops 2147483648 | bytes 14000000 | tf_op jit(solution)/shard_map/ffn_backward/pallas_call | solution.py:51
  252.9 5.9 all-to-all-start.4
  258.8 16.8 %collective-permute-done.36.refs_5_ = bf16[2,256,512]{2,1,0:T(8,128)(2,1)S(1)} collective-permute-done((bf16[2,256,512]{2,1,0:T(8,128)(2,1)S(1)}, bf16[2,256,512]{2,1,0:T(8,128)(2,1)S(1)}, u32[]{:S(2)}, u32[]{:S(2)}) %collective-permute-start.36) | collective-permute-done | bytes 524320 | tf_op jit(solution)/shard_map/ppermute | solution.py:727
  277.4 8.9 %attend_backward.2.refs_11_ = bf16[8,640,128]{2,1,0:T(8,128)(2,1)} custom-call(s32[9]{0:T(128)} %stack.24.sc.refs_0_, f32[16,2048]{1,0:T(8,128)} %bitcast_add_fusion.refs_1_, bf16[8,640,128]{2,1,0:T(8,128)(2,1)} %all-to-all-done.2.refs_2_, bf16[8,128,128]{2,1,0:T(8,128)(2,1)} %copy-done.71, bf16[3,256,512]{2,1,0:T(8,128)(2,1)} %copy-done.98, ...), custom_call_target="tpu_custom_call" | custom-call | flops 2684354560 | bytes 4000000 | tf_op jit(solution)/shard_map/attend_backward/pallas_call | solution.py:51
  293.4 27.0 %collective-permute-done.37.refs_7_ = bf16[2,256,512]{2,1,0:T(8,128)(2,1)S(1)} collective-permute-done((bf16[2,256,512]{2,1,0:T(8,128)(2,1)S(1)}, bf16[2,256,512]{2,1,0:T(8,128)(2,1)S(1)}, u32[]{:S(2)}, u32[]{:S(2)}) %collective-permute-start.37) | collective-permute-done | bytes 524320 | tf_op jit(solution)/shard_map/ppermute | solution.py:727
  321.4 9.2 %weight_grad_ffn.2 = (bf16[4,512,512]{2,1,0:T(8,128)(2,1)}, bf16[4,512,512]{2,1,0:T(8,128)(2,1)}) custom-call(s32[9]{0:T(128)} %stack.24.sc.refs_0_, bf16[256,512]{1,0:T(8,128)(2,1)} %get-tuple-element.128.refs_1_, bf16[3,256,512]{2,1,0:T(8,128)(2,1)} %get-tuple-element.126.refs_2_, bf16[3,256,512]{2,1,0:T(8,128)(2,1)} %copy-done.98, ...), custom_call_target="tpu_custom_call" | custom-call | flops 2147483648 | bytes 8000000 | tf_op jit(solution)/shard_map/weight_grad_ffn/pallas_call | solution.py:51
  346.2 10.5 %ffn_backward.3 = (bf16[256,512]{1,0:T(8,128)(2,1)}, bf16[2,256,512]{2,1,0:T(8,128)(2,1)}, bf16[3,256,512]{2,1,0:T(8,128)(2,1)}, f32[1,2048]{1,0:T(1,128)}, f32[...) custom-call(s32[9]{0:T(128)} %stack.24.sc.refs_0_, f32[256,1024]{1,0:T(8,128)} %get-tuple-element.134.refs_1_, ...), custom_call_target="tpu_custom_call" | custom-call | flops 2147483648 | bytes 14000000 | tf_op jit(solution)/shard_map/ffn_backward/pallas_call | solution.py:51
  396.5 8.9 %attend_backward.3.refs_15_ = bf16[8,640,128]{2,1,0:T(8,128)(2,1)} custom-call(s32[9]{0:T(128)} %stack.24.sc.refs_0_, f32[16,2048]{1,0:T(8,128)} %bitcast_add_fusion.refs_1_, bf16[8,640,128]{2,1,0:T(8,128)(2,1)} %copy-done.4, bf16[8,128,128]{2,1,0:T(8,128)(2,1)} %copy-done.70, bf16[1,512,512]{2,1,0:T(8,128)(2,1)} %get-tuple-element.147.refs_4_.refs_0_, ...), custom_call_target="tpu_custom_call" | custom-call | flops 2684354560 | bytes 4000000 | tf_op jit(solution)/shard_map/attend_backward/pallas_call | solution.py:51
  412.5 14.9 %collective-permute-done.48.refs_9_ = bf16[3,256,512]{2,1,0:T(8,128)(2,1)S(1)} collective-permute-done((bf16[3,256,512]{2,1,0:T(8,128)(2,1)S(1)}, bf16[3,256,512]{2,1,0:T(8,128)(2,1)S(1)}, u32[]{:S(2)}, u32[]{:S(2)}) %collective-permute-start.48) | collective-permute-done | bytes 786464 | tf_op jit(solution)/shard_map/ppermute | solution.py:727
  427.5 5.6 collective-permute-done.49.refs_14_
  433.8 10.3 %weight_grad_ffn.3 = (bf16[4,576,512]{2,1,0:T(8,128)(2,1)}, bf16[4,576,512]{2,1,0:T(8,128)(2,1)}) custom-call(s32[9]{0:T(128)} %stack.24.sc.refs_0_, bf16[256,512]{1,0:T(8,128)(2,1)} %get-tuple-element.151.refs_1_, bf16[3,256,512]{2,1,0:T(8,128)(2,1)} %get-tuple-element.116.refs_2_, bf16[3,256,512]{2,1,0:T(8,128)(2,1)} %collective-permute-done.25.refs_7_.refs_3_, ...), custom_call_target="tpu_custom_call" | custom-call | flops 2415919104 | bytes 8000000 | tf_op jit(solution)/shard_map/weight_grad_ffn/pallas_call | solution.py:51
  463.1 16.2 %collective-permute-done.53.refs_1_ = bf16[1,512,512]{2,1,0:T(8,128)(2,1)S(1)} collective-permute-done((bf16[1,512,512]{2,1,0:T(8,128)(2,1)}, bf16[1,512,512]{2,1,0:T(8,128)(2,1)S(1)}, u32[]{:S(2)}, u32[]{:S(2)}) %collective-permute-start.53) | collective-permute-done | bytes 524320 | tf_op jit(solution)/shard_map/ppermute | solution.py:742
  500.9 22.9 %collective-permute-done.55.refs_1_ = bf16[4,256,512]{2,1,0:T(8,128)(2,1)S(1)} collective-permute-done((bf16[4,256,512]{2,1,0:T(8,128)(2,1)}, bf16[4,256,512]{2,1,0:T(8,128)(2,1)S(1)}, u32[]{:S(2)}, u32[]{:S(2)}) %collective-permute-start.55) | collective-permute-done | bytes 1048608 | tf_op jit(solution)/shard_map/ppermute | solution.py:742
  539.9 14.2 %collective-permute-done.60.refs_1_ = bf16[2,256,512]{2,1,0:T(8,128)(2,1)S(1)} collective-permute-done((bf16[2,256,512]{2,1,0:T(8,128)(2,1)S(1)}, bf16[2,256,512]{2,1,0:T(8,128)(2,1)S(1)}, u32[]{:S(2)}, u32[]{:S(2)}) %collective-permute-start.60) | collective-permute-done | bytes 524320 | tf_op jit(solution)/shard_map/ppermute | solution.py:742
  564.9 65.2 %collective-permute-done.57.refs_1_ = bf16[2,208,512]{2,1,0:T(8,128)(2,1)S(1)} collective-permute-done((bf16[2,208,512]{2,1,0:T(8,128)(2,1)S(1)}, bf16[2,208,512]{2,1,0:T(8,128)(2,1)S(1)}, u32[]{:S(2)}, u32[]{:S(2)}) %collective-permute-start.57) | collective-permute-done | bytes 426016 | tf_op jit(solution)/shard_map/ppermute | solution.py:742
  657.2 6.2 place_ffn.2
  677.2 12.7 %collective-permute-done.71.refs_3_ = bf16[4,256,512]{2,1,0:T(8,128)(2,1)S(1)} collective-permute-done((bf16[4,256,512]{2,1,0:T(8,128)(2,1)S(1)}, bf16[4,256,512]{2,1,0:T(8,128)(2,1)S(1)}, u32[]{:S(2)}, u32[]{:S(2)}) %collective-permute-start.71) | collective-permute-done | bytes 1048608 | tf_op jit(solution)/shard_map/ppermute | solution.py:742
  694.7 27.4 %collective-permute-done.70.refs_3_ = bf16[4,208,512]{2,1,0:T(8,128)(2,1)S(1)} collective-permute-done((bf16[4,208,512]{2,1,0:T(8,128)(2,1)S(1)}, bf16[4,208,512]{2,1,0:T(8,128)(2,1)S(1)}, u32[]{:S(2)}, u32[]{:S(2)}) %collective-permute-start.70) | collective-permute-done | bytes 852000 | tf_op jit(solution)/shard_map/ppermute | solution.py:742
  734.2 25.3 %collective-permute-done.74.refs_3_ = bf16[4,576,512]{2,1,0:T(8,128)(2,1)} collective-permute-done((bf16[4,576,512]{2,1,0:T(8,128)(2,1)}, bf16[4,576,512]{2,1,0:T(8,128)(2,1)}, u32[]{:S(2)}, u32[]{:S(2)}) %collective-permute-start.74) | collective-permute-done | bytes 2359328 | tf_op jit(solution)/shard_map/ppermute | solution.py:742
  759.6 6.7 place_ffn.3
  (470 shorter events, 325.1 us)
Async XLA Ops:
  11.4 28.2 %collective-permute-start.4 = (bf16[512,512]{1,0:T(8,128)(2,1)}, bf16[512,512]{1,0:T(8,128)(2,1)S(1)}, u32[]{:S(2)}, u32[]{:S(2)}) collective-permute-start(bf16[512,512]{1,0:T(8,128)(2,1)} %take.14.refs_0_), channel_id=1, source_target_pairs={{0,16},{16,0},{1,17},{17,1},{2,18},{18,2},{3,19},{19,3},{4,20},{20... | collective-permute-start | bytes 1572872 | tf_op jit(solution)/shard_map/ppermute | solution.py:727
  45.3 37.9 %all-to-all-start = ((bf16[8,640,128]{2,1,0:T(8,128)(2,1)}), bf16[8,640,128]{2,1,0:T(8,128)(2,1)S(1)}, u32[]{:S(2)}, u32[]{:S(2)}) async-start(bf16[8,640,128]{2,1,0:T(8,128)(2,1)} %get-tuple-element.109), calls=%async_computation | async-start | bytes 2621440 | tf_op jit(solution)/shard_map/all_to_all | solution.py:836
  50.9 32.2 %collective-permute-start.8 = (bf16[512,512]{1,0:T(8,128)(2,1)}, bf16[512,512]{1,0:T(8,128)(2,1)S(1)}, u32[]{:S(2)}, u32[]{:S(2)}) collective-permute-start(bf16[512,512]{1,0:T(8,128)(2,1)} %take.16.refs_0_), channel_id=1, source_target_pairs={{0,16},{16,0},{1,17},{17,1},{2,18},{18,2},{3,19},{19,3},{4,20},{20... | collective-permute-start | bytes 1572872 | tf_op jit(solution)/shard_map/ppermute | solution.py:727
  52.1 31.0 %collective-permute-start.7 = (bf16[512,512]{1,0:T(8,128)(2,1)}, bf16[512,512]{1,0:T(8,128)(2,1)}, u32[]{:S(2)}, u32[]{:S(2)}) collective-permute-start(bf16[512,512]{1,0:T(8,128)(2,1)} %take.15.refs_0_), channel_id=1, source_target_pairs={{0,16},{16,0},{1,17},{17,1},{2,18},{18,2},{3,19},{19,3},{4,20},{20... | collective-permute-start | bytes 1572872 | tf_op jit(solution)/shard_map/ppermute | solution.py:727
  53.2 30.0 %collective-permute-start.6 = (bf16[512,512]{1,0:T(8,128)(2,1)S(1)}, bf16[512,512]{1,0:T(8,128)(2,1)}, u32[]{:S(2)}, u32[]{:S(2)}) collective-permute-start(bf16[512,512]{1,0:T(8,128)(2,1)S(1)} %copy-done.8), channel_id=1, source_target_pairs={{0,2},{1,5},{2,0},{3,7},{4,6},{5,1},{6,4},{7,3},{8,10},{9,13},{10,... | collective-permute-start | bytes 1572872 | tf_op jit(solution)/shard_map/ppermute | solution.py:742
  53.5 28.5 %collective-permute-start.5 = (bf16[256,512]{1,0:T(8,128)(2,1)S(1)}, bf16[256,512]{1,0:T(8,128)(2,1)S(1)}, u32[]{:S(2)}, u32[]{:S(2)}) collective-permute-start(bf16[256,512]{1,0:T(8,128)(2,1)S(1)} %copy-done.21), channel_id=1, source_target_pairs={{0,2},{1,5},{2,0},{3,7},{4,6},{5,1},{6,4},{7,3},{8,10},{9,13},{10,... | collective-permute-start | bytes 786440 | tf_op jit(solution)/shard_map/ppermute | solution.py:742
  57.4 50.0 %collective-permute-start.10 = (bf16[3,256,512]{2,1,0:T(8,128)(2,1)}, bf16[3,256,512]{2,1,0:T(8,128)(2,1)S(1)}, u32[]{:S(2)}, u32[]{:S(2)}) collective-permute-start(bf16[3,256,512]{2,1,0:T(8,128)(2,1)} %take.18.refs_0_), channel_id=1, source_target_pairs={{0,16},{16,0},{1,17},{17,1},{2,18},{18,2},{3,19},{19,3},{4,20},{20... | collective-permute-start | bytes 2359304 | tf_op jit(solution)/shard_map/ppermute | solution.py:727
  140.0 37.7 %all-to-all-start.2 = ((bf16[8,640,128]{2,1,0:T(8,128)(2,1)}), bf16[8,640,128]{2,1,0:T(8,128)(2,1)}, u32[]{:S(2)}, u32[]{:S(2)}) async-start(bf16[8,640,128]{2,1,0:T(8,128)(2,1)} %get-tuple-element.114), calls=%async_computation.2 | async-start | bytes 2621440 | tf_op jit(solution)/shard_map/all_to_all | solution.py:836
  145.9 31.6 %collective-permute-start.22 = (bf16[512,512]{1,0:T(8,128)(2,1)}, bf16[512,512]{1,0:T(8,128)(2,1)S(1)}, u32[]{:S(2)}, u32[]{:S(2)}) collective-permute-start(bf16[512,512]{1,0:T(8,128)(2,1)} %take.22.refs_0_), channel_id=1, source_target_pairs={{0,16},{16,0},{1,17},{17,1},{2,18},{18,2},{3,19},{19,3},{4,20},{20... | collective-permute-start | bytes 1572872 | tf_op jit(solution)/shard_map/ppermute | solution.py:727
  146.5 31.0 %collective-permute-start.21 = (bf16[512,512]{1,0:T(8,128)(2,1)}, bf16[512,512]{1,0:T(8,128)(2,1)S(1)}, u32[]{:S(2)}, u32[]{:S(2)}) collective-permute-start(bf16[512,512]{1,0:T(8,128)(2,1)} %take.21.refs_0_), channel_id=1, source_target_pairs={{0,16},{16,0},{1,17},{17,1},{2,18},{18,2},{3,19},{19,3},{4,20},{20... | collective-permute-start | bytes 1572872 | tf_op jit(solution)/shard_map/ppermute | solution.py:727
  147.4 30.2 %collective-permute-start.20 = (bf16[512,512]{1,0:T(8,128)(2,1)S(1)}, bf16[512,512]{1,0:T(8,128)(2,1)S(1)}, u32[]{:S(2)}, u32[]{:S(2)}) collective-permute-start(bf16[512,512]{1,0:T(8,128)(2,1)S(1)} %copy-done.13), channel_id=1, source_target_pairs={{0,2},{1,5},{2,0},{3,7},{4,6},{5,1},{6,4},{7,3},{8,10},{9,13},{10,... | collective-permute-start | bytes 1572872 | tf_op jit(solution)/shard_map/ppermute | solution.py:742
  147.7 29.2 %collective-permute-start.19 = (bf16[256,512]{1,0:T(8,128)(2,1)S(1)}, bf16[256,512]{1,0:T(8,128)(2,1)S(1)}, u32[]{:S(2)}, u32[]{:S(2)}) collective-permute-start(bf16[256,512]{1,0:T(8,128)(2,1)S(1)} %copy-done.24), channel_id=1, source_target_pairs={{0,2},{1,5},{2,0},{3,7},{4,6},{5,1},{6,4},{7,3},{8,10},{9,13},{10,... | collective-permute-start | bytes 786440 | tf_op jit(solution)/shard_map/ppermute | solution.py:742
  148.9 53.6 %collective-permute-start.25 = (bf16[3,256,512]{2,1,0:T(8,128)(2,1)}, bf16[3,256,512]{2,1,0:T(8,128)(2,1)}, u32[]{:S(2)}, u32[]{:S(2)}) collective-permute-start(bf16[3,256,512]{2,1,0:T(8,128)(2,1)} %get-tuple-element.116.refs_2_), channel_id=1, source_target_pairs={{0,16},{16,0},{1,17},{17,1},{2,18},{18,2},{3,19},{19,3},{4,20},{20... | collective-permute-start | bytes 2359304 | tf_op jit(solution)/shard_map/ppermute | solution.py:727
  245.7 29.9 %collective-permute-start.35 = (bf16[3,256,512]{2,1,0:T(8,128)(2,1)S(1)}, bf16[3,256,512]{2,1,0:T(8,128)(2,1)S(1)}, u32[]{:S(2)}, u32[]{:S(2)}) collective-permute-start(bf16[3,256,512]{2,1,0:T(8,128)(2,1)S(1)} %copy-done.96), channel_id=1, source_target_pairs={{0,16},{16,0},{1,17},{17,1},{2,18},{18,2},{3,19},{19,3},{4,20},{20... | collective-permute-start | bytes 2359304 | tf_op jit(solution)/shard_map/ppermute | solution.py:727
  246.1 29.5 %collective-permute-start.36 = (bf16[2,256,512]{2,1,0:T(8,128)(2,1)S(1)}, bf16[2,256,512]{2,1,0:T(8,128)(2,1)S(1)}, u32[]{:S(2)}, u32[]{:S(2)}) collective-permute-start(bf16[2,256,512]{2,1,0:T(8,128)(2,1)S(1)} %copy-done.104), channel_id=1, source_target_pairs={{0,16},{16,0},{1,17},{17,1},{2,18},{18,2},{3,19},{19,3},{4,20},{20... | collective-permute-start | bytes 1572872 | tf_op jit(solution)/shard_map/ppermute | solution.py:727
  286.3 44.5 %all-to-all-start.5 = ((bf16[8,640,128]{2,1,0:T(8,128)(2,1)}), bf16[8,640,128]{2,1,0:T(8,128)(2,1)S(1)}, u32[]{:S(2)}, u32[]{:S(2)}) async-start(bf16[8,640,128]{2,1,0:T(8,128)(2,1)} %attend_backward.2.refs_11_), calls=%async_computation.5 | async-start | bytes 2621440 | tf_op jit(solution)/shard_map/all_to_all | solution.py:836
  291.9 28.4 %collective-permute-start.38 = (bf16[3,256,512]{2,1,0:T(8,128)(2,1)S(1)}, bf16[3,256,512]{2,1,0:T(8,128)(2,1)S(1)}, u32[]{:S(2)}, u32[]{:S(2)}) collective-permute-start(bf16[3,256,512]{2,1,0:T(8,128)(2,1)S(1)} %copy-done.97), channel_id=1, source_target_pairs={{0,16},{16,0},{1,17},{17,1},{2,18},{18,2},{3,19},{19,3},{4,20},{20... | collective-permute-start | bytes 2359304 | tf_op jit(solution)/shard_map/ppermute | solution.py:727
  361.8 28.9 %collective-permute-start.43 = (bf16[2,512,512]{2,1,0:T(8,128)(2,1)}, bf16[2,512,512]{2,1,0:T(8,128)(2,1)S(1)}, u32[]{:S(2)}, u32[]{:S(2)}) collective-permute-start(bf16[2,512,512]{2,1,0:T(8,128)(2,1)} %get-tuple-element.142), channel_id=1, source_target_pairs={{0,4},{1,3},{2,6},{3,1},{4,0},{5,7},{6,2},{7,5},{8,12},{9,11},{10,... | collective-permute-start | bytes 3145736 | tf_op jit(solution)/shard_map/ppermute | solution.py:742
  365.3 30.3 %collective-permute-start.45 = (bf16[2,256,512]{2,1,0:T(8,128)(2,1)}, bf16[2,256,512]{2,1,0:T(8,128)(2,1)S(1)}, u32[]{:S(2)}, u32[]{:S(2)}) collective-permute-start(bf16[2,256,512]{2,1,0:T(8,128)(2,1)} %get-tuple-element.148.refs_6_), channel_id=1, source_target_pairs={{0,16},{16,0},{1,17},{17,1},{2,18},{18,2},{3,19},{19,3},{4,20},{20... | collective-permute-start | bytes 1572872 | tf_op jit(solution)/shard_map/ppermute | solution.py:727
  405.5 38.6 %all-to-all-start.7 = ((bf16[8,640,128]{2,1,0:T(8,128)(2,1)}), bf16[8,640,128]{2,1,0:T(8,128)(2,1)S(1)}, u32[]{:S(2)}, u32[]{:S(2)}) async-start(bf16[8,640,128]{2,1,0:T(8,128)(2,1)} %attend_backward.3.refs_15_), calls=%async_computation.7 | async-start | bytes 2621440 | tf_op jit(solution)/shard_map/all_to_all | solution.py:836
  453.3 39.9 %collective-permute-start.56 = (bf16[4,576,512]{2,1,0:T(8,128)(2,1)}, bf16[4,576,512]{2,1,0:T(8,128)(2,1)S(1)}, u32[]{:S(2)}, u32[]{:S(2)}) collective-permute-start(bf16[4,576,512]{2,1,0:T(8,128)(2,1)} %get-tuple-element.181), channel_id=1, source_target_pairs={{0,2},{1,5},{2,0},{3,7},{4,6},{5,1},{6,4},{7,3},{8,10},{9,13},{10,... | collective-permute-start | bytes 7077896 | tf_op jit(solution)/shard_map/ppermute | solution.py:742
  454.1 28.9 %collective-permute-start.51 = (bf16[3,256,512]{2,1,0:T(8,128)(2,1)}, bf16[3,256,512]{2,1,0:T(8,128)(2,1)}, u32[]{:S(2)}, u32[]{:S(2)}) collective-permute-start(bf16[3,256,512]{2,1,0:T(8,128)(2,1)} %get-tuple-element.160.refs_3_), channel_id=1, source_target_pairs={{0,16},{16,0},{1,17},{17,1},{2,18},{18,2},{3,19},{19,3},{4,20},{20... | collective-permute-start | bytes 2359304 | tf_op jit(solution)/shard_map/ppermute | solution.py:727
  461.7 62.1 %collective-permute-start.55 = (bf16[4,256,512]{2,1,0:T(8,128)(2,1)}, bf16[4,256,512]{2,1,0:T(8,128)(2,1)S(1)}, u32[]{:S(2)}, u32[]{:S(2)}) collective-permute-start(bf16[4,256,512]{2,1,0:T(8,128)(2,1)} %get-tuple-element.180), channel_id=1, source_target_pairs={{0,2},{1,5},{2,0},{3,7},{4,6},{5,1},{6,4},{7,3},{8,10},{9,13},{10,... | collective-permute-start | bytes 3145736 | tf_op jit(solution)/shard_map/ppermute | solution.py:742
  487.4 40.0 %collective-permute-start.54 = (bf16[4,208,512]{2,1,0:T(8,128)(2,1)}, bf16[4,208,512]{2,1,0:T(8,128)(2,1)S(1)}, u32[]{:S(2)}, u32[]{:S(2)}) collective-permute-start(bf16[4,208,512]{2,1,0:T(8,128)(2,1)} %get-tuple-element.179), channel_id=1, source_target_pairs={{0,2},{1,3},{2,0},{3,1},{4,6},{5,7},{6,4},{7,5},{8,10},{9,11},{10,... | collective-permute-start | bytes 2555912 | tf_op jit(solution)/shard_map/ppermute | solution.py:742
  488.7 42.2 %collective-permute-start.58 = (bf16[1,512,512]{2,1,0:T(8,128)(2,1)S(1)}, bf16[1,512,512]{2,1,0:T(8,128)(2,1)S(1)}, u32[]{:S(2)}, u32[]{:S(2)}) collective-permute-start(bf16[1,512,512]{2,1,0:T(8,128)(2,1)S(1)} %copy-done), channel_id=1, source_target_pairs={{0,8},{1,9},{2,10},{3,11},{4,12},{5,13},{6,14},{7,15},{8,0},{9,1},... | collective-permute-start | bytes 1572872 | tf_op jit(solution)/shard_map/ppermute | solution.py:742
  498.6 37.5 %collective-permute-start.61 = (bf16[2,576,512]{2,1,0:T(8,128)(2,1)}, bf16[2,576,512]{2,1,0:T(8,128)(2,1)S(1)}, u32[]{:S(2)}, u32[]{:S(2)}) collective-permute-start(bf16[2,576,512]{2,1,0:T(8,128)(2,1)} %get-tuple-element.187), channel_id=1, source_target_pairs={{0,4},{1,3},{2,6},{3,1},{4,0},{5,7},{6,2},{7,5},{8,12},{9,11},{10,... | collective-permute-start | bytes 3538952 | tf_op jit(solution)/shard_map/ppermute | solution.py:742
  561.0 94.8 %collective-permute-start.69 = (bf16[4,512,512]{2,1,0:T(8,128)(2,1)}, bf16[4,512,512]{2,1,0:T(8,128)(2,1)S(1)}, u32[]{:S(2)}, u32[]{:S(2)}) collective-permute-start(bf16[4,512,512]{2,1,0:T(8,128)(2,1)} %join.9.refs_2_), channel_id=1, source_target_pairs={{0,2},{1,5},{2,0},{3,7},{4,6},{5,1},{6,4},{7,3},{8,10},{9,13},{10,... | collective-permute-start | bytes 6291464 | tf_op jit(solution)/shard_map/ppermute | solution.py:742
  561.0 69.1 %collective-permute-start.57 = (bf16[2,208,512]{2,1,0:T(8,128)(2,1)S(1)}, bf16[2,208,512]{2,1,0:T(8,128)(2,1)S(1)}, u32[]{:S(2)}, u32[]{:S(2)}) collective-permute-start(bf16[2,208,512]{2,1,0:T(8,128)(2,1)S(1)} %copy-done.109), channel_id=1, source_target_pairs={{0,4},{1,5},{2,6},{3,7},{4,0},{5,1},{6,2},{7,3},{8,12},{9,13},{10,... | collective-permute-start | bytes 1277960 | tf_op jit(solution)/shard_map/ppermute | solution.py:742
  562.5 82.8 %collective-permute-start.66 = (bf16[1,576,512]{2,1,0:T(8,128)(2,1)S(1)}, bf16[1,576,512]{2,1,0:T(8,128)(2,1)S(1)}, u32[]{:S(2)}, u32[]{:S(2)}) collective-permute-start(bf16[1,576,512]{2,1,0:T(8,128)(2,1)S(1)} %copy-done.101), channel_id=1, source_target_pairs={{0,8},{1,9},{2,10},{3,11},{4,12},{5,13},{6,14},{7,15},{8,0},{9,1},... | collective-permute-start | bytes 1769480 | tf_op jit(solution)/shard_map/ppermute | solution.py:742
  563.3 69.5 %collective-permute-start.63 = (bf16[1,256,512]{2,1,0:T(8,128)(2,1)S(1)}, bf16[1,256,512]{2,1,0:T(8,128)(2,1)S(1)}, u32[]{:S(2)}, u32[]{:S(2)}) collective-permute-start(bf16[1,256,512]{2,1,0:T(8,128)(2,1)S(1)} %copy-done.116), channel_id=1, source_target_pairs={{0,8},{1,9},{2,10},{3,11},{4,12},{5,13},{6,14},{7,15},{8,0},{9,1},... | collective-permute-start | bytes 786440 | tf_op jit(solution)/shard_map/ppermute | solution.py:742
  675.6 51.5 %collective-permute-start.73 = (bf16[2,576,512]{2,1,0:T(8,128)(2,1)}, bf16[2,576,512]{2,1,0:T(8,128)(2,1)S(1)}, u32[]{:S(2)}, u32[]{:S(2)}) collective-permute-start(bf16[2,576,512]{2,1,0:T(8,128)(2,1)} %join.14.refs_4_), channel_id=1, source_target_pairs={{0,4},{1,3},{2,6},{3,1},{4,0},{5,7},{6,2},{7,5},{8,12},{9,11},{10,... | collective-permute-start | bytes 3538952 | tf_op jit(solution)/shard_map/ppermute | solution.py:742
  675.9 46.3 %collective-permute-start.70 = (bf16[4,208,512]{2,1,0:T(8,128)(2,1)S(1)}, bf16[4,208,512]{2,1,0:T(8,128)(2,1)S(1)}, u32[]{:S(2)}, u32[]{:S(2)}) collective-permute-start(bf16[4,208,512]{2,1,0:T(8,128)(2,1)S(1)} %copy-done.16), channel_id=1, source_target_pairs={{0,2},{1,3},{2,0},{3,1},{4,6},{5,7},{6,4},{7,5},{8,10},{9,11},{10,... | collective-permute-start | bytes 2555912 | tf_op jit(solution)/shard_map/ppermute | solution.py:742
  (171 other events, 1402.9 us)

commit v5 on v4

--- a/solution.py
+++ b/solution.py
@@ -1048,24 +1048,21 @@
     ffn_kinds = (("cols", tiles), ("mats", tiles))
     qkv_kinds = (("mats", 3), ("mats", 1))
     last = 2 * d.bits - 1
-    for unit in (f0, q1, q0, f1, f0, q1, f1, q0, q1, q0, f0, q1, q0):
+    for unit in (f0, q1, q0, f1, f0, q1, f1, q0, f0, q1, q0, f0, q1, q0):
         if unit.at < last:
             a = unit.step(a)
     while f1.at < last:
         a = f1.step(a)
     g_ffn = place(d, 1, sc, f1, (), ffn_kinds, "ffn", (a,))
     a = g_ffn[0]
-    for unit in (q1, q0):
+    for unit in (q1, q0, f0):
         while unit.at < last:
             a = unit.step(a)
-    while f0.at < last - 1:
-        a = f0.step(a)
-    g_qkv, g_out = place(d, 1, sc, q1, (), qkv_kinds, "qkv", (a,))
+    g_up, g_down, g_out = place(d, 0, sc, f0, (*g_ffn, None), (*ffn_kinds, ("mats", 1)),
+                                "ffn", (a,))
+    g_qkv, g_out = place(d, 1, sc, q1, (None, g_out), qkv_kinds, "qkv", (g_up,))
     g_qkv, qv_grad, up_grad, gain_grad, bias_grad = place(
         d, 0, sc, q0, (g_qkv,), (("mats", 3),), "qkv", (g_out,))
-    a = f0.step(g_qkv)
-    g_up, g_down, g_out = place(d, 0, sc, f0, (*g_ffn, g_out), (*ffn_kinds, ("mats", 1)),
-                                "ffn", (a,))
     return (
         output,
         mine(grad),

time: 777 us -> 743 us (0.956)
  the two profiles are of different devices: /device:TPU:25 before, /device:TPU:0 now
where the time goes in v5:
time: 743 us; the launch traced here: 733 us
  waiting for transfers between devices  313 us (42%)
  Pallas kernels  243 us (33%)
  starting transfers between devices  123 us (17%)
  local copies, waits for them, and re-layouts  45.9 us (6%)
    pallas_call x42, Pallas kernels, kernel_call(): pl.pallas_call(ordered, in_specs=list(in_specs) + [pl.BlockSpec(memory_sp...  192 us
    ppermute x36, waiting for transfers between devices, cross(): return lax.ppermute(values, ('ctx', 'tp'), pairs)  185 us
    ppermute x39, waiting for transfers between devices, swap(): return lax.ppermute(values, axis, [(0, 1), (1, 0)])  118 us
    ppermute x36, starting transfers between devices, cross(): return lax.ppermute(values, ('ctx', 'tp'), pairs)  47.9 us
    all_to_all x8, starting transfers between devices, all_to_all(): return lax.all_to_all(values, 'ctx', 0, 0)  40.9 us
    unnamed x253, local copies, waits for them, and re-layouts  40.8 us
    ppermute x39, starting transfers between devices, swap(): return lax.ppermute(values, axis, [(0, 1), (1, 0)])  33.7 us
    pallas_call x12, Pallas kernels, take(): pl.pallas_call(take_body, grid_spec=pltpu.PrefetchScalarGridSpec(num_scal...  30.7 us
  transfers between devices with their start and end apart: 83, of which 39 were waited for; matrix products, arithmetic and copies ran while one was open for 2% of the time, Pallas kernels for 26%

profile of v5, /device:TPU:0, one launch (start us, length us, event | category | flops | bytes accessed | tf_op | source)
XLA Modules:
  0.0 732.6 jit_solution(11041441648756911596)
XLA Ops:
  13.9 11.7 %collective-permute-done.1.refs_5_.refs_2_ = bf16[3,256,512]{2,1,0:T(8,128)(2,1)S(1)} collective-permute-done((bf16[3,256,512]{2,1,0:T(8,128)(2,1)}, bf16[3,256,512]{2,1,0:T(8,128)(2,1)S(1)}, u32[]{:S(2)}, u32[]{:S(2)}) %collective-permute-start.1) | collective-permute-done | bytes 786464 | tf_op jit(solution)/shard_map/ppermute | solution.py:727
  47.3 6.2 all-to-all-start
  98.0 10.0 %collective-permute-done.9.refs_5_.refs_16_.refs_11_ = bf16[512,512]{1,0:T(8,128)(2,1)} collective-permute-done((bf16[512,512]{1,0:T(8,128)(2,1)}, bf16[512,512]{1,0:T(8,128)(2,1)}, u32[]{:S(2)}, u32[]{:S(2)}) %collective-permute-start.9) | collective-permute-done | bytes 524320 | tf_op jit(solution)/shard_map/ppermute | solution.py:727
  120.7 12.0 %ffn_forward.2 = (f32[256,1024]{1,0:T(8,128)}, bf16[256,512]{1,0:T(8,128)(2,1)}, bf16[3,256,512]{2,1,0:T(8,128)(2,1)}, bf16[2,256,512]{2,1,0:T(8,128)(2,1)}, bf1...) custom-call(s32[9]{0:T(128)} %stack.24.sc.refs_0_, f32[256,1024]{1,0:T(8,128)} %get-tuple-element.108.refs_0_.refs_1_.refs_3_, ...), custom_call_target="tpu_custom_call" | custom-call | flops 2147483648 | bytes 14000000 | tf_op jit(solution)/shard_map/ffn_forward/pallas_call | solution.py:51
  151.6 20.6 %collective-permute-done.19.refs_3_.refs_8_ = bf16[256,512]{1,0:T(8,128)(2,1)S(1)} collective-permute-done((bf16[256,512]{1,0:T(8,128)(2,1)S(1)}, bf16[256,512]{1,0:T(8,128)(2,1)S(1)}, u32[]{:S(2)}, u32[]{:S(2)}) %collective-permute-start.19) | collective-permute-done | bytes 262176 | tf_op jit(solution)/shard_map/ppermute | solution.py:742
  173.1 5.9 all-to-all-done.2.refs_2_
  179.0 5.4 attend_forward.3
  189.1 12.0 %collective-permute-done.23.refs_5_.refs_16_.refs_11_ = bf16[512,512]{1,0:T(8,128)(2,1)S(1)} collective-permute-done((bf16[512,512]{1,0:T(8,128)(2,1)S(1)}, bf16[512,512]{1,0:T(8,128)(2,1)S(1)}, u32[]{:S(2)}, u32[]{:S(2)}) %collective-permute-start.23) | collective-permute-done | bytes 524320 | tf_op jit(solution)/shard_map/ppermute | solution.py:727
  215.9 5.6 collective-permute-done.27.refs_11_.refs_7_
  222.6 12.0 %ffn_forward.3 = (f32[256,1024]{1,0:T(8,128)}, bf16[256,512]{1,0:T(8,128)(2,1)}, bf16[3,256,512]{2,1,0:T(8,128)(2,1)}, bf16[2,256,512]{2,1,0:T(8,128)(2,1)}, bf1...) custom-call(s32[9]{0:T(128)} %stack.24.sc.refs_0_, f32[256,1024]{1,0:T(8,128)} %get-tuple-element.113.refs_1_.refs_3_, ...), custom_call_target="tpu_custom_call" | custom-call | flops 2147483648 | bytes 14000000 | tf_op jit(solution)/shard_map/ffn_forward/pallas_call | solution.py:51
  235.6 10.4 %ffn_backward.2 = (bf16[256,512]{1,0:T(8,128)(2,1)}, bf16[2,256,512]{2,1,0:T(8,128)(2,1)}, bf16[3,256,512]{2,1,0:T(8,128)(2,1)}, f32[1,2048]{1,0:T(1,128)}, f32[...) custom-call(s32[9]{0:T(128)} %stack.24.sc.refs_0_, bf16[256,1024]{1,0:T(8,128)(2,1)} %maximum_select_fusion.1.refs_1_, ...), custom_call_target="tpu_custom_call" | custom-call | flops 2147483648 | bytes 14000000 | tf_op jit(solution)/shard_map/ffn_backward/pallas_call | solution.py:51
  253.7 6.4 all-to-all-start.4
  260.1 17.2 %collective-permute-done.36.refs_5_ = bf16[2,256,512]{2,1,0:T(8,128)(2,1)S(1)} collective-permute-done((bf16[2,256,512]{2,1,0:T(8,128)(2,1)S(1)}, bf16[2,256,512]{2,1,0:T(8,128)(2,1)S(1)}, u32[]{:S(2)}, u32[]{:S(2)}) %collective-permute-start.36) | collective-permute-done | bytes 524320 | tf_op jit(solution)/shard_map/ppermute | solution.py:727
  279.2 8.9 %attend_backward.2.refs_11_ = bf16[8,640,128]{2,1,0:T(8,128)(2,1)} custom-call(s32[9]{0:T(128)} %stack.24.sc.refs_0_, f32[16,2048]{1,0:T(8,128)} %bitcast_add_fusion.refs_1_, bf16[8,640,128]{2,1,0:T(8,128)(2,1)} %all-to-all-done.2.refs_2_, bf16[8,128,128]{2,1,0:T(8,128)(2,1)} %copy-done.70, bf16[3,256,512]{2,1,0:T(8,128)(2,1)} %copy-done.97, ...), custom_call_target="tpu_custom_call" | custom-call | flops 2684354560 | bytes 4000000 | tf_op jit(solution)/shard_map/attend_backward/pallas_call | solution.py:51
  288.1 6.1 all-to-all-start.5
  296.3 27.6 %collective-permute-done.37.refs_7_ = bf16[2,256,512]{2,1,0:T(8,128)(2,1)S(1)} collective-permute-done((bf16[2,256,512]{2,1,0:T(8,128)(2,1)S(1)}, bf16[2,256,512]{2,1,0:T(8,128)(2,1)S(1)}, u32[]{:S(2)}, u32[]{:S(2)}) %collective-permute-start.37) | collective-permute-done | bytes 524320 | tf_op jit(solution)/shard_map/ppermute | solution.py:727
  325.0 9.2 %weight_grad_ffn.2 = (bf16[4,512,512]{2,1,0:T(8,128)(2,1)}, bf16[4,512,512]{2,1,0:T(8,128)(2,1)}) custom-call(s32[9]{0:T(128)} %stack.24.sc.refs_0_, bf16[256,512]{1,0:T(8,128)(2,1)} %get-tuple-element.128.refs_1_, bf16[3,256,512]{2,1,0:T(8,128)(2,1)} %get-tuple-element.126.refs_2_, bf16[3,256,512]{2,1,0:T(8,128)(2,1)} %copy-done.97, ...), custom_call_target="tpu_custom_call" | custom-call | flops 2147483648 | bytes 8000000 | tf_op jit(solution)/shard_map/weight_grad_ffn/pallas_call | solution.py:51
  347.6 10.5 %ffn_backward.3 = (bf16[256,512]{1,0:T(8,128)(2,1)}, bf16[2,256,512]{2,1,0:T(8,128)(2,1)}, bf16[3,256,512]{2,1,0:T(8,128)(2,1)}, f32[1,2048]{1,0:T(1,128)}, f32[...) custom-call(s32[9]{0:T(128)} %stack.24.sc.refs_0_, f32[256,1024]{1,0:T(8,128)} %get-tuple-element.134.refs_1_, ...), custom_call_target="tpu_custom_call" | custom-call | flops 2147483648 | bytes 14000000 | tf_op jit(solution)/shard_map/ffn_backward/pallas_call | solution.py:51
  381.8 6.4 collective-permute-done.44.refs_8_
  389.0 5.6 weight_grad_qkv.2
  399.7 8.9 %attend_backward.3.refs_15_ = bf16[8,640,128]{2,1,0:T(8,128)(2,1)} custom-call(s32[9]{0:T(128)} %stack.24.sc.refs_0_, f32[16,2048]{1,0:T(8,128)} %bitcast_add_fusion.refs_1_, bf16[8,640,128]{2,1,0:T(8,128)(2,1)} %copy-done.6, bf16[8,128,128]{2,1,0:T(8,128)(2,1)} %copy-done.69, bf16[1,512,512]{2,1,0:T(8,128)(2,1)} %get-tuple-element.147.refs_4_.refs_0_, ...), custom_call_target="tpu_custom_call" | custom-call | flops 2684354560 | bytes 4000000 | tf_op jit(solution)/shard_map/attend_backward/pallas_call | solution.py:51
  408.6 5.6 all-to-all-start.7
  416.3 18.4 %collective-permute-done.48.refs_9_ = bf16[3,256,512]{2,1,0:T(8,128)(2,1)S(1)} collective-permute-done((bf16[3,256,512]{2,1,0:T(8,128)(2,1)S(1)}, bf16[3,256,512]{2,1,0:T(8,128)(2,1)S(1)}, u32[]{:S(2)}, u32[]{:S(2)}) %collective-permute-start.48) | collective-permute-done | bytes 786464 | tf_op jit(solution)/shard_map/ppermute | solution.py:727
  438.2 10.3 %weight_grad_ffn.3 = (bf16[4,576,512]{2,1,0:T(8,128)(2,1)}, bf16[4,576,512]{2,1,0:T(8,128)(2,1)}) custom-call(s32[9]{0:T(128)} %stack.24.sc.refs_0_, bf16[256,512]{1,0:T(8,128)(2,1)} %get-tuple-element.151.refs_1_, bf16[3,256,512]{2,1,0:T(8,128)(2,1)} %get-tuple-element.116.refs_2_, bf16[3,256,512]{2,1,0:T(8,128)(2,1)} %collective-permute-done.25.refs_7_.refs_3_, ...), custom_call_target="tpu_custom_call" | custom-call | flops 2415919104 | bytes 8000000 | tf_op jit(solution)/shard_map/weight_grad_ffn/pallas_call | solution.py:51
  467.5 13.1 %collective-permute-done.53.refs_1_ = bf16[1,512,512]{2,1,0:T(8,128)(2,1)S(1)} collective-permute-done((bf16[1,512,512]{2,1,0:T(8,128)(2,1)}, bf16[1,512,512]{2,1,0:T(8,128)(2,1)S(1)}, u32[]{:S(2)}, u32[]{:S(2)}) %collective-permute-start.53) | collective-permute-done | bytes 524320 | tf_op jit(solution)/shard_map/ppermute | solution.py:742
  505.6 14.7 %collective-permute-done.54.refs_1_ = bf16[4,208,512]{2,1,0:T(8,128)(2,1)S(1)} collective-permute-done((bf16[4,208,512]{2,1,0:T(8,128)(2,1)}, bf16[4,208,512]{2,1,0:T(8,128)(2,1)S(1)}, u32[]{:S(2)}, u32[]{:S(2)}) %collective-permute-start.54) | collective-permute-done | bytes 852000 | tf_op jit(solution)/shard_map/ppermute | solution.py:742
  537.0 23.7 %collective-permute-done.60.refs_1_ = bf16[2,256,512]{2,1,0:T(8,128)(2,1)S(1)} collective-permute-done((bf16[2,256,512]{2,1,0:T(8,128)(2,1)S(1)}, bf16[2,256,512]{2,1,0:T(8,128)(2,1)S(1)}, u32[]{:S(2)}, u32[]{:S(2)}) %collective-permute-start.60) | collective-permute-done | bytes 524320 | tf_op jit(solution)/shard_map/ppermute | solution.py:742
  580.6 38.0 %collective-permute-done.63.refs_1_ = bf16[1,256,512]{2,1,0:T(8,128)(2,1)S(1)} collective-permute-done((bf16[1,256,512]{2,1,0:T(8,128)(2,1)S(1)}, bf16[1,256,512]{2,1,0:T(8,128)(2,1)S(1)}, u32[]{:S(2)}, u32[]{:S(2)}) %collective-permute-start.63) | collective-permute-done | bytes 262176 | tf_op jit(solution)/shard_map/ppermute | solution.py:742
  629.7 17.6 %collective-permute-done.66.refs_1_ = bf16[1,256,512]{2,1,0:T(8,128)(2,1)S(1)} collective-permute-done((bf16[1,256,512]{2,1,0:T(8,128)(2,1)S(1)}, bf16[1,256,512]{2,1,0:T(8,128)(2,1)S(1)}, u32[]{:S(2)}, u32[]{:S(2)}) %collective-permute-start.66) | collective-permute-done | bytes 262176 | tf_op jit(solution)/shard_map/ppermute | solution.py:742
  657.1 6.2 place_ffn.2
  685.7 22.1 %collective-permute-done.74.refs_3_ = bf16[4,576,512]{2,1,0:T(8,128)(2,1)} collective-permute-done((bf16[4,576,512]{2,1,0:T(8,128)(2,1)}, bf16[4,576,512]{2,1,0:T(8,128)(2,1)}, u32[]{:S(2)}, u32[]{:S(2)}) %collective-permute-start.74) | collective-permute-done | bytes 2359328 | tf_op jit(solution)/shard_map/ppermute | solution.py:742
  707.8 6.7 place_ffn.3
  (466 shorter events, 335.4 us)
Async XLA Ops:
  7.0 30.3 %collective-permute-start = (bf16[128,1024]{1,0:T(8,128)(2,1)S(1)}, bf16[128,1024]{1,0:T(8,128)(2,1)S(1)}, u32[]{:S(2)}, u32[]{:S(2)}) collective-permute-start(bf16[128,1024]{1,0:T(8,128)(2,1)S(1)} %copy-done.71), channel_id=1, source_target_pairs={{0,1},{1,0},{2,3},{3,2},{4,5},{5,4},{6,7},{7,6},{8,9},{9,8},{10,11... | collective-permute-start | bytes 786440 | tf_op jit(solution)/shard_map/ppermute | solution.py:727
  12.0 29.6 %collective-permute-start.4 = (bf16[512,512]{1,0:T(8,128)(2,1)}, bf16[512,512]{1,0:T(8,128)(2,1)S(1)}, u32[]{:S(2)}, u32[]{:S(2)}) collective-permute-start(bf16[512,512]{1,0:T(8,128)(2,1)} %take.14.refs_0_), channel_id=1, source_target_pairs={{0,16},{16,0},{1,17},{17,1},{2,18},{18,2},{3,19},{19,3},{4,20},{20... | collective-permute-start | bytes 1572872 | tf_op jit(solution)/shard_map/ppermute | solution.py:727
  47.3 37.1 %all-to-all-start = ((bf16[8,640,128]{2,1,0:T(8,128)(2,1)}), bf16[8,640,128]{2,1,0:T(8,128)(2,1)S(1)}, u32[]{:S(2)}, u32[]{:S(2)}) async-start(bf16[8,640,128]{2,1,0:T(8,128)(2,1)} %get-tuple-element.109), calls=%async_computation | async-start | bytes 2621440 | tf_op jit(solution)/shard_map/all_to_all | solution.py:836
  61.2 50.0 %collective-permute-start.10 = (bf16[3,256,512]{2,1,0:T(8,128)(2,1)}, bf16[3,256,512]{2,1,0:T(8,128)(2,1)S(1)}, u32[]{:S(2)}, u32[]{:S(2)}) collective-permute-start(bf16[3,256,512]{2,1,0:T(8,128)(2,1)} %take.18.refs_0_), channel_id=1, source_target_pairs={{0,16},{16,0},{1,17},{17,1},{2,18},{18,2},{3,19},{19,3},{4,20},{20... | collective-permute-start | bytes 2359304 | tf_op jit(solution)/shard_map/ppermute | solution.py:727
  77.6 30.5 %collective-permute-start.9 = (bf16[512,512]{1,0:T(8,128)(2,1)}, bf16[512,512]{1,0:T(8,128)(2,1)}, u32[]{:S(2)}, u32[]{:S(2)}) collective-permute-start(bf16[512,512]{1,0:T(8,128)(2,1)} %take.17.refs_10_), channel_id=1, source_target_pairs={{0,16},{16,0},{1,17},{17,1},{2,18},{18,2},{3,19},{19,3},{4,20},{20... | collective-permute-start | bytes 1572872 | tf_op jit(solution)/shard_map/ppermute | solution.py:727
  142.1 36.9 %all-to-all-start.2 = ((bf16[8,640,128]{2,1,0:T(8,128)(2,1)}), bf16[8,640,128]{2,1,0:T(8,128)(2,1)}, u32[]{:S(2)}, u32[]{:S(2)}) async-start(bf16[8,640,128]{2,1,0:T(8,128)(2,1)} %get-tuple-element.114), calls=%async_computation.2 | async-start | bytes 2621440 | tf_op jit(solution)/shard_map/all_to_all | solution.py:836
  150.9 52.3 %collective-permute-start.25 = (bf16[3,256,512]{2,1,0:T(8,128)(2,1)}, bf16[3,256,512]{2,1,0:T(8,128)(2,1)}, u32[]{:S(2)}, u32[]{:S(2)}) collective-permute-start(bf16[3,256,512]{2,1,0:T(8,128)(2,1)} %get-tuple-element.116.refs_2_), channel_id=1, source_target_pairs={{0,16},{16,0},{1,17},{17,1},{2,18},{18,2},{3,19},{19,3},{4,20},{20... | collective-permute-start | bytes 2359304 | tf_op jit(solution)/shard_map/ppermute | solution.py:727
  246.5 30.8 %collective-permute-start.35 = (bf16[3,256,512]{2,1,0:T(8,128)(2,1)S(1)}, bf16[3,256,512]{2,1,0:T(8,128)(2,1)S(1)}, u32[]{:S(2)}, u32[]{:S(2)}) collective-permute-start(bf16[3,256,512]{2,1,0:T(8,128)(2,1)S(1)} %copy-done.95), channel_id=1, source_target_pairs={{0,16},{16,0},{1,17},{17,1},{2,18},{18,2},{3,19},{19,3},{4,20},{20... | collective-permute-start | bytes 2359304 | tf_op jit(solution)/shard_map/ppermute | solution.py:727
  247.3 30.0 %collective-permute-start.36 = (bf16[2,256,512]{2,1,0:T(8,128)(2,1)S(1)}, bf16[2,256,512]{2,1,0:T(8,128)(2,1)S(1)}, u32[]{:S(2)}, u32[]{:S(2)}) collective-permute-start(bf16[2,256,512]{2,1,0:T(8,128)(2,1)S(1)} %copy-done.102), channel_id=1, source_target_pairs={{0,16},{16,0},{1,17},{17,1},{2,18},{18,2},{3,19},{19,3},{4,20},{20... | collective-permute-start | bytes 1572872 | tf_op jit(solution)/shard_map/ppermute | solution.py:727
  288.1 47.8 %all-to-all-start.5 = ((bf16[8,640,128]{2,1,0:T(8,128)(2,1)}), bf16[8,640,128]{2,1,0:T(8,128)(2,1)S(1)}, u32[]{:S(2)}, u32[]{:S(2)}) async-start(bf16[8,640,128]{2,1,0:T(8,128)(2,1)} %attend_backward.2.refs_11_), calls=%async_computation.5 | async-start | bytes 2621440 | tf_op jit(solution)/shard_map/all_to_all | solution.py:836
  294.2 29.7 %collective-permute-start.38 = (bf16[3,256,512]{2,1,0:T(8,128)(2,1)S(1)}, bf16[3,256,512]{2,1,0:T(8,128)(2,1)S(1)}, u32[]{:S(2)}, u32[]{:S(2)}) collective-permute-start(bf16[3,256,512]{2,1,0:T(8,128)(2,1)S(1)} %copy-done.96), channel_id=1, source_target_pairs={{0,16},{16,0},{1,17},{17,1},{2,18},{18,2},{3,19},{19,3},{4,20},{20... | collective-permute-start | bytes 2359304 | tf_op jit(solution)/shard_map/ppermute | solution.py:727
  295.1 28.9 %collective-permute-start.37 = (bf16[2,256,512]{2,1,0:T(8,128)(2,1)S(1)}, bf16[2,256,512]{2,1,0:T(8,128)(2,1)S(1)}, u32[]{:S(2)}, u32[]{:S(2)}) collective-permute-start(bf16[2,256,512]{2,1,0:T(8,128)(2,1)S(1)} %copy-done.103), channel_id=1, source_target_pairs={{0,16},{16,0},{1,17},{17,1},{2,18},{18,2},{3,19},{19,3},{4,20},{20... | collective-permute-start | bytes 1572872 | tf_op jit(solution)/shard_map/ppermute | solution.py:727
  365.7 28.9 %collective-permute-start.43 = (bf16[2,512,512]{2,1,0:T(8,128)(2,1)}, bf16[2,512,512]{2,1,0:T(8,128)(2,1)S(1)}, u32[]{:S(2)}, u32[]{:S(2)}) collective-permute-start(bf16[2,512,512]{2,1,0:T(8,128)(2,1)} %get-tuple-element.142), channel_id=1, source_target_pairs={{0,4},{1,3},{2,6},{3,1},{4,0},{5,7},{6,2},{7,5},{8,12},{9,11},{10,... | collective-permute-start | bytes 3145736 | tf_op jit(solution)/shard_map/ppermute | solution.py:742
  367.4 31.4 %collective-permute-start.45 = (bf16[2,256,512]{2,1,0:T(8,128)(2,1)}, bf16[2,256,512]{2,1,0:T(8,128)(2,1)S(1)}, u32[]{:S(2)}, u32[]{:S(2)}) collective-permute-start(bf16[2,256,512]{2,1,0:T(8,128)(2,1)} %get-tuple-element.148.refs_6_), channel_id=1, source_target_pairs={{0,16},{16,0},{1,17},{17,1},{2,18},{18,2},{3,19},{19,3},{4,20},{20... | collective-permute-start | bytes 1572872 | tf_op jit(solution)/shard_map/ppermute | solution.py:727
  408.6 39.9 %all-to-all-start.7 = ((bf16[8,640,128]{2,1,0:T(8,128)(2,1)}), bf16[8,640,128]{2,1,0:T(8,128)(2,1)S(1)}, u32[]{:S(2)}, u32[]{:S(2)}) async-start(bf16[8,640,128]{2,1,0:T(8,128)(2,1)} %attend_backward.3.refs_15_), calls=%async_computation.7 | async-start | bytes 2621440 | tf_op jit(solution)/shard_map/all_to_all | solution.py:836
  456.6 34.6 %collective-permute-start.56 = (bf16[4,576,512]{2,1,0:T(8,128)(2,1)}, bf16[4,576,512]{2,1,0:T(8,128)(2,1)S(1)}, u32[]{:S(2)}, u32[]{:S(2)}) collective-permute-start(bf16[4,576,512]{2,1,0:T(8,128)(2,1)} %get-tuple-element.181), channel_id=1, source_target_pairs={{0,2},{1,5},{2,0},{3,7},{4,6},{5,1},{6,4},{7,3},{8,10},{9,13},{10,... | collective-permute-start | bytes 7077896 | tf_op jit(solution)/shard_map/ppermute | solution.py:742
  467.0 35.0 %collective-permute-start.55 = (bf16[4,256,512]{2,1,0:T(8,128)(2,1)}, bf16[4,256,512]{2,1,0:T(8,128)(2,1)S(1)}, u32[]{:S(2)}, u32[]{:S(2)}) collective-permute-start(bf16[4,256,512]{2,1,0:T(8,128)(2,1)} %get-tuple-element.180), channel_id=1, source_target_pairs={{0,2},{1,5},{2,0},{3,7},{4,6},{5,1},{6,4},{7,3},{8,10},{9,13},{10,... | collective-permute-start | bytes 3145736 | tf_op jit(solution)/shard_map/ppermute | solution.py:742
  489.1 31.1 %collective-permute-start.54 = (bf16[4,208,512]{2,1,0:T(8,128)(2,1)}, bf16[4,208,512]{2,1,0:T(8,128)(2,1)S(1)}, u32[]{:S(2)}, u32[]{:S(2)}) collective-permute-start(bf16[4,208,512]{2,1,0:T(8,128)(2,1)} %get-tuple-element.179), channel_id=1, source_target_pairs={{0,2},{1,3},{2,0},{3,1},{4,6},{5,7},{6,4},{7,5},{8,10},{9,11},{10,... | collective-permute-start | bytes 2555912 | tf_op jit(solution)/shard_map/ppermute | solution.py:742
  490.6 33.0 %collective-permute-start.58 = (bf16[1,512,512]{2,1,0:T(8,128)(2,1)S(1)}, bf16[1,512,512]{2,1,0:T(8,128)(2,1)S(1)}, u32[]{:S(2)}, u32[]{:S(2)}) collective-permute-start(bf16[1,512,512]{2,1,0:T(8,128)(2,1)S(1)} %copy-done), channel_id=1, source_target_pairs={{0,8},{1,9},{2,10},{3,11},{4,12},{5,13},{6,14},{7,15},{8,0},{9,1},... | collective-permute-start | bytes 1572872 | tf_op jit(solution)/shard_map/ppermute | solution.py:742
  496.6 33.4 %collective-permute-start.61 = (bf16[2,576,512]{2,1,0:T(8,128)(2,1)}, bf16[2,576,512]{2,1,0:T(8,128)(2,1)S(1)}, u32[]{:S(2)}, u32[]{:S(2)}) collective-permute-start(bf16[2,576,512]{2,1,0:T(8,128)(2,1)} %get-tuple-element.187), channel_id=1, source_target_pairs={{0,4},{1,3},{2,6},{3,1},{4,0},{5,7},{6,2},{7,5},{8,12},{9,11},{10,... | collective-permute-start | bytes 3538952 | tf_op jit(solution)/shard_map/ppermute | solution.py:742
  526.7 36.9 %collective-permute-start.59 = (bf16[2,512,512]{2,1,0:T(8,128)(2,1)}, bf16[2,512,512]{2,1,0:T(8,128)(2,1)S(1)}, u32[]{:S(2)}, u32[]{:S(2)}) collective-permute-start(bf16[2,512,512]{2,1,0:T(8,128)(2,1)} %join.8.refs_2_), channel_id=1, source_target_pairs={{0,4},{1,3},{2,6},{3,1},{4,0},{5,7},{6,2},{7,5},{8,12},{9,11},{10,... | collective-permute-start | bytes 3145736 | tf_op jit(solution)/shard_map/ppermute | solution.py:742
  528.7 31.9 %collective-permute-start.60 = (bf16[2,256,512]{2,1,0:T(8,128)(2,1)S(1)}, bf16[2,256,512]{2,1,0:T(8,128)(2,1)S(1)}, u32[]{:S(2)}, u32[]{:S(2)}) collective-permute-start(bf16[2,256,512]{2,1,0:T(8,128)(2,1)S(1)} %copy-done.105), channel_id=1, source_target_pairs={{0,4},{1,3},{2,6},{3,1},{4,0},{5,7},{6,2},{7,5},{8,12},{9,11},{10,... | collective-permute-start | bytes 1572872 | tf_op jit(solution)/shard_map/ppermute | solution.py:742
  533.7 40.8 %collective-permute-start.64 = (bf16[1,576,512]{2,1,0:T(8,128)(2,1)}, bf16[1,576,512]{2,1,0:T(8,128)(2,1)S(1)}, u32[]{:S(2)}, u32[]{:S(2)}) collective-permute-start(bf16[1,576,512]{2,1,0:T(8,128)(2,1)} %get-tuple-element.193), channel_id=1, source_target_pairs={{0,8},{1,9},{2,10},{3,11},{4,12},{5,13},{6,14},{7,15},{8,0},{9,1},... | collective-permute-start | bytes 1769480 | tf_op jit(solution)/shard_map/ppermute | solution.py:742
  535.3 36.6 %collective-permute-start.57 = (bf16[2,208,512]{2,1,0:T(8,128)(2,1)S(1)}, bf16[2,208,512]{2,1,0:T(8,128)(2,1)S(1)}, u32[]{:S(2)}, u32[]{:S(2)}) collective-permute-start(bf16[2,208,512]{2,1,0:T(8,128)(2,1)S(1)} %copy-done.107), channel_id=1, source_target_pairs={{0,4},{1,5},{2,6},{3,7},{4,0},{5,1},{6,2},{7,3},{8,12},{9,13},{10,... | collective-permute-start | bytes 1277960 | tf_op jit(solution)/shard_map/ppermute | solution.py:742
  567.5 88.2 %collective-permute-start.70 = (bf16[4,512,512]{2,1,0:T(8,128)(2,1)}, bf16[4,512,512]{2,1,0:T(8,128)(2,1)S(1)}, u32[]{:S(2)}, u32[]{:S(2)}) collective-permute-start(bf16[4,512,512]{2,1,0:T(8,128)(2,1)} %join.9.refs_2_), channel_id=1, source_target_pairs={{0,2},{1,5},{2,0},{3,7},{4,6},{5,1},{6,4},{7,3},{8,10},{9,13},{10,... | collective-permute-start | bytes 6291464 | tf_op jit(solution)/shard_map/ppermute | solution.py:742
  577.5 46.0 %collective-permute-start.67 = (bf16[1,576,512]{2,1,0:T(8,128)(2,1)}, bf16[1,576,512]{2,1,0:T(8,128)(2,1)S(1)}, u32[]{:S(2)}, u32[]{:S(2)}) collective-permute-start(bf16[1,576,512]{2,1,0:T(8,128)(2,1)} %fold.21.refs_2_.refs_0_), channel_id=1, source_target_pairs={{0,8},{1,9},{2,10},{3,11},{4,12},{5,13},{6,14},{7,15},{8,0},{9,1},... | collective-permute-start | bytes 1769480 | tf_op jit(solution)/shard_map/ppermute | solution.py:742
  577.7 41.0 %collective-permute-start.63 = (bf16[1,256,512]{2,1,0:T(8,128)(2,1)S(1)}, bf16[1,256,512]{2,1,0:T(8,128)(2,1)S(1)}, u32[]{:S(2)}, u32[]{:S(2)}) collective-permute-start(bf16[1,256,512]{2,1,0:T(8,128)(2,1)S(1)} %copy-done.114), channel_id=1, source_target_pairs={{0,8},{1,9},{2,10},{3,11},{4,12},{5,13},{6,14},{7,15},{8,0},{9,1},... | collective-permute-start | bytes 786440 | tf_op jit(solution)/shard_map/ppermute | solution.py:742
  580.5 40.7 %collective-permute-start.62 = (bf16[1,208,512]{2,1,0:T(8,128)(2,1)}, bf16[1,208,512]{2,1,0:T(8,128)(2,1)S(1)}, u32[]{:S(2)}, u32[]{:S(2)}) collective-permute-start(bf16[1,208,512]{2,1,0:T(8,128)(2,1)} %get-tuple-element.191), channel_id=1, source_target_pairs={{0,8},{1,9},{2,10},{3,11},{4,12},{5,13},{6,14},{7,15},{8,0},{9,1},... | collective-permute-start | bytes 638984 | tf_op jit(solution)/shard_map/ppermute | solution.py:742
  626.8 47.2 %collective-permute-start.73 = (bf16[2,576,512]{2,1,0:T(8,128)(2,1)}, bf16[2,576,512]{2,1,0:T(8,128)(2,1)S(1)}, u32[]{:S(2)}, u32[]{:S(2)}) collective-permute-start(bf16[2,576,512]{2,1,0:T(8,128)(2,1)} %join.10.refs_2_), channel_id=1, source_target_pairs={{0,4},{1,3},{2,6},{3,1},{4,0},{5,7},{6,2},{7,5},{8,12},{9,11},{10,... | collective-permute-start | bytes 3538952 | tf_op jit(solution)/shard_map/ppermute | solution.py:742
  678.6 29.2 %collective-permute-start.74 = (bf16[4,576,512]{2,1,0:T(8,128)(2,1)}, bf16[4,576,512]{2,1,0:T(8,128)(2,1)}, u32[]{:S(2)}, u32[]{:S(2)}) collective-permute-start(bf16[4,576,512]{2,1,0:T(8,128)(2,1)} %join.15.refs_6_), channel_id=1, source_target_pairs={{0,2},{1,5},{2,0},{3,7},{4,6},{5,1},{6,4},{7,3},{8,10},{9,13},{10,... | collective-permute-start | bytes 7077896 | tf_op jit(solution)/shard_map/ppermute | solution.py:742
  680.0 39.0 %collective-permute-start.72 = (bf16[4,256,512]{2,1,0:T(8,128)(2,1)S(1)}, bf16[4,256,512]{2,1,0:T(8,128)(2,1)}, u32[]{:S(2)}, u32[]{:S(2)}) collective-permute-start(bf16[4,256,512]{2,1,0:T(8,128)(2,1)S(1)} %copy-done.17), channel_id=1, source_target_pairs={{0,2},{1,5},{2,0},{3,7},{4,6},{5,1},{6,4},{7,3},{8,10},{9,13},{10,... | collective-permute-start | bytes 3145736 | tf_op jit(solution)/shard_map/ppermute | solution.py:742
  680.6 47.5 %collective-permute-start.71 = (bf16[4,208,512]{2,1,0:T(8,128)(2,1)S(1)}, bf16[4,208,512]{2,1,0:T(8,128)(2,1)}, u32[]{:S(2)}, u32[]{:S(2)}) collective-permute-start(bf16[4,208,512]{2,1,0:T(8,128)(2,1)S(1)} %copy-done.18), channel_id=1, source_target_pairs={{0,2},{1,3},{2,0},{3,1},{4,6},{5,7},{6,4},{7,5},{8,10},{9,11},{10,... | collective-permute-start | bytes 2555912 | tf_op jit(solution)/shard_map/ppermute | solution.py:742
  (169 other events, 1540.7 us)

commit v6 on v5

--- a/solution.py
+++ b/solution.py
@@ -582,7 +582,7 @@
 
 
 def shift_at(d, mix):
-    return SHIFT if mix else SHIFT + d.bits
+    return SHIFT + d.bits * (2 if mix == "z" else 0 if mix else 1)
 
 
 def wgrad_body(d, tiles, mix, flat, sc, *refs):
@@ -729,7 +729,7 @@
 
 def way(d, core, step, mix=True):
     if mix and step < 2 and d.bits > 1:
-        return step if core == 0 else 1 - step
+        return step if core == 0 and mix != "z" else 1 - step
     return step
 
 
@@ -862,7 +862,8 @@
     t = lax.axis_index("tp")
     first = [jnp.where(t == 0, way(d, 0, k), way(d, 1, k)) for k in range(d.bits)]
     bit = (c >> first[0]) % 2
-    sc = jnp.stack([x, bit, c, *first, *range(d.bits)]).astype(jnp.int32)
+    turned = [way(d, 0, k, "z") for k in range(d.bits)]
+    sc = jnp.stack([x, bit, c, *first, *range(d.bits), *turned]).astype(jnp.int32)
     w_qkv = qkv_weight.transpose(0, 2, 1, 3)
     tiles = d.F // FT
     half = tiles // 2
@@ -1032,7 +1033,7 @@
     part = back_ffn(0, k0, grad)
     a = f1.step(part)
     dchunks = back_context(0, k0, grad, part, (a, k1.xc_r))
-    q1 = grad_qkv(k1, True, True, None, (dchunks,))
+    q1 = grad_qkv(k1, True, False, None, (dchunks,))
     a = f1.step(q1.keep)
     dback = attend_backward(d, sc, kb, k0.chunks, all_to_all(dchunks),
                             deps=(a, k0.xba_r, k0.ctx_r, k0.n_r))
@@ -1043,7 +1044,7 @@
     flat = small_sums()
     flat = flat + swap(flat, "fsdp")
     a = f1.step(grad)
-    q0 = grad_qkv(k0, False, False, flat, (a,))
+    q0 = grad_qkv(k0, False, "z", flat, (a,))
     a = q0.keep
     ffn_kinds = (("cols", tiles), ("mats", tiles))
     qkv_kinds = (("mats", 3), ("mats", 1))

time: 743 us -> 758 us (1.020)
  starting transfers between devices: 123 us -> 142 us
    ppermute x36, starting transfers between devices: 47.9 us -> 67 us  [cross(): return lax.ppermute(values, ('ctx', 'tp'), pairs)]
  transfers between devices with their start and end apart: 83 -> 83, of which waited for: 39 -> 37; matrix products, arithmetic and copies ran while one was open for 2% -> 2% of each run, Pallas kernels for 26% -> 26%
where the time goes in v6:
time: 758 us; the launch traced here: 747 us
  waiting for transfers between devices  308 us (41%)
  Pallas kernels  243 us (32%)
  starting transfers between devices  142 us (19%)
  local copies, waits for them, and re-layouts  45.9 us (6%)
    pallas_call x42, Pallas kernels, kernel_call(): pl.pallas_call(ordered, in_specs=list(in_specs) + [pl.BlockSpec(memory_sp...  192 us
    ppermute x36, waiting for transfers between devices, cross(): return lax.ppermute(values, ('ctx', 'tp'), pairs)  180 us
    ppermute x39, waiting for transfers between devices, swap(): return lax.ppermute(values, axis, [(0, 1), (1, 0)])  118 us
    ppermute x36, starting transfers between devices, cross(): return lax.ppermute(values, ('ctx', 'tp'), pairs)  67 us
    all_to_all x8, starting transfers between devices, all_to_all(): return lax.all_to_all(values, 'ctx', 0, 0)  40.9 us
    unnamed x253, local copies, waits for them, and re-layouts  40.8 us
    ppermute x39, starting transfers between devices, swap(): return lax.ppermute(values, axis, [(0, 1), (1, 0)])  33.7 us
    pallas_call x12, Pallas kernels, take(): pl.pallas_call(take_body, grid_spec=pltpu.PrefetchScalarGridSpec(num_scal...  30.7 us
  transfers between devices with their start and end apart: 83, of which 37 were waited for; matrix products, arithmetic and copies ran while one was open for 2% of the time, Pallas kernels for 26%

profile of v6, /device:TPU:0, one launch (start us, length us, event | category | flops | bytes accessed | tf_op | source)
XLA Modules:
  0.0 746.9 jit_solution(11445859413003508)
XLA Ops:
  13.9 11.7 %collective-permute-done.1.refs_5_.refs_2_ = bf16[3,256,512]{2,1,0:T(8,128)(2,1)S(1)} collective-permute-done((bf16[3,256,512]{2,1,0:T(8,128)(2,1)}, bf16[3,256,512]{2,1,0:T(8,128)(2,1)S(1)}, u32[]{:S(2)}, u32[]{:S(2)}) %collective-permute-start.1) | collective-permute-done | bytes 786464 | tf_op jit(solution)/shard_map/ppermute | solution.py:727
  47.3 6.2 all-to-all-start
  98.0 10.0 %collective-permute-done.9.refs_5_.refs_16_.refs_11_ = bf16[512,512]{1,0:T(8,128)(2,1)} collective-permute-done((bf16[512,512]{1,0:T(8,128)(2,1)}, bf16[512,512]{1,0:T(8,128)(2,1)}, u32[]{:S(2)}, u32[]{:S(2)}) %collective-permute-start.9) | collective-permute-done | bytes 524320 | tf_op jit(solution)/shard_map/ppermute | solution.py:727
  120.7 12.0 %ffn_forward.2 = (f32[256,1024]{1,0:T(8,128)}, bf16[256,512]{1,0:T(8,128)(2,1)}, bf16[3,256,512]{2,1,0:T(8,128)(2,1)}, bf16[2,256,512]{2,1,0:T(8,128)(2,1)}, bf1...) custom-call(s32[12]{0:T(128)} %stack.24.sc.refs_0_, f32[256,1024]{1,0:T(8,128)} %get-tuple-element.108.refs_0_.refs_1_.refs_3_, ...), custom_call_target="tpu_custom_call" | custom-call | flops 2147483648 | bytes 14000000 | tf_op jit(solution)/shard_map/ffn_forward/pallas_call | solution.py:51
  151.7 20.6 %collective-permute-done.19.refs_3_.refs_8_ = bf16[256,512]{1,0:T(8,128)(2,1)S(1)} collective-permute-done((bf16[256,512]{1,0:T(8,128)(2,1)S(1)}, bf16[256,512]{1,0:T(8,128)(2,1)S(1)}, u32[]{:S(2)}, u32[]{:S(2)}) %collective-permute-start.19) | collective-permute-done | bytes 262176 | tf_op jit(solution)/shard_map/ppermute | solution.py:742
  173.1 5.9 all-to-all-done.2.refs_2_
  189.1 12.0 %collective-permute-done.23.refs_5_.refs_16_.refs_11_ = bf16[512,512]{1,0:T(8,128)(2,1)S(1)} collective-permute-done((bf16[512,512]{1,0:T(8,128)(2,1)S(1)}, bf16[512,512]{1,0:T(8,128)(2,1)S(1)}, u32[]{:S(2)}, u32[]{:S(2)}) %collective-permute-start.23) | collective-permute-done | bytes 524320 | tf_op jit(solution)/shard_map/ppermute | solution.py:727
  215.9 5.6 collective-permute-done.27.refs_11_.refs_7_
  222.6 12.0 %ffn_forward.3 = (f32[256,1024]{1,0:T(8,128)}, bf16[256,512]{1,0:T(8,128)(2,1)}, bf16[3,256,512]{2,1,0:T(8,128)(2,1)}, bf16[2,256,512]{2,1,0:T(8,128)(2,1)}, bf1...) custom-call(s32[12]{0:T(128)} %stack.24.sc.refs_0_, f32[256,1024]{1,0:T(8,128)} %get-tuple-element.113.refs_1_.refs_3_, ...), custom_call_target="tpu_custom_call" | custom-call | flops 2147483648 | bytes 14000000 | tf_op jit(solution)/shard_map/ffn_forward/pallas_call | solution.py:51
  235.5 10.4 %ffn_backward.2 = (bf16[256,512]{1,0:T(8,128)(2,1)}, bf16[2,256,512]{2,1,0:T(8,128)(2,1)}, bf16[3,256,512]{2,1,0:T(8,128)(2,1)}, f32[1,2048]{1,0:T(1,128)}, f32[...) custom-call(s32[12]{0:T(128)} %stack.24.sc.refs_0_, bf16[256,1024]{1,0:T(8,128)(2,1)} %maximum_select_fusion.1.refs_1_, ...), custom_call_target="tpu_custom_call" | custom-call | flops 2147483648 | bytes 14000000 | tf_op jit(solution)/shard_map/ffn_backward/pallas_call | solution.py:51
  253.7 6.4 all-to-all-start.4
  260.1 17.2 %collective-permute-done.36.refs_5_ = bf16[2,256,512]{2,1,0:T(8,128)(2,1)S(1)} collective-permute-done((bf16[2,256,512]{2,1,0:T(8,128)(2,1)S(1)}, bf16[2,256,512]{2,1,0:T(8,128)(2,1)S(1)}, u32[]{:S(2)}, u32[]{:S(2)}) %collective-permute-start.36) | collective-permute-done | bytes 524320 | tf_op jit(solution)/shard_map/ppermute | solution.py:727
  279.2 8.9 %attend_backward.2.refs_11_ = bf16[8,640,128]{2,1,0:T(8,128)(2,1)} custom-call(s32[12]{0:T(128)} %stack.24.sc.refs_0_, f32[16,2048]{1,0:T(8,128)} %bitcast_add_fusion.refs_1_, bf16[8,640,128]{2,1,0:T(8,128)(2,1)} %all-to-all-done.2.refs_2_, bf16[8,128,128]{2,1,0:T(8,128)(2,1)} %copy-done.70, bf16[3,256,512]{2,1,0:T(8,128)(2,1)} %copy-done.97, ...), custom_call_target="tpu_custom_call" | custom-call | flops 2684354560 | bytes 4000000 | tf_op jit(solution)/shard_map/attend_backward/pallas_call | solution.py:51
  288.1 6.1 all-to-all-start.5
  296.3 27.6 %collective-permute-done.37.refs_7_ = bf16[2,256,512]{2,1,0:T(8,128)(2,1)S(1)} collective-permute-done((bf16[2,256,512]{2,1,0:T(8,128)(2,1)S(1)}, bf16[2,256,512]{2,1,0:T(8,128)(2,1)S(1)}, u32[]{:S(2)}, u32[]{:S(2)}) %collective-permute-start.37) | collective-permute-done | bytes 524320 | tf_op jit(solution)/shard_map/ppermute | solution.py:727
  325.0 9.2 %weight_grad_ffn.2 = (bf16[4,512,512]{2,1,0:T(8,128)(2,1)}, bf16[4,512,512]{2,1,0:T(8,128)(2,1)}) custom-call(s32[12]{0:T(128)} %stack.24.sc.refs_0_, bf16[256,512]{1,0:T(8,128)(2,1)} %get-tuple-element.128.refs_1_, bf16[3,256,512]{2,1,0:T(8,128)(2,1)} %get-tuple-element.126.refs_2_, bf16[3,256,512]{2,1,0:T(8,128)(2,1)} %copy-done.97, ...), custom_call_target="tpu_custom_call" | custom-call | flops 2147483648 | bytes 8000000 | tf_op jit(solution)/shard_map/weight_grad_ffn/pallas_call | solution.py:51
  347.6 10.5 %ffn_backward.3 = (bf16[256,512]{1,0:T(8,128)(2,1)}, bf16[2,256,512]{2,1,0:T(8,128)(2,1)}, bf16[3,256,512]{2,1,0:T(8,128)(2,1)}, f32[1,2048]{1,0:T(1,128)}, f32[...) custom-call(s32[12]{0:T(128)} %stack.24.sc.refs_0_, f32[256,1024]{1,0:T(8,128)} %get-tuple-element.134.refs_1_, ...), custom_call_target="tpu_custom_call" | custom-call | flops 2147483648 | bytes 14000000 | tf_op jit(solution)/shard_map/ffn_backward/pallas_call | solution.py:51
  381.8 6.4 collective-permute-done.44.refs_8_
  389.0 5.6 weight_grad_qkv.2
  399.7 8.9 %attend_backward.3.refs_15_ = bf16[8,640,128]{2,1,0:T(8,128)(2,1)} custom-call(s32[12]{0:T(128)} %stack.24.sc.refs_0_, f32[16,2048]{1,0:T(8,128)} %bitcast_add_fusion.refs_1_, bf16[8,640,128]{2,1,0:T(8,128)(2,1)} %copy-done.6, bf16[8,128,128]{2,1,0:T(8,128)(2,1)} %copy-done.69, bf16[1,512,512]{2,1,0:T(8,128)(2,1)} %get-tuple-element.147.refs_4_.refs_0_, ...), custom_call_target="tpu_custom_call" | custom-call | flops 2684354560 | bytes 4000000 | tf_op jit(solution)/shard_map/attend_backward/pallas_call | solution.py:51
  416.3 18.4 %collective-permute-done.48.refs_9_ = bf16[3,256,512]{2,1,0:T(8,128)(2,1)S(1)} collective-permute-done((bf16[3,256,512]{2,1,0:T(8,128)(2,1)S(1)}, bf16[3,256,512]{2,1,0:T(8,128)(2,1)S(1)}, u32[]{:S(2)}, u32[]{:S(2)}) %collective-permute-start.48) | collective-permute-done | bytes 786464 | tf_op jit(solution)/shard_map/ppermute | solution.py:727
  438.2 10.3 %weight_grad_ffn.3 = (bf16[4,576,512]{2,1,0:T(8,128)(2,1)}, bf16[4,576,512]{2,1,0:T(8,128)(2,1)}) custom-call(s32[12]{0:T(128)} %stack.24.sc.refs_0_, bf16[256,512]{1,0:T(8,128)(2,1)} %get-tuple-element.151.refs_1_, bf16[3,256,512]{2,1,0:T(8,128)(2,1)} %get-tuple-element.116.refs_2_, bf16[3,256,512]{2,1,0:T(8,128)(2,1)} %collective-permute-done.25.refs_7_.refs_3_, ...), custom_call_target="tpu_custom_call" | custom-call | flops 2415919104 | bytes 8000000 | tf_op jit(solution)/shard_map/weight_grad_ffn/pallas_call | solution.py:51
  467.5 13.1 %collective-permute-done.53.refs_1_ = bf16[1,512,512]{2,1,0:T(8,128)(2,1)S(1)} collective-permute-done((bf16[1,512,512]{2,1,0:T(8,128)(2,1)}, bf16[1,512,512]{2,1,0:T(8,128)(2,1)S(1)}, u32[]{:S(2)}, u32[]{:S(2)}) %collective-permute-start.53) | collective-permute-done | bytes 524320 | tf_op jit(solution)/shard_map/ppermute | solution.py:742
  511.7 10.8 %collective-permute-done.54.refs_1_ = bf16[4,208,512]{2,1,0:T(8,128)(2,1)S(1)} collective-permute-done((bf16[4,208,512]{2,1,0:T(8,128)(2,1)}, bf16[4,208,512]{2,1,0:T(8,128)(2,1)S(1)}, u32[]{:S(2)}, u32[]{:S(2)}) %collective-permute-start.54) | collective-permute-done | bytes 852000 | tf_op jit(solution)/shard_map/ppermute | solution.py:742
  530.9 6.4 collective-permute-done.61.refs_1_
  545.6 27.8 %collective-permute-done.60.refs_1_ = bf16[2,256,512]{2,1,0:T(8,128)(2,1)S(1)} collective-permute-done((bf16[2,256,512]{2,1,0:T(8,128)(2,1)S(1)}, bf16[2,256,512]{2,1,0:T(8,128)(2,1)S(1)}, u32[]{:S(2)}, u32[]{:S(2)}) %collective-permute-start.60) | collective-permute-done | bytes 524320 | tf_op jit(solution)/shard_map/ppermute | solution.py:742
  589.1 13.2 %collective-permute-start.67 = (bf16[1,576,512]{2,1,0:T(8,128)(2,1)}, bf16[1,576,512]{2,1,0:T(8,128)(2,1)S(1)}, u32[]{:S(2)}, u32[]{:S(2)}) collective-permute-start(bf16[1,576,512]{2,1,0:T(8,128)(2,1)} %fold.21.refs_2_.refs_0_), channel_id=1, source_target_pairs={{0,8},{1,9},{2,10},{3,11},{4,12},{5,13},{6,14},{7,15},{8,0},{9,1},... | collective-permute-start | bytes 1769480 | tf_op jit(solution)/shard_map/ppermute | solution.py:742
  605.2 32.6 %collective-permute-done.63.refs_1_ = bf16[1,256,512]{2,1,0:T(8,128)(2,1)S(1)} collective-permute-done((bf16[1,256,512]{2,1,0:T(8,128)(2,1)S(1)}, bf16[1,256,512]{2,1,0:T(8,128)(2,1)S(1)}, u32[]{:S(2)}, u32[]{:S(2)}) %collective-permute-start.63) | collective-permute-done | bytes 262176 | tf_op jit(solution)/shard_map/ppermute | solution.py:742
  648.9 19.6 %collective-permute-done.66.refs_1_ = bf16[1,256,512]{2,1,0:T(8,128)(2,1)S(1)} collective-permute-done((bf16[1,256,512]{2,1,0:T(8,128)(2,1)S(1)}, bf16[1,256,512]{2,1,0:T(8,128)(2,1)S(1)}, u32[]{:S(2)}, u32[]{:S(2)}) %collective-permute-start.66) | collective-permute-done | bytes 262176 | tf_op jit(solution)/shard_map/ppermute | solution.py:742
  679.7 6.2 place_ffn.2
  705.9 21.4 %collective-permute-done.74.refs_3_ = bf16[4,576,512]{2,1,0:T(8,128)(2,1)} collective-permute-done((bf16[4,576,512]{2,1,0:T(8,128)(2,1)}, bf16[4,576,512]{2,1,0:T(8,128)(2,1)}, u32[]{:S(2)}, u32[]{:S(2)}) %collective-permute-start.74) | collective-permute-done | bytes 2359328 | tf_op jit(solution)/shard_map/ppermute | solution.py:742
  727.3 6.7 place_ffn.3
  (466 shorter events, 344.9 us)
Async XLA Ops:
  7.0 30.3 %collective-permute-start = (bf16[128,1024]{1,0:T(8,128)(2,1)S(1)}, bf16[128,1024]{1,0:T(8,128)(2,1)S(1)}, u32[]{:S(2)}, u32[]{:S(2)}) collective-permute-start(bf16[128,1024]{1,0:T(8,128)(2,1)S(1)} %copy-done.71), channel_id=1, source_target_pairs={{0,1},{1,0},{2,3},{3,2},{4,5},{5,4},{6,7},{7,6},{8,9},{9,8},{10,11... | collective-permute-start | bytes 786440 | tf_op jit(solution)/shard_map/ppermute | solution.py:727
  12.0 29.6 %collective-permute-start.4 = (bf16[512,512]{1,0:T(8,128)(2,1)}, bf16[512,512]{1,0:T(8,128)(2,1)S(1)}, u32[]{:S(2)}, u32[]{:S(2)}) collective-permute-start(bf16[512,512]{1,0:T(8,128)(2,1)} %take.14.refs_0_), channel_id=1, source_target_pairs={{0,16},{16,0},{1,17},{17,1},{2,18},{18,2},{3,19},{19,3},{4,20},{20... | collective-permute-start | bytes 1572872 | tf_op jit(solution)/shard_map/ppermute | solution.py:727
  47.3 37.1 %all-to-all-start = ((bf16[8,640,128]{2,1,0:T(8,128)(2,1)}), bf16[8,640,128]{2,1,0:T(8,128)(2,1)S(1)}, u32[]{:S(2)}, u32[]{:S(2)}) async-start(bf16[8,640,128]{2,1,0:T(8,128)(2,1)} %get-tuple-element.109), calls=%async_computation | async-start | bytes 2621440 | tf_op jit(solution)/shard_map/all_to_all | solution.py:836
  61.2 50.0 %collective-permute-start.10 = (bf16[3,256,512]{2,1,0:T(8,128)(2,1)}, bf16[3,256,512]{2,1,0:T(8,128)(2,1)S(1)}, u32[]{:S(2)}, u32[]{:S(2)}) collective-permute-start(bf16[3,256,512]{2,1,0:T(8,128)(2,1)} %take.18.refs_0_), channel_id=1, source_target_pairs={{0,16},{16,0},{1,17},{17,1},{2,18},{18,2},{3,19},{19,3},{4,20},{20... | collective-permute-start | bytes 2359304 | tf_op jit(solution)/shard_map/ppermute | solution.py:727
  77.6 30.5 %collective-permute-start.9 = (bf16[512,512]{1,0:T(8,128)(2,1)}, bf16[512,512]{1,0:T(8,128)(2,1)}, u32[]{:S(2)}, u32[]{:S(2)}) collective-permute-start(bf16[512,512]{1,0:T(8,128)(2,1)} %take.17.refs_10_), channel_id=1, source_target_pairs={{0,16},{16,0},{1,17},{17,1},{2,18},{18,2},{3,19},{19,3},{4,20},{20... | collective-permute-start | bytes 1572872 | tf_op jit(solution)/shard_map/ppermute | solution.py:727
  142.1 36.9 %all-to-all-start.2 = ((bf16[8,640,128]{2,1,0:T(8,128)(2,1)}), bf16[8,640,128]{2,1,0:T(8,128)(2,1)}, u32[]{:S(2)}, u32[]{:S(2)}) async-start(bf16[8,640,128]{2,1,0:T(8,128)(2,1)} %get-tuple-element.114), calls=%async_computation.2 | async-start | bytes 2621440 | tf_op jit(solution)/shard_map/all_to_all | solution.py:836
  150.9 52.3 %collective-permute-start.25 = (bf16[3,256,512]{2,1,0:T(8,128)(2,1)}, bf16[3,256,512]{2,1,0:T(8,128)(2,1)}, u32[]{:S(2)}, u32[]{:S(2)}) collective-permute-start(bf16[3,256,512]{2,1,0:T(8,128)(2,1)} %get-tuple-element.116.refs_2_), channel_id=1, source_target_pairs={{0,16},{16,0},{1,17},{17,1},{2,18},{18,2},{3,19},{19,3},{4,20},{20... | collective-permute-start | bytes 2359304 | tf_op jit(solution)/shard_map/ppermute | solution.py:727
  246.5 30.8 %collective-permute-start.35 = (bf16[3,256,512]{2,1,0:T(8,128)(2,1)S(1)}, bf16[3,256,512]{2,1,0:T(8,128)(2,1)S(1)}, u32[]{:S(2)}, u32[]{:S(2)}) collective-permute-start(bf16[3,256,512]{2,1,0:T(8,128)(2,1)S(1)} %copy-done.95), channel_id=1, source_target_pairs={{0,16},{16,0},{1,17},{17,1},{2,18},{18,2},{3,19},{19,3},{4,20},{20... | collective-permute-start | bytes 2359304 | tf_op jit(solution)/shard_map/ppermute | solution.py:727
  247.3 30.0 %collective-permute-start.36 = (bf16[2,256,512]{2,1,0:T(8,128)(2,1)S(1)}, bf16[2,256,512]{2,1,0:T(8,128)(2,1)S(1)}, u32[]{:S(2)}, u32[]{:S(2)}) collective-permute-start(bf16[2,256,512]{2,1,0:T(8,128)(2,1)S(1)} %copy-done.102), channel_id=1, source_target_pairs={{0,16},{16,0},{1,17},{17,1},{2,18},{18,2},{3,19},{19,3},{4,20},{20... | collective-permute-start | bytes 1572872 | tf_op jit(solution)/shard_map/ppermute | solution.py:727
  288.1 47.8 %all-to-all-start.5 = ((bf16[8,640,128]{2,1,0:T(8,128)(2,1)}), bf16[8,640,128]{2,1,0:T(8,128)(2,1)S(1)}, u32[]{:S(2)}, u32[]{:S(2)}) async-start(bf16[8,640,128]{2,1,0:T(8,128)(2,1)} %attend_backward.2.refs_11_), calls=%async_computation.5 | async-start | bytes 2621440 | tf_op jit(solution)/shard_map/all_to_all | solution.py:836
  294.2 29.7 %collective-permute-start.38 = (bf16[3,256,512]{2,1,0:T(8,128)(2,1)S(1)}, bf16[3,256,512]{2,1,0:T(8,128)(2,1)S(1)}, u32[]{:S(2)}, u32[]{:S(2)}) collective-permute-start(bf16[3,256,512]{2,1,0:T(8,128)(2,1)S(1)} %copy-done.96), channel_id=1, source_target_pairs={{0,16},{16,0},{1,17},{17,1},{2,18},{18,2},{3,19},{19,3},{4,20},{20... | collective-permute-start | bytes 2359304 | tf_op jit(solution)/shard_map/ppermute | solution.py:727
  295.1 28.9 %collective-permute-start.37 = (bf16[2,256,512]{2,1,0:T(8,128)(2,1)S(1)}, bf16[2,256,512]{2,1,0:T(8,128)(2,1)S(1)}, u32[]{:S(2)}, u32[]{:S(2)}) collective-permute-start(bf16[2,256,512]{2,1,0:T(8,128)(2,1)S(1)} %copy-done.103), channel_id=1, source_target_pairs={{0,16},{16,0},{1,17},{17,1},{2,18},{18,2},{3,19},{19,3},{4,20},{20... | collective-permute-start | bytes 1572872 | tf_op jit(solution)/shard_map/ppermute | solution.py:727
  365.7 28.9 %collective-permute-start.43 = (bf16[2,512,512]{2,1,0:T(8,128)(2,1)}, bf16[2,512,512]{2,1,0:T(8,128)(2,1)S(1)}, u32[]{:S(2)}, u32[]{:S(2)}) collective-permute-start(bf16[2,512,512]{2,1,0:T(8,128)(2,1)} %get-tuple-element.142), channel_id=1, source_target_pairs={{0,4},{1,3},{2,6},{3,1},{4,0},{5,7},{6,2},{7,5},{8,12},{9,11},{10,... | collective-permute-start | bytes 3145736 | tf_op jit(solution)/shard_map/ppermute | solution.py:742
  367.4 31.4 %collective-permute-start.45 = (bf16[2,256,512]{2,1,0:T(8,128)(2,1)}, bf16[2,256,512]{2,1,0:T(8,128)(2,1)S(1)}, u32[]{:S(2)}, u32[]{:S(2)}) collective-permute-start(bf16[2,256,512]{2,1,0:T(8,128)(2,1)} %get-tuple-element.148.refs_6_), channel_id=1, source_target_pairs={{0,16},{16,0},{1,17},{17,1},{2,18},{18,2},{3,19},{19,3},{4,20},{20... | collective-permute-start | bytes 1572872 | tf_op jit(solution)/shard_map/ppermute | solution.py:727
  408.6 39.9 %all-to-all-start.7 = ((bf16[8,640,128]{2,1,0:T(8,128)(2,1)}), bf16[8,640,128]{2,1,0:T(8,128)(2,1)S(1)}, u32[]{:S(2)}, u32[]{:S(2)}) async-start(bf16[8,640,128]{2,1,0:T(8,128)(2,1)} %attend_backward.3.refs_15_), calls=%async_computation.7 | async-start | bytes 2621440 | tf_op jit(solution)/shard_map/all_to_all | solution.py:836
  456.6 40.3 %collective-permute-start.56 = (bf16[4,576,512]{2,1,0:T(8,128)(2,1)}, bf16[4,576,512]{2,1,0:T(8,128)(2,1)S(1)}, u32[]{:S(2)}, u32[]{:S(2)}) collective-permute-start(bf16[4,576,512]{2,1,0:T(8,128)(2,1)} %get-tuple-element.181), channel_id=1, source_target_pairs={{0,2},{1,5},{2,0},{3,7},{4,6},{5,1},{6,4},{7,3},{8,10},{9,13},{10,... | collective-permute-start | bytes 7077896 | tf_op jit(solution)/shard_map/ppermute | solution.py:742
  467.0 41.1 %collective-permute-start.55 = (bf16[4,256,512]{2,1,0:T(8,128)(2,1)}, bf16[4,256,512]{2,1,0:T(8,128)(2,1)S(1)}, u32[]{:S(2)}, u32[]{:S(2)}) collective-permute-start(bf16[4,256,512]{2,1,0:T(8,128)(2,1)} %get-tuple-element.180), channel_id=1, source_target_pairs={{0,2},{1,3},{2,0},{3,1},{4,6},{5,7},{6,4},{7,5},{8,10},{9,11},{10,... | collective-permute-start | bytes 3145736 | tf_op jit(solution)/shard_map/ppermute | solution.py:742
  489.1 33.3 %collective-permute-start.54 = (bf16[4,208,512]{2,1,0:T(8,128)(2,1)}, bf16[4,208,512]{2,1,0:T(8,128)(2,1)S(1)}, u32[]{:S(2)}, u32[]{:S(2)}) collective-permute-start(bf16[4,208,512]{2,1,0:T(8,128)(2,1)} %get-tuple-element.179), channel_id=1, source_target_pairs={{0,4},{1,5},{2,6},{3,7},{4,0},{5,1},{6,2},{7,3},{8,12},{9,13},{10,... | collective-permute-start | bytes 2555912 | tf_op jit(solution)/shard_map/ppermute | solution.py:742
  489.7 36.1 %collective-permute-start.58 = (bf16[1,512,512]{2,1,0:T(8,128)(2,1)S(1)}, bf16[1,512,512]{2,1,0:T(8,128)(2,1)S(1)}, u32[]{:S(2)}, u32[]{:S(2)}) collective-permute-start(bf16[1,512,512]{2,1,0:T(8,128)(2,1)S(1)} %copy-done), channel_id=1, source_target_pairs={{0,8},{1,9},{2,10},{3,11},{4,12},{5,13},{6,14},{7,15},{8,0},{9,1},... | collective-permute-start | bytes 1572872 | tf_op jit(solution)/shard_map/ppermute | solution.py:742
  502.3 35.1 %collective-permute-start.61 = (bf16[2,576,512]{2,1,0:T(8,128)(2,1)}, bf16[2,576,512]{2,1,0:T(8,128)(2,1)S(1)}, u32[]{:S(2)}, u32[]{:S(2)}) collective-permute-start(bf16[2,576,512]{2,1,0:T(8,128)(2,1)} %get-tuple-element.187), channel_id=1, source_target_pairs={{0,4},{1,3},{2,6},{3,1},{4,0},{5,7},{6,2},{7,5},{8,12},{9,11},{10,... | collective-permute-start | bytes 3538952 | tf_op jit(solution)/shard_map/ppermute | solution.py:742
  528.9 47.4 %collective-permute-start.59 = (bf16[2,512,512]{2,1,0:T(8,128)(2,1)}, bf16[2,512,512]{2,1,0:T(8,128)(2,1)S(1)}, u32[]{:S(2)}, u32[]{:S(2)}) collective-permute-start(bf16[2,512,512]{2,1,0:T(8,128)(2,1)} %join.8.refs_2_), channel_id=1, source_target_pairs={{0,4},{1,3},{2,6},{3,1},{4,0},{5,7},{6,2},{7,5},{8,12},{9,11},{10,... | collective-permute-start | bytes 3145736 | tf_op jit(solution)/shard_map/ppermute | solution.py:742
  528.9 44.6 %collective-permute-start.60 = (bf16[2,256,512]{2,1,0:T(8,128)(2,1)S(1)}, bf16[2,256,512]{2,1,0:T(8,128)(2,1)S(1)}, u32[]{:S(2)}, u32[]{:S(2)}) collective-permute-start(bf16[2,256,512]{2,1,0:T(8,128)(2,1)S(1)} %copy-done.105), channel_id=1, source_target_pairs={{0,4},{1,5},{2,6},{3,7},{4,0},{5,1},{6,2},{7,3},{8,12},{9,13},{10,... | collective-permute-start | bytes 1572872 | tf_op jit(solution)/shard_map/ppermute | solution.py:742
  541.1 44.9 %collective-permute-start.64 = (bf16[1,576,512]{2,1,0:T(8,128)(2,1)}, bf16[1,576,512]{2,1,0:T(8,128)(2,1)S(1)}, u32[]{:S(2)}, u32[]{:S(2)}) collective-permute-start(bf16[1,576,512]{2,1,0:T(8,128)(2,1)} %get-tuple-element.193), channel_id=1, source_target_pairs={{0,8},{1,9},{2,10},{3,11},{4,12},{5,13},{6,14},{7,15},{8,0},{9,1},... | collective-permute-start | bytes 1769480 | tf_op jit(solution)/shard_map/ppermute | solution.py:742
  543.2 40.2 %collective-permute-start.57 = (bf16[2,208,512]{2,1,0:T(8,128)(2,1)S(1)}, bf16[2,208,512]{2,1,0:T(8,128)(2,1)S(1)}, u32[]{:S(2)}, u32[]{:S(2)}) collective-permute-start(bf16[2,208,512]{2,1,0:T(8,128)(2,1)S(1)} %copy-done.107), channel_id=1, source_target_pairs={{0,2},{1,3},{2,0},{3,1},{4,6},{5,7},{6,4},{7,5},{8,10},{9,11},{10,... | collective-permute-start | bytes 1277960 | tf_op jit(solution)/shard_map/ppermute | solution.py:742
  580.3 98.1 %collective-permute-start.70 = (bf16[4,512,512]{2,1,0:T(8,128)(2,1)}, bf16[4,512,512]{2,1,0:T(8,128)(2,1)S(1)}, u32[]{:S(2)}, u32[]{:S(2)}) collective-permute-start(bf16[4,512,512]{2,1,0:T(8,128)(2,1)} %join.9.refs_2_), channel_id=1, source_target_pairs={{0,2},{1,5},{2,0},{3,7},{4,6},{5,1},{6,4},{7,3},{8,10},{9,13},{10,... | collective-permute-start | bytes 6291464 | tf_op jit(solution)/shard_map/ppermute | solution.py:742
  589.1 53.6 %collective-permute-start.67 = (bf16[1,576,512]{2,1,0:T(8,128)(2,1)}, bf16[1,576,512]{2,1,0:T(8,128)(2,1)S(1)}, u32[]{:S(2)}, u32[]{:S(2)}) collective-permute-start(bf16[1,576,512]{2,1,0:T(8,128)(2,1)} %fold.21.refs_2_.refs_0_), channel_id=1, source_target_pairs={{0,8},{1,9},{2,10},{3,11},{4,12},{5,13},{6,14},{7,15},{8,0},{9,1},... | collective-permute-start | bytes 1769480 | tf_op jit(solution)/shard_map/ppermute | solution.py:742
  602.2 35.5 %collective-permute-start.63 = (bf16[1,256,512]{2,1,0:T(8,128)(2,1)S(1)}, bf16[1,256,512]{2,1,0:T(8,128)(2,1)S(1)}, u32[]{:S(2)}, u32[]{:S(2)}) collective-permute-start(bf16[1,256,512]{2,1,0:T(8,128)(2,1)S(1)} %copy-done.114), channel_id=1, source_target_pairs={{0,8},{1,9},{2,10},{3,11},{4,12},{5,13},{6,14},{7,15},{8,0},{9,1},... | collective-permute-start | bytes 786440 | tf_op jit(solution)/shard_map/ppermute | solution.py:742
  602.3 38.0 %collective-permute-start.62 = (bf16[1,208,512]{2,1,0:T(8,128)(2,1)}, bf16[1,208,512]{2,1,0:T(8,128)(2,1)S(1)}, u32[]{:S(2)}, u32[]{:S(2)}) collective-permute-start(bf16[1,208,512]{2,1,0:T(8,128)(2,1)} %get-tuple-element.191), channel_id=1, source_target_pairs={{0,8},{1,9},{2,10},{3,11},{4,12},{5,13},{6,14},{7,15},{8,0},{9,1},... | collective-permute-start | bytes 638984 | tf_op jit(solution)/shard_map/ppermute | solution.py:742
  645.9 47.6 %collective-permute-start.73 = (bf16[2,576,512]{2,1,0:T(8,128)(2,1)}, bf16[2,576,512]{2,1,0:T(8,128)(2,1)S(1)}, u32[]{:S(2)}, u32[]{:S(2)}) collective-permute-start(bf16[2,576,512]{2,1,0:T(8,128)(2,1)} %join.10.refs_2_), channel_id=1, source_target_pairs={{0,4},{1,3},{2,6},{3,1},{4,0},{5,7},{6,2},{7,5},{8,12},{9,11},{10,... | collective-permute-start | bytes 3538952 | tf_op jit(solution)/shard_map/ppermute | solution.py:742
  698.1 29.2 %collective-permute-start.74 = (bf16[4,576,512]{2,1,0:T(8,128)(2,1)}, bf16[4,576,512]{2,1,0:T(8,128)(2,1)}, u32[]{:S(2)}, u32[]{:S(2)}) collective-permute-start(bf16[4,576,512]{2,1,0:T(8,128)(2,1)} %join.15.refs_6_), channel_id=1, source_target_pairs={{0,2},{1,5},{2,0},{3,7},{4,6},{5,1},{6,4},{7,3},{8,10},{9,13},{10,... | collective-permute-start | bytes 7077896 | tf_op jit(solution)/shard_map/ppermute | solution.py:742
  699.6 38.9 %collective-permute-start.72 = (bf16[4,256,512]{2,1,0:T(8,128)(2,1)S(1)}, bf16[4,256,512]{2,1,0:T(8,128)(2,1)}, u32[]{:S(2)}, u32[]{:S(2)}) collective-permute-start(bf16[4,256,512]{2,1,0:T(8,128)(2,1)S(1)} %copy-done.17), channel_id=1, source_target_pairs={{0,2},{1,3},{2,0},{3,1},{4,6},{5,7},{6,4},{7,5},{8,10},{9,11},{10,... | collective-permute-start | bytes 3145736 | tf_op jit(solution)/shard_map/ppermute | solution.py:742
  700.2 42.2 %collective-permute-start.71 = (bf16[4,208,512]{2,1,0:T(8,128)(2,1)S(1)}, bf16[4,208,512]{2,1,0:T(8,128)(2,1)}, u32[]{:S(2)}, u32[]{:S(2)}) collective-permute-start(bf16[4,208,512]{2,1,0:T(8,128)(2,1)S(1)} %copy-done.18), channel_id=1, source_target_pairs={{0,4},{1,5},{2,6},{3,7},{4,0},{5,1},{6,2},{7,3},{8,12},{9,13},{10,... | collective-permute-start | bytes 2555912 | tf_op jit(solution)/shard_map/ppermute | solution.py:742
  (169 other events, 1562.2 us)
